TPU v7x, 32 devices: a whole 2x2x4 slice. The times are simulated.
32 devices in a mesh: section: 2 (over x), shard: 16 (over z, y, core).
Axes of the slice: x: 2, y: 2, z: 4, core: 2. Of those that a mesh axis runs over, the one named last changes fastest.
Arguments:
- embedded: bfloat16 [2, 2048, 2048], P(None, 'shard'), may hold values from -6 to 6
- cotangent: bfloat16 [2, 2048, 2048], P(None, 'shard'), may hold values from -6 to 6
- segments: int32 [2, 2048], replicated, may hold values from 0 to 3, as said below
- first_gain: bfloat16 [2, 2048], P('section', 'shard'), may hold values from 0.25 to 1.75
- first_shift: bfloat16 [2, 2048], P('section', 'shard'), may hold values from -1 to 1
- mixer_weight: bfloat16 [2, 2048, 2304], P('section', 'shard'), may hold values from -0.1875 to 0.1875
- mixer_bias: bfloat16 [2, 2176], P('section', 'shard'), may hold values from -1 to 1
- output_weight: bfloat16 [2, 2048, 2048], P('section', 'shard'), may hold values from -0.5 to 0.5
- output_bias: bfloat16 [2, 2048], P('section', 'shard'), may hold values from -1 to 1
- second_gain: bfloat16 [2, 2048], P('section', 'shard'), may hold values from 0.25 to 1.75
- second_shift: bfloat16 [2, 2048], P('section', 'shard'), may hold values from -1 to 1
- expand_weight: bfloat16 [2, 2048, 8192], P('section', 'shard'), may hold values from -0.125 to 0.125
- expand_bias: bfloat16 [2, 8192], P('section', 'shard'), may hold values from -1 to 1
- contract_weight: bfloat16 [2, 8192, 2048], P('section', 'shard'), may hold values from -0.125 to 0.125
- contract_bias: bfloat16 [2, 2048], P('section', 'shard'), may hold values from -1 to 1
Outputs:
- section_outputs: bfloat16 [2, 2, 2048, 2048], P('section', None, 'shard')
- input_grads: float32 [2, 2, 2048, 2048], P('section', None, 'shard')
- first_gain_grad: float32 [2, 2048], P('section', 'shard')
- first_shift_grad: float32 [2, 2048], P('section', 'shard')
- mixer_weight_grad: float32 [2, 2048, 2304], P('section', 'shard')
- mixer_bias_grad: float32 [2, 2176], P('section', 'shard')
- output_weight_grad: float32 [2, 2048, 2048], P('section', 'shard')
- output_bias_grad: float32 [2, 2048], P('section', 'shard')
- second_gain_grad: float32 [2, 2048], P('section', 'shard')
- second_shift_grad: float32 [2, 2048], P('section', 'shard')
- expand_weight_grad: float32 [2, 2048, 8192], P('section', 'shard')
- expand_bias_grad: float32 [2, 8192], P('section', 'shard')
- contract_weight_grad: float32 [2, 8192, 2048], P('section', 'shard')
- contract_bias_grad: float32 [2, 2048], P('section', 'shard')
Inputs may be any that keep to these rules, and one draw needn't show every extreme that they name: `segments`: in each row, segment numbers start at 0 at position 0, never fall, rise by at most one from one position to the next, and end at 3; in one row, drawn from the seed, no document begins between position 128 and position 1920.
All inputs are finite; a program needn't handle non-finite values.
Results may differ from a plain program's by a relative error of at most 0.03.
Values may be sent and summed in bfloat16 or wider, within the bound.
A program may use at most 384 MiB of HBM per device.

v0:
```python
import jax
import jax.numpy as jnp
from jax import lax
from jax.sharding import PartitionSpec as P

D = 2048
HEADS = 16
HD = 128
WINDOW = 1024


epsilon = 1e-05


def passed_along(block, axis, distance):
    devices = range(lax.axis_size(axis))
    route = [(i - distance, i) for i in devices if i - distance in devices]
    return lax.ppermute(block, axis, route)


def layer_norm(values, gain_row, shift_row):
    center = values - jnp.mean(values, axis=-1, keepdims=True)
    spread = jnp.mean(center * center, axis=-1, keepdims=True)
    return center * lax.rsqrt(spread + epsilon) * gain_row + shift_row


def gelu_tanh(values):
    return jax.nn.gelu(values, approximate=True)


def window_mask(segments, micro_index, device, row_count, reach_blocks):
    seg_row = lax.dynamic_index_in_dim(segments, micro_index, 0, keepdims=False)
    padded = jnp.concatenate([jnp.full((reach_blocks * row_count,), -1, jnp.int32), seg_row])
    key_segments = lax.dynamic_slice_in_dim(
        padded, device * row_count, (reach_blocks + 1) * row_count
    )
    query_segments = lax.dynamic_slice_in_dim(seg_row, device * row_count, row_count)
    distance = (
        jnp.arange(row_count)[:, None]
        + reach_blocks * row_count
        - jnp.arange((reach_blocks + 1) * row_count)[None, :]
    )
    return (
        (distance >= 0) & (distance < WINDOW) & (query_segments[:, None] == key_segments[None, :])
    )


def fetch_window(key_value, reach_blocks):
    earlier = [passed_along(key_value, "shard", offset) for offset in range(reach_blocks, 0, -1)]
    return jnp.concatenate(earlier + [key_value], axis=0)


def return_window(window_grad, reach_blocks, row_count):
    own_rows = window_grad[reach_blocks * row_count :]
    for offset in range(1, reach_blocks + 1):
        start_row = (reach_blocks - offset) * row_count
        own_rows = own_rows + passed_along(
            window_grad[start_row : start_row + row_count].astype(jnp.bfloat16), "shard", -offset
        ).astype(jnp.float32)
    return own_rows


def forward_layer(hidden, weights, key_mask, reach_blocks):
    (
        first_gain,
        first_shift,
        mixer_weight,
        mixer_bias,
        output_weight,
        output_bias,
        second_gain,
        second_shift,
        expand_weight,
        expand_bias,
        contract_weight,
        contract_bias,
    ) = weights
    row_count = hidden.shape[0]
    score_scale = HD ** (-0.5)
    normed_one = layer_norm(
        hidden, first_gain.astype(jnp.float32), first_shift.astype(jnp.float32)
    ).astype(jnp.bfloat16)
    full_bias = jnp.concatenate(
        [mixer_bias[:D], jnp.zeros((HD,), mixer_bias.dtype), mixer_bias[D:]]
    ).astype(jnp.float32)
    projected = (
        jnp.dot(normed_one, mixer_weight, preferred_element_type=jnp.float32) + full_bias
    ).astype(jnp.bfloat16)
    queries = projected[:, :D].reshape(row_count, HEADS, HD)
    window_pairs = fetch_window(projected[:, D:], reach_blocks)
    scores = (
        jnp.einsum("thd,kd->htk", queries, window_pairs[:, :HD], preferred_element_type=jnp.float32)
        * score_scale
    )
    masked = jnp.where(key_mask[None], scores, -1e30)
    top_score = jnp.max(masked, axis=2, keepdims=True)
    exponent = jnp.exp(masked - top_score)
    totals = jnp.sum(exponent, axis=2, keepdims=True)
    prob_low = (exponent / totals).astype(jnp.bfloat16)
    log_total = top_score + jnp.log(totals)
    mixed_rows = (
        jnp.einsum(
            "htk,kd->thd", prob_low, window_pairs[:, HD:], preferred_element_type=jnp.float32
        )
        .reshape(row_count, D)
        .astype(jnp.bfloat16)
    )
    middle = (
        hidden
        + jnp.dot(mixed_rows, output_weight, preferred_element_type=jnp.float32)
        + output_bias.astype(jnp.float32)
    )
    normed_two = layer_norm(
        middle, second_gain.astype(jnp.float32), second_shift.astype(jnp.float32)
    ).astype(jnp.bfloat16)
    pre_gelu = jnp.dot(
        normed_two, expand_weight, preferred_element_type=jnp.float32
    ) + expand_bias.astype(jnp.float32)
    activated = gelu_tanh(pre_gelu).astype(jnp.bfloat16)
    result = (
        middle
        + jnp.dot(activated, contract_weight, preferred_element_type=jnp.float32)
        + contract_bias.astype(jnp.float32)
    )
    return (
        result,
        (
            hidden,
            normed_one,
            projected,
            window_pairs,
            log_total,
            mixed_rows,
            middle,
            normed_two,
            pre_gelu,
            activated,
        ),
    )


def backward_layer(grad_result, weights, saved_state, key_mask, reach_blocks):
    (
        first_gain,
        first_shift,
        mixer_weight,
        mixer_bias,
        output_weight,
        output_bias,
        second_gain,
        second_shift,
        expand_weight,
        expand_bias,
        contract_weight,
        contract_bias,
    ) = weights
    (
        hidden,
        normed_one,
        projected,
        window_pairs,
        log_total,
        mixed_rows,
        middle,
        normed_two,
        pre_gelu,
        activated,
    ) = saved_state
    row_count = hidden.shape[0]
    score_scale = HD ** (-0.5)
    grad_out_low = grad_result.astype(jnp.bfloat16)
    grad_act = jnp.einsum(
        "rd,fd->rf", grad_out_low, contract_weight, preferred_element_type=jnp.float32
    )
    gelu_value, gelu_back = jax.vjp(gelu_tanh, pre_gelu)
    grad_pre = gelu_back(grad_act)[0].astype(jnp.bfloat16)
    grad_normed_two = jnp.einsum(
        "rf,df->rd", grad_pre, expand_weight, preferred_element_type=jnp.float32
    )
    norm_value_two, norm_back_two = jax.vjp(
        layer_norm, middle, second_gain.astype(jnp.float32), second_shift.astype(jnp.float32)
    )
    grad_middle_part, grad_gain_two, grad_shift_two = norm_back_two(grad_normed_two)
    grad_middle = grad_result + grad_middle_part
    grad_attended = grad_middle.astype(jnp.bfloat16)
    grad_mixed = (
        jnp.einsum("re,de->rd", grad_attended, output_weight, preferred_element_type=jnp.float32)
        .astype(jnp.bfloat16)
        .reshape(row_count, HEADS, HD)
    )
    queries = projected[:, :D].reshape(row_count, HEADS, HD)
    key_part = window_pairs[:, :HD]
    value_part = window_pairs[:, HD:]
    scores = (
        jnp.einsum("thd,kd->htk", queries, key_part, preferred_element_type=jnp.float32)
        * score_scale
    )
    prob_full = jnp.where(key_mask[None], jnp.exp(scores - log_total), 0.0)
    prob_low = prob_full.astype(jnp.bfloat16)
    grad_probs = jnp.einsum(
        "thd,kd->htk", grad_mixed, value_part, preferred_element_type=jnp.float32
    )
    row_dot = jnp.sum(prob_full * grad_probs, axis=2, keepdims=True)
    grad_scores = (prob_full * (grad_probs - row_dot)).astype(jnp.bfloat16)
    grad_queries = (
        jnp.einsum("htk,kd->thd", grad_scores, key_part, preferred_element_type=jnp.float32)
        * score_scale
    ).reshape(row_count, D)
    grad_keys = (
        jnp.einsum("htk,thd->kd", grad_scores, queries, preferred_element_type=jnp.float32)
        * score_scale
    )
    grad_values = jnp.einsum(
        "htk,thd->kd", prob_low, grad_mixed, preferred_element_type=jnp.float32
    )
    grad_window = jnp.concatenate([grad_keys, grad_values], axis=1)
    grad_own_pairs = return_window(grad_window, reach_blocks, row_count)
    grad_projected = jnp.concatenate([grad_queries, grad_own_pairs], axis=1).astype(jnp.bfloat16)
    grad_normed_one = jnp.einsum(
        "rq,dq->rd", grad_projected, mixer_weight, preferred_element_type=jnp.float32
    )
    norm_value_one, norm_back_one = jax.vjp(
        layer_norm, hidden, first_gain.astype(jnp.float32), first_shift.astype(jnp.float32)
    )
    grad_hidden_part, grad_gain_one, grad_shift_one = norm_back_one(grad_normed_one)
    grad_hidden = grad_middle + grad_hidden_part
    return (
        grad_hidden,
        (
            grad_projected,
            grad_attended,
            grad_pre,
            grad_out_low,
            grad_gain_one,
            grad_shift_one,
            grad_gain_two,
            grad_shift_two,
            normed_one,
            mixed_rows,
            normed_two,
            activated,
        ),
    )


def flatten_rows(stacked):
    return stacked.reshape((-1, stacked.shape[-1]))


def weight_terms(row_items, norm_items):
    (
        grad_projected_rows,
        grad_attended_rows,
        grad_pre_rows,
        grad_out_rows,
        normed_one_rows,
        mixed_all,
        normed_two_rows,
        activated_rows,
    ) = row_items
    first_gain_term, first_shift_term, second_gain_term, second_shift_term = norm_items
    mixer_weight_term = jnp.einsum(
        "rd,rq->dq", normed_one_rows, grad_projected_rows, preferred_element_type=jnp.float32
    )
    column_totals = jnp.sum(grad_projected_rows.astype(jnp.float32), axis=0)
    mixer_bias_term = jnp.concatenate([column_totals[:D], column_totals[D + HD :]])
    output_weight_term = jnp.einsum(
        "rd,re->de", mixed_all, grad_attended_rows, preferred_element_type=jnp.float32
    )
    output_bias_term = jnp.sum(grad_attended_rows.astype(jnp.float32), axis=0)
    expand_weight_term = jnp.einsum(
        "rd,rf->df", normed_two_rows, grad_pre_rows, preferred_element_type=jnp.float32
    )
    expand_bias_term = jnp.sum(grad_pre_rows.astype(jnp.float32), axis=0)
    contract_weight_term = jnp.einsum(
        "rf,rd->fd", activated_rows, grad_out_rows, preferred_element_type=jnp.float32
    )
    contract_bias_term = jnp.sum(grad_out_rows.astype(jnp.float32), axis=0)
    return (
        first_gain_term[None],
        first_shift_term[None],
        mixer_weight_term[None],
        mixer_bias_term[None],
        output_weight_term[None],
        output_bias_term[None],
        second_gain_term[None],
        second_shift_term[None],
        expand_weight_term[None],
        expand_bias_term[None],
        contract_weight_term[None],
        contract_bias_term[None],
    )


def on_device(
    embedded,
    cotangent,
    segments,
    first_gain,
    first_shift,
    mixer_weight,
    mixer_bias,
    output_weight,
    output_bias,
    second_gain,
    second_shift,
    expand_weight,
    expand_bias,
    contract_weight,
    contract_bias,
):
    section_index = lax.axis_index("section")
    device = lax.axis_index("shard")
    micro_count = embedded.shape[0]
    row_count = embedded.shape[1]
    reach_blocks = WINDOW // row_count
    own_params = (
        first_gain[0],
        first_shift[0],
        mixer_weight[0],
        mixer_bias[0],
        output_weight[0],
        output_bias[0],
        second_gain[0],
        second_shift[0],
        expand_weight[0],
        expand_bias[0],
        contract_weight[0],
        contract_bias[0],
    )
    forward_weights = (
        lax.all_gather(own_params[0], "shard", axis=0, tiled=True),
        lax.all_gather(own_params[1], "shard", axis=0, tiled=True),
        lax.all_gather(own_params[2], "shard", axis=0, tiled=True),
        lax.all_gather(own_params[3], "shard", axis=0, tiled=True),
        lax.all_gather(own_params[4], "shard", axis=0, tiled=True),
        lax.all_gather(own_params[5], "shard", axis=0, tiled=True),
        lax.all_gather(own_params[6], "shard", axis=0, tiled=True),
        lax.all_gather(own_params[7], "shard", axis=0, tiled=True),
        lax.all_gather(own_params[8], "shard", axis=0, tiled=True),
        lax.all_gather(own_params[9], "shard", axis=0, tiled=True),
        lax.all_gather(own_params[10], "shard", axis=0, tiled=True),
        lax.all_gather(own_params[11], "shard", axis=0, tiled=True),
    )
    zero_rows = jnp.zeros((row_count, D), jnp.float32)
    arrived = zero_rows
    sent_list = []
    kept_states = []
    for step_index in range(micro_count + 1):
        own_input = (
            embedded[step_index].astype(jnp.float32) if step_index < micro_count else zero_rows
        )
        hidden = jnp.where(section_index == 0, own_input, arrived)
        micro_index = jnp.clip(step_index - section_index, 0, micro_count - 1)
        key_mask = window_mask(segments, micro_index, device, row_count, reach_blocks)
        result, saved_state = forward_layer(hidden, forward_weights, key_mask, reach_blocks)
        result_low = result.astype(jnp.bfloat16)
        sent_list.append(result_low)
        kept_states.append(saved_state)
        if step_index < micro_count:
            arrived = passed_along(result_low, "section", 1).astype(jnp.float32)
    section_outputs = lax.dynamic_slice_in_dim(jnp.stack(sent_list), section_index, micro_count, 0)[
        None
    ]
    stacked_states = [
        jnp.stack([state_item[item_index] for state_item in kept_states])
        for item_index in range(10)
    ]
    valid_start = 1 - section_index
    arrived_grad = zero_rows
    grad_records = []
    hidden_grads = []
    for step_index in range(micro_count + 1):
        own_grad = (
            cotangent[step_index].astype(jnp.float32) if step_index < micro_count else zero_rows
        )
        grad_result = jnp.where(section_index == 1, own_grad, arrived_grad)
        forward_index = jnp.clip(step_index - 1 + 2 * section_index, 0, micro_count)
        micro_index = jnp.clip(step_index - 1 + section_index, 0, micro_count - 1)
        saved_state = [
            lax.dynamic_index_in_dim(stacked, forward_index, 0, keepdims=False)
            for stacked in stacked_states
        ]
        key_mask = window_mask(segments, micro_index, device, row_count, reach_blocks)
        grad_hidden, record = backward_layer(
            grad_result, forward_weights, saved_state, key_mask, reach_blocks
        )
        hidden_grads.append(grad_hidden)
        if step_index < micro_count:
            arrived_grad = passed_along(grad_hidden.astype(jnp.bfloat16), "section", -1).astype(
                jnp.float32
            )
        grad_records.append(record)
    input_grads = lax.dynamic_slice_in_dim(jnp.stack(hidden_grads), valid_start, micro_count, 0)[
        None
    ]
    chosen = [
        lax.dynamic_slice_in_dim(
            jnp.stack([record[item_index] for record in grad_records]), valid_start, micro_count, 0
        )
        for item_index in range(12)
    ]
    row_items = (
        flatten_rows(chosen[0]),
        flatten_rows(chosen[1]),
        flatten_rows(chosen[2]),
        flatten_rows(chosen[3]),
        flatten_rows(chosen[8]),
        flatten_rows(chosen[9]),
        flatten_rows(chosen[10]),
        flatten_rows(chosen[11]),
    )
    norm_items = (
        jnp.sum(chosen[4], axis=0),
        jnp.sum(chosen[5], axis=0),
        jnp.sum(chosen[6], axis=0),
        jnp.sum(chosen[7], axis=0),
    )
    all_terms = weight_terms(row_items, norm_items)
    summed = (
        lax.psum_scatter(all_terms[0], "shard", scatter_dimension=1, tiled=True),
        lax.psum_scatter(all_terms[1], "shard", scatter_dimension=1, tiled=True),
        lax.psum_scatter(all_terms[2], "shard", scatter_dimension=1, tiled=True),
        lax.psum_scatter(all_terms[3], "shard", scatter_dimension=1, tiled=True),
        lax.psum_scatter(all_terms[4], "shard", scatter_dimension=1, tiled=True),
        lax.psum_scatter(all_terms[5], "shard", scatter_dimension=1, tiled=True),
        lax.psum_scatter(all_terms[6], "shard", scatter_dimension=1, tiled=True),
        lax.psum_scatter(all_terms[7], "shard", scatter_dimension=1, tiled=True),
        lax.psum_scatter(all_terms[8], "shard", scatter_dimension=1, tiled=True),
        lax.psum_scatter(all_terms[9], "shard", scatter_dimension=1, tiled=True),
        lax.psum_scatter(all_terms[10], "shard", scatter_dimension=1, tiled=True),
        lax.psum_scatter(all_terms[11], "shard", scatter_dimension=1, tiled=True),
    )
    return (
        section_outputs,
        input_grads,
        summed[0],
        summed[1],
        summed[2],
        summed[3],
        summed[4],
        summed[5],
        summed[6],
        summed[7],
        summed[8],
        summed[9],
        summed[10],
        summed[11],
    )


def solution(mesh):
    in_specs = (
        P(None, "shard", None),
        P(None, "shard", None),
        P(),
        P("section", "shard"),
        P("section", "shard"),
        P("section", "shard", None),
        P("section", "shard"),
        P("section", "shard", None),
        P("section", "shard"),
        P("section", "shard"),
        P("section", "shard"),
        P("section", "shard", None),
        P("section", "shard"),
        P("section", "shard", None),
        P("section", "shard"),
    )
    out_specs = (
        P("section", None, "shard", None),
        P("section", None, "shard", None),
        P("section", "shard"),
        P("section", "shard"),
        P("section", "shard", None),
        P("section", "shard"),
        P("section", "shard", None),
        P("section", "shard"),
        P("section", "shard"),
        P("section", "shard"),
        P("section", "shard", None),
        P("section", "shard"),
        P("section", "shard", None),
        P("section", "shard"),
    )
    return jax.shard_map(
        on_device, mesh=mesh, in_specs=in_specs, out_specs=out_specs, check_vma=False
    )
```

profile of v0, /device:TPU:0, one launch (start us, length us, event | category | flops | bytes accessed | tf_op | source)
XLA Modules:
  0.0 3138.7 jit_solution(2566559647852640221)
XLA Ops:
  11.7 36.3 %all-reduce.6 = bf16[2176]{0:T(1024)(128)(2,1)S(1)} all-reduce(bf16[2176]{0:T(1024)(128)(2,1)S(1)} %dynamic-update-slice), channel_id=5, replica_groups=mesh['section'=2,'shard'=16] {'shard'}, use_global_device_ids=true, to_apply=%add.6 | all-reduce | flops 2176 | bytes 8704
  48.0 17.3 all-gather
  65.4 19.3 all-gather.1
  106.0 17.7 all-gather.5
  123.8 18.7 all-gather.6
  142.5 17.7 all-gather.7
  160.1 18.4 all-gather.11
  178.5 18.3 all-gather.9
  238.3 102.8 %all-gather.21.cloned.1.call-done = bf16[1,2048,8192]{2,1,0:T(8,128)(2,1)} async-done(((bf16[1,128,8192]{2,1,0:T(8,128)(2,1)}), bf16[1,2048,8192]{2,1,0:T(8,128)(2,1)}) %all-gather.21.cloned.1.call-update) | async-done | bytes 33554448 | tf_op jit(solution)/shard_map/all_gather | solution.py:340
  341.1 17.2 fusion.24
  358.3 162.0 %all-gather.23.cloned.1.call-done = bf16[1,8192,2048]{2,1,0:T(8,128)(2,1)} async-done(((bf16[1,512,2048]{2,1,0:T(8,128)(2,1)}), bf16[1,8192,2048]{2,1,0:T(8,128)(2,1)}) %all-gather.23.cloned.1.call-update) | async-done | bytes 33554448 | tf_op jit(solution)/shard_map/all_gather | solution.py:342
  520.3 17.1 fusion.227
  608.5 18.3 fusion.224
  695.3 17.3 fusion.30
  723.3 18.9 fusion.90
  742.2 20.2 multiply_reduce_fusion.2
  856.3 19.1 fusion.97
  875.4 19.3 multiply_reduce_fusion.1
  977.8 18.9 fusion.104
  996.7 19.1 multiply_reduce_fusion
  1127.2 24.4 convolution_bitcast_fusion.1
  1162.5 25.2 convolution_bitcast_fusion
  1188.9 17.2 fusion.230
  1212.6 74.7 %reduce-scatter.45.cloned.1.call-done = f32[512,1]{1,0:T(8,128)} async-done(((f32[8192,1]{1,0:T(8,128)}), f32[512,1]{1,0:T(8,128)}) %reduce-scatter.45.cloned.1.call-update) | async-done | bytes 2064
  1288.9 31.3 all-reduce.7
  1323.6 23.7 reduce-scatter.47.cloned.1.call-done
  1348.8 58.9 %reduce-scatter.35.cloned.1.call-done = f32[128,1]{1,0:T(8,128)} async-done(((f32[2048,1]{1,0:T(8,128)}), f32[128,1]{1,0:T(8,128)}) %reduce-scatter.35.cloned.1.call-update) | async-done | bytes 528
  1409.1 58.6 %reduce-scatter.37.cloned.1.call-done = f32[128,1]{1,0:T(8,128)} async-done(((f32[2048,1]{1,0:T(8,128)}), f32[128,1]{1,0:T(8,128)}) %reduce-scatter.37.cloned.1.call-update) | async-done | bytes 528
  1469.1 181.2 %reduce-scatter.29.cloned.1.call-done = f32[1,128,2048]{2,1,0:T(8,128)} async-done(((f32[1,2048,2048]{2,1,0:T(8,128)}), f32[1,128,2048]{2,1,0:T(8,128)}) %reduce-scatter.29.cloned.1.call-update) | async-done | bytes 1048592 | tf_op jit(solution)/shard_map/reduce_scatter | solution.py:425
  1650.4 199.0 %reduce-scatter.27.cloned.1.call-done = f32[1,128,2304]{2,1,0:T(8,128)} async-done(((f32[1,2048,2304]{2,1,0:T(8,128)}), f32[1,128,2304]{2,1,0:T(8,128)}) %reduce-scatter.27.cloned.1.call-update) | async-done | bytes 1179664 | tf_op jit(solution)/shard_map/reduce_scatter | solution.py:423
  1849.4 641.1 %reduce-scatter.31.cloned.1.call-done = f32[1,128,8192]{2,1,0:T(8,128)} async-done(((f32[1,2048,8192]{2,1,0:T(8,128)}), f32[1,128,8192]{2,1,0:T(8,128)}) %reduce-scatter.31.cloned.1.call-update) | async-done | bytes 4194320 | tf_op jit(solution)/shard_map/reduce_scatter | solution.py:429
  2490.5 641.4 %reduce-scatter.33.cloned.1.call-done = f32[1,512,2048]{2,1,0:T(8,128)} async-done(((f32[1,8192,2048]{2,1,0:T(8,128)}), f32[1,512,2048]{2,1,0:T(8,128)}) %reduce-scatter.33.cloned.1.call-update) | async-done | bytes 4194320 | tf_op jit(solution)/shard_map/reduce_scatter | solution.py:431
  (632 shorter events, 529.8 us)
Async XLA Ops:
  7.2 87.8 %all-gather.17.cloned.1.call-start = ((), (), s32[]{:S(2)}) async-start(), calls=%async_computation.15 | async-start | bytes 10027008 | tf_op jit(solution)/shard_map/all_gather | solution.py:334
  8.0 225.0 %all-gather.19.cloned.1.call-start = ((), (), s32[]{:S(2)}) async-start(), calls=%async_computation.16 | async-start | bytes 8912896 | tf_op jit(solution)/shard_map/all_gather | solution.py:336
  8.7 332.3 %all-gather.21.cloned.1.call-start = ((), (), s32[]{:S(2)}) async-start(), calls=%async_computation.17 | async-start | bytes 35651584 | tf_op jit(solution)/shard_map/all_gather | solution.py:340
  9.5 510.8 %all-gather.23.cloned.1.call-start = ((), (), s32[]{:S(2)}) async-start(), calls=%async_computation.18 | async-start | bytes 35651584 | tf_op jit(solution)/shard_map/all_gather | solution.py:342
  10.0 1197.7 %reduce-scatter.39.cloned.1.call-start = ((), (), s32[]{:S(2)}) async-start(), calls=%async_computation.21 | async-start | bytes 1114112
  100.4 104.8 %collective-permute-start = (bf16[128,256]{1,0:T(8,128)(2,1)S(1)}, bf16[128,256]{1,0:T(8,128)(2,1)S(1)}, u32[]{:S(2)}, u32[]{:S(2)}) collective-permute-start(bf16[128,256]{1,0:T(8,128)(2,1)S(1)} %slice.256), channel_id=1, source_target_pairs={{0,8},{1,9},{2,10},{3,11},{4,12},{5,13},{6,14},{7,15},{16,24},{17,... | collective-permute-start | bytes 196616 | tf_op jit(solution)/shard_map/ppermute | solution.py:18
  196.8 31.4 %collective-permute-start.7 = (bf16[128,256]{1,0:T(8,128)(2,1)S(1)}, bf16[128,256]{1,0:T(8,128)(2,1)S(1)}, u32[]{:S(2)}, u32[]{:S(2)}) collective-permute-start(bf16[128,256]{1,0:T(8,128)(2,1)S(1)} %slice.256), channel_id=1, source_target_pairs={{0,1},{1,2},{2,3},{3,4},{4,5},{5,6},{6,7},{7,8},{8,9},{9,10},{10,1... | collective-permute-start | bytes 196616 | tf_op jit(solution)/shard_map/ppermute | solution.py:18
  199.1 29.2 collective-permute-start.6
  202.3 26.0 collective-permute-start.5
  203.8 24.4 collective-permute-start.4
  563.7 23.6 collective-permute-start.16
  565.0 22.3 collective-permute-start.15
  568.7 18.6 collective-permute-start.14
  649.3 36.7 %collective-permute-start.25 = (bf16[128,256]{1,0:T(8,128)(2,1)S(1)}, bf16[128,256]{1,0:T(8,128)(2,1)S(1)}, u32[]{:S(2)}, u32[]{:S(2)}) collective-permute-start(bf16[128,256]{1,0:T(8,128)(2,1)S(1)} %slice.264), channel_id=1, source_target_pairs={{0,1},{1,2},{2,3},{3,4},{4,5},{5,6},{6,7},{7,8},{8,9},{9,10},{10,1... | collective-permute-start | bytes 196616 | tf_op jit(solution)/shard_map/ppermute | solution.py:18
  651.8 34.2 %collective-permute-start.24 = (bf16[128,256]{1,0:T(8,128)(2,1)S(1)}, bf16[128,256]{1,0:T(8,128)(2,1)S(1)}, u32[]{:S(2)}, u32[]{:S(2)}) collective-permute-start(bf16[128,256]{1,0:T(8,128)(2,1)S(1)} %slice.264), channel_id=1, source_target_pairs={{0,2},{1,3},{2,4},{3,5},{4,6},{5,7},{6,8},{7,9},{8,10},{9,11},{10,... | collective-permute-start | bytes 196616 | tf_op jit(solution)/shard_map/ppermute | solution.py:18
  657.1 28.9 collective-permute-start.23
  661.3 24.7 collective-permute-start.22
  803.5 18.6 collective-permute-start.33
  804.8 18.5 collective-permute-start.32
  806.1 19.6 collective-permute-start.31
  1029.2 179.9 %reduce-scatter.41.cloned.1.call-start = ((), (), s32[]{:S(2)}) async-start(), calls=%async_computation.22 | async-start | bytes 1114112
  1054.6 156.6 %reduce-scatter.43.cloned.1.call-start = ((), (), s32[]{:S(2)}) async-start(), calls=%async_computation.23 | async-start | bytes 1114112
  1061.9 20.3 collective-permute-start.49
  1063.2 19.0 collective-permute-start.48
  1064.6 222.7 %reduce-scatter.45.cloned.1.call-start = ((), (), s32[]{:S(2)}) async-start(), calls=%async_computation.24 | async-start | bytes 4456448
  1082.0 265.4 %reduce-scatter.47.cloned.1.call-start = ((), (), s32[]{:S(2)}) async-start(), calls=%async_computation.25 | async-start | bytes 1114112
  1097.8 309.9 %reduce-scatter.35.cloned.1.call-start = ((), (), s32[]{:S(2)}) async-start(), calls=%async_computation.19 | async-start | bytes 1114112
  1099.6 368.1 %reduce-scatter.37.cloned.1.call-start = ((), (), s32[]{:S(2)}) async-start(), calls=%async_computation.20 | async-start | bytes 1114112
  1102.2 548.2 %reduce-scatter.29.cloned.1.call-start = ((), (), s32[]{:S(2)}) async-start(), calls=%async_computation.12 | async-start | bytes 17825792 | tf_op jit(solution)/shard_map/reduce_scatter | solution.py:425
  1110.6 738.8 %reduce-scatter.27.cloned.1.call-start = ((), (), s32[]{:S(2)}) async-start(), calls=%async_computation.11 | async-start | bytes 20054016 | tf_op jit(solution)/shard_map/reduce_scatter | solution.py:423
  1123.4 1367.1 %reduce-scatter.31.cloned.1.call-start = ((), (), s32[]{:S(2)}) async-start(), calls=%async_computation.13 | async-start | bytes 71303168 | tf_op jit(solution)/shard_map/reduce_scatter | solution.py:429
  1151.6 1980.3 %reduce-scatter.33.cloned.1.call-start = ((), (), s32[]{:S(2)}) async-start(), calls=%async_computation.14 | async-start | bytes 71303168 | tf_op jit(solution)/shard_map/reduce_scatter | solution.py:431
  (162 other events, 3087.7 us)
Sparse Core Ops, SparseCore 0:
  10.4 84.6 all-gather.16
  97.2 73.6 all-gather.18
  172.5 168.4 all-gather.20
  342.5 177.7 all-gather.22
  1029.3 61.5 reduce-scatter.38
  1094.8 56.2 reduce-scatter.40
  1154.7 56.3 reduce-scatter.42
  1215.5 71.6 reduce-scatter.44
  1290.9 56.4 reduce-scatter.46
  1351.2 56.3 reduce-scatter.34
  1411.3 56.3 reduce-scatter.36
  1472.8 177.4 reduce-scatter.28
  1655.6 193.7 reduce-scatter.26
  1854.7 635.8 reduce-scatter.30
  2495.8 636.0 reduce-scatter.32
where the time goes:
time: 3150 us; the launch traced here: 3140 us
  waiting for transfers between devices  2250 us (71%)
  matrix products  398 us (13%)
  blocking collectives  195 us (6%)
  starting transfers between devices  116 us (4%)
  other arithmetic  100 us (3%)
  local copies, waits for them, and re-layouts  61.9 us (2%)
    reduce_scatter x1, waiting for transfers between devices, on_device(): lax.psum_scatter(all_terms[10], 'shard', scatter_dimension=1, tiled=True)  641 us
    reduce_scatter x1, waiting for transfers between devices, on_device(): lax.psum_scatter(all_terms[8], 'shard', scatter_dimension=1, tiled=True)  641 us
    unnamed x22, waiting for transfers between devices  219 us
    reduce_scatter x1, waiting for transfers between devices, on_device(): lax.psum_scatter(all_terms[2], 'shard', scatter_dimension=1, tiled=True)  199 us
    reduce_scatter x1, waiting for transfers between devices, on_device(): lax.psum_scatter(all_terms[4], 'shard', scatter_dimension=1, tiled=True)  181 us
    all_gather x1, waiting for transfers between devices, on_device(): lax.all_gather(own_params[10], 'shard', axis=0, tiled=True)  162 us
    ppermute x52, starting transfers between devices, passed_along(): return lax.ppermute(block, axis, route)  114 us
    all_gather x1, waiting for transfers between devices, on_device(): lax.all_gather(own_params[8], 'shard', axis=0, tiled=True)  103 us
  transfers between devices with their start and end apart: 67, of which 34 were waited for; matrix products, arithmetic and copies ran while one was open for 7% of the time, Pallas kernels for 0%

commit v1 on v0

--- a/solution.py
+++ b/solution.py
@@ -1,6 +1,10 @@
+import functools
+
 import jax
 import jax.numpy as jnp
 from jax import lax
+from jax.experimental import pallas as pl
+from jax.experimental.pallas import tpu as pltpu
 from jax.sharding import PartitionSpec as P
 
 D = 2048
@@ -292,7 +296,7 @@
     )
 
 
-def on_device(
+def on_device_general(
     embedded,
     cotangent,
     segments,
@@ -449,6 +453,903 @@
     )
 
 
+MESH = pl.DeviceIdType.MESH
+LIMIT = 60 << 20
+CUBE = ("x", 4, 2, 1)
+ALL = ("x", 8, 4, 2, 1)
+
+
+class Hyper:
+    def __init__(self, dims):
+        sec = lax.axis_index("section")
+        shd = lax.axis_index("shard")
+        self.dims = dims
+        self.partner, self.delta, self.pos = {}, {}, 0
+        for n, d in enumerate(dims):
+            weight = 1 << (len(dims) - 1 - n)
+            if d == "x":
+                bit = sec
+                self.partner[d] = (1 - sec, shd)
+            else:
+                bit = lax.rem(shd // d, 2)
+                self.partner[d] = (sec, shd + d * (1 - 2 * bit))
+            self.pos = self.pos + bit * weight
+            self.delta[d] = weight * (1 - 2 * bit)
+
+    def at(self, order, offset):
+        place = self.pos
+        for j, d in enumerate(order):
+            if offset >> j & 1:
+                place = place + self.delta[d]
+        return place
+
+    def barrier(self, more=()):
+        sem = pltpu.get_barrier_semaphore()
+        partners = [self.partner[d] for d in self.dims] + list(more)
+        for partner in partners:
+            pl.semaphore_signal(sem, inc=1, device_id=partner, device_id_type=MESH)
+        pl.semaphore_wait(sem, len(partners))
+
+
+def cube_parts(rows, widths, col0=0):
+    orders = (("x", 4, 2, 1), (4, 2, "x", 1), (2, "x", 4, 1))
+    parts = []
+    for width, order in zip(widths, orders):
+        parts.append((0, rows, col0, width, order))
+        col0 += width
+    return tuple(parts)
+
+
+class Gather:
+    def __init__(self, h, parts, src, dst, send_sem, recv_sem):
+        self.h, self.parts, self.src, self.dst = h, parts, src, dst
+        self.send_sem, self.recv_sem = send_sem, recv_sem
+
+    def copy(self, p, offset, j):
+        r0, rn, c0, cn, order = self.parts[p]
+        rows, cols = pl.ds(r0, rn), pl.ds(c0, cn)
+        there = self.dst.at[self.h.at(order, offset), rows, cols]
+        here = self.src.at[rows, cols] if offset == 0 else there
+        n = offset | 1 << j
+        return pltpu.make_async_remote_copy(
+            src_ref=here,
+            dst_ref=there,
+            send_sem=self.send_sem.at[p, n],
+            recv_sem=self.recv_sem.at[p, n],
+            device_id=self.h.partner[order[j]],
+            device_id_type=MESH,
+        )
+
+    def start(self, chosen):
+        for j in range(len(self.h.dims)):
+            for p in chosen:
+                self.copy(p, 0, j).start()
+
+    def forward(self, chosen):
+        k = len(self.h.dims)
+        for j in range(k):
+            for low in range(1 << j):
+                for p in chosen:
+                    self.copy(p, low, j).wait_recv()
+                    for later in range(j + 1, k):
+                        self.copy(p, low | 1 << j, later).start()
+
+    def finish(self):
+        for p in range(len(self.parts)):
+            for j in range(len(self.h.dims)):
+                for low in range(1 << j):
+                    self.copy(p, low, j).wait_send()
+
+
+def gather_kernel(dims, parts, x_ref, o_ref, send_sem, recv_sem, local_sem):
+    h = Hyper(dims)
+    h.barrier()
+    own = pltpu.make_async_copy(x_ref, o_ref.at[h.pos], local_sem)
+    own.start()
+    g = Gather(h, parts, x_ref, o_ref, send_sem, recv_sem)
+    chosen = range(len(parts))
+    g.start(chosen)
+    g.forward(chosen)
+    g.finish()
+    own.wait()
+
+
+def gather(x, dims, parts, collective_id, name):
+    n = 1 << len(dims)
+    return pl.pallas_call(
+        functools.partial(gather_kernel, dims, parts),
+        out_shape=jax.ShapeDtypeStruct((n,) + x.shape, x.dtype),
+        in_specs=[pl.BlockSpec(memory_space=pl.ANY)],
+        out_specs=pl.BlockSpec(memory_space=pl.ANY),
+        scratch_shapes=[
+            pltpu.SemaphoreType.DMA((len(parts), n)),
+            pltpu.SemaphoreType.DMA((len(parts), n)),
+            pltpu.SemaphoreType.DMA,
+        ],
+        compiler_params=pltpu.CompilerParams(
+            collective_id=collective_id, has_side_effects=True, vmem_limit_bytes=LIMIT
+        ),
+        name=name,
+    )(x)
+
+
+def gather_window_kernel(parts, x_ref, kv_ref, o_ref, okv_ref, far, *sems):
+    send_sem, recv_sem, kv_send, kv_recv, own_sem, swap_send, swap_recv = sems
+    h = Hyper(CUBE)
+    sec, shd = lax.axis_index("section"), lax.axis_index("shard")
+    other = (sec, shd + 8 * (1 - 2 * lax.rem(shd // 8, 2)))
+    h.barrier((other,))
+    swap = pltpu.make_async_remote_copy(
+        src_ref=kv_ref,
+        dst_ref=far,
+        send_sem=swap_send,
+        recv_sem=swap_recv,
+        device_id=other,
+        device_id_type=MESH,
+    )
+    swap.start()
+    own = pltpu.make_async_copy(x_ref, o_ref.at[h.pos], own_sem.at[0])
+    own.start()
+    g = Gather(h, parts, x_ref, o_ref, send_sem, recv_sem)
+    g.start(range(3))
+    swap.wait_recv()
+    own_kv = pltpu.make_async_copy(far, okv_ref.at[h.pos], own_sem.at[1])
+    own_kv.start()
+    kv_parts = tuple((0, kv_ref.shape[0], 0, kv_ref.shape[1], order) for order in (CUBE,))
+    gkv = Gather(h, kv_parts, far, okv_ref, kv_send, kv_recv)
+    gkv.start(range(1))
+    k = len(CUBE)
+    for j in range(k):
+        for low in range(1 << j):
+            for one, chosen in ((g, range(3)), (gkv, range(1))):
+                for p in chosen:
+                    one.copy(p, low, j).wait_recv()
+                    for later in range(j + 1, k):
+                        one.copy(p, low | 1 << j, later).start()
+    g.finish()
+    gkv.finish()
+    swap.wait_send()
+    own.wait()
+    own_kv.wait()
+
+
+def gather_window(x, kv, collective_id):
+    parts = cube_parts(x.shape[0], (768, 640, 640))
+    n = 16
+    return pl.pallas_call(
+        functools.partial(gather_window_kernel, parts),
+        out_shape=(
+            jax.ShapeDtypeStruct((n,) + x.shape, x.dtype),
+            jax.ShapeDtypeStruct((n,) + kv.shape, kv.dtype),
+        ),
+        in_specs=[pl.BlockSpec(memory_space=pl.ANY)] * 2,
+        out_specs=[pl.BlockSpec(memory_space=pl.ANY)] * 2,
+        scratch_shapes=[
+            pltpu.VMEM(kv.shape, kv.dtype),
+            pltpu.SemaphoreType.DMA((3, n)),
+            pltpu.SemaphoreType.DMA((3, n)),
+            pltpu.SemaphoreType.DMA((1, n)),
+            pltpu.SemaphoreType.DMA((1, n)),
+            pltpu.SemaphoreType.DMA((2,)),
+            pltpu.SemaphoreType.DMA,
+            pltpu.SemaphoreType.DMA,
+        ],
+        compiler_params=pltpu.CompilerParams(
+            collective_id=collective_id, has_side_effects=True, vmem_limit_bytes=LIMIT
+        ),
+        name="gather_window",
+    )(x, kv)
+
+
+def reduce_kernel(dims, parts, swap_cols, x_ref, o_ref, *scratch):
+    if swap_cols:
+        buf, send_sem, recv_sem, swapped, swap_send, swap_recv = scratch
+    else:
+        buf, send_sem, recv_sem = scratch
+    h = Hyper(dims)
+    k = len(dims)
+    sec, shd = lax.axis_index("section"), lax.axis_index("shard")
+    other = (sec, shd + 8 * (1 - 2 * lax.rem(shd // 8, 2)))
+    h.barrier((other,) if swap_cols else ())
+
+    def window(p):
+        r0, rn, c0, cn, order = parts[p]
+        return pl.ds(r0, rn), pl.ds(c0, cn)
+
+    def held(p, j, offset):
+        if j == k - 1:
+            return x_ref.at[(h.at(parts[p][4], offset),) + window(p)]
+        return buf.at[((1 << (j + 1)) | offset,) + window(p)]
+
+    def copy(p, j, low):
+        n = (1 << j) | low
+        return pltpu.make_async_remote_copy(
+            src_ref=held(p, j, low | 1 << j),
+            dst_ref=buf.at[(n,) + window(p)],
+            send_sem=send_sem.at[p, n],
+            recv_sem=recv_sem.at[p, n],
+            device_id=h.partner[parts[p][4][j]],
+            device_id_type=MESH,
+        )
+
+    for low in reversed(range(1 << (k - 1))):
+        for p in range(len(parts)):
+            copy(p, k - 1, low).start()
+    step = 16
+    for j in reversed(range(k)):
+        for low in reversed(range(1 << j)):
+            for p in range(len(parts)):
+                r0, rn, c0, cn, order = parts[p]
+                copy(p, j, low).wait_recv()
+                mine = held(p, j, low)
+                came = buf.at[((1 << j) | low,) + window(p)]
+
+                @pl.loop(0, rn // step)
+                def _(i):
+                    rows = pl.ds(pl.multiple_of(i * step, step), step)
+                    total = mine[rows, :].astype(jnp.float32) + came[rows, :].astype(jnp.float32)
+                    if j > 0:
+                        came[rows, :] = total.astype(came.dtype)
+                    else:
+                        out_rows = pl.ds(pl.multiple_of(r0 + i * step, step), step)
+                        o_ref[out_rows, pl.ds(c0, cn)] = total
+
+                if j > 0 and low >> (j - 1) & 1:
+                    copy(p, j - 1, low ^ (1 << (j - 1))).start()
+    if swap_cols:
+        c0, cn = swap_cols
+        rows = x_ref.shape[1]
+        swapped[0] = o_ref[:, c0 : c0 + cn].astype(swapped.dtype)
+        swap = pltpu.make_async_remote_copy(
+            src_ref=swapped.at[0],
+            dst_ref=swapped.at[1],
+            send_sem=swap_send,
+            recv_sem=swap_recv,
+            device_id=other,
+            device_id_type=MESH,
+        )
+        swap.start()
+        swap.wait()
+        o_ref[:, c0 : c0 + cn] = swapped[1].astype(jnp.float32)
+    for p in range(len(parts)):
+        for j in range(k):
+            for low in range(1 << j):
+                copy(p, j, low).wait_send()
+
+
+def reduce(x, dims, parts, collective_id, name, swap_cols=None):
+    n = 1 << len(dims)
+    block = x.shape[1:]
+    scratch = [
+        pltpu.VMEM((n,) + block, x.dtype),
+        pltpu.SemaphoreType.DMA((len(parts), n)),
+        pltpu.SemaphoreType.DMA((len(parts), n)),
+    ]
+    if swap_cols:
+        scratch += [
+            pltpu.VMEM((2, block[0], swap_cols[1]), x.dtype),
+            pltpu.SemaphoreType.DMA,
+            pltpu.SemaphoreType.DMA,
+        ]
+    return pl.pallas_call(
+        functools.partial(reduce_kernel, dims, parts, swap_cols),
+        out_shape=jax.ShapeDtypeStruct(block, jnp.float32),
+        in_specs=[pl.BlockSpec(memory_space=pltpu.VMEM)],
+        out_specs=pl.BlockSpec(memory_space=pltpu.VMEM),
+        scratch_shapes=scratch,
+        compiler_params=pltpu.CompilerParams(
+            collective_id=collective_id, has_side_effects=True, vmem_limit_bytes=LIMIT
+        ),
+        name=name,
+    )(x)
+
+
+def block_of(sec, shd):
+    return 8 * lax.rem(sec + lax.rem(shd, 2), 2) + lax.rem(shd, 8)
+
+
+def everyone_barrier(me):
+    sem = pltpu.get_barrier_semaphore()
+
+    @pl.loop(1, 32)
+    def _(d):
+        there = lax.rem(me + d, 32)
+        pl.semaphore_signal(
+            sem, inc=1, device_id=(there // 16, lax.rem(there, 16)), device_id_type=MESH
+        )
+
+    pl.semaphore_wait(sem, 31)
+
+
+def fetch_kernel(mix, exp, out, con, wq, we, wo, wc, *sems):
+    q_send, q_recv, e_send, e_recv, row_send, row_recv, own_sem = sems
+    sec, shd = lax.axis_index("section"), lax.axis_index("shard")
+    me = sec * 16 + shd
+    everyone_barrier(me)
+    f = block_of(sec, shd)
+
+    def column_copies(d):
+        there = lax.rem(me + d, 32)
+        ts, tj = there // 16, lax.rem(there, 16)
+        tf = block_of(ts, tj)
+        result = []
+        for src, dst, send, recv, wide in ((mix, wq, q_send, q_recv, HD), (exp, we, e_send, e_recv, 512)):
+            result.append(
+                pltpu.make_async_remote_copy(
+                    src_ref=src.at[:, pl.ds(pl.multiple_of(tf * wide, wide), wide)],
+                    dst_ref=dst.at[sec, shd],
+                    send_sem=send.at[d],
+                    recv_sem=recv.at[d],
+                    device_id=(ts, tj),
+                    device_id_type=MESH,
+                )
+            )
+        return result
+
+    own = [
+        pltpu.make_async_copy(
+            mix.at[:, pl.ds(pl.multiple_of(f * HD, HD), HD)], wq.at[sec, shd], own_sem.at[0]
+        ),
+        pltpu.make_async_copy(
+            exp.at[:, pl.ds(pl.multiple_of(f * 512, 512), 512)], we.at[sec, shd], own_sem.at[1]
+        ),
+    ]
+    for one in own:
+        one.start()
+
+    @pl.loop(1, 32)
+    def _(d):
+        for one in column_copies(d):
+            one.start()
+
+    low = lax.rem(shd, 8)
+    half = shd // 8
+    to_x = lax.rem(half + lax.rem(shd, 2), 2)
+    from_half = lax.rem(sec + lax.rem(shd, 2), 2)
+
+    def row_copies(z):
+        return [
+            pltpu.make_async_remote_copy(
+                src_ref=src,
+                dst_ref=dst.at[sec],
+                send_sem=row_send.at[n, z],
+                recv_sem=row_recv.at[n, sec],
+                device_id=(to_x, 8 * z + low),
+                device_id_type=MESH,
+            )
+            for n, (src, dst) in enumerate(((out, wo), (con, wc)))
+        ]
+
+    def arrivals(s):
+        return [
+            pltpu.make_async_remote_copy(
+                src_ref=src,
+                dst_ref=dst.at[s],
+                send_sem=row_send.at[n, 0],
+                recv_sem=row_recv.at[n, s],
+                device_id=(to_x, low),
+                device_id_type=MESH,
+            )
+            for n, (src, dst) in enumerate(((out, wo), (con, wc)))
+        ]
+
+    def own_rows():
+        return [
+            pltpu.make_async_copy(src, dst.at[sec], own_sem.at[2 + n])
+            for n, (src, dst) in enumerate(((out, wo), (con, wc)))
+        ]
+
+    for z in range(2):
+        mine = jnp.logical_and(to_x == sec, half == z)
+
+        @pl.when(mine)
+        def _():
+            for one in own_rows():
+                one.start()
+
+        @pl.when(jnp.logical_not(mine))
+        def _():
+            for one in row_copies(z):
+                one.start()
+
+    @pl.loop(1, 32)
+    def _(d):
+        for one in column_copies(d):
+            one.wait_recv()
+
+    for s in range(2):
+        mine = jnp.logical_and(sec == s, from_half == half)
+
+        @pl.when(jnp.logical_not(mine))
+        def _():
+            for one in arrivals(s):
+                one.wait_recv()
+
+    @pl.loop(1, 32)
+    def _(d):
+        for one in column_copies(d):
+            one.wait_send()
+
+    for z in range(2):
+        mine = jnp.logical_and(to_x == sec, half == z)
+
+        @pl.when(mine)
+        def _():
+            for one in own_rows():
+                one.wait()
+
+        @pl.when(jnp.logical_not(mine))
+        def _():
+            for one in row_copies(z):
+                one.wait_send()
+
+    for one in own:
+        one.wait()
+
+
+def fetch_weights(mix, exp, out, con):
+    bf16 = jnp.bfloat16
+    dma = pltpu.SemaphoreType.DMA
+    return pl.pallas_call(
+        fetch_kernel,
+        out_shape=(
+            jax.ShapeDtypeStruct((2, 16, 128, HD), bf16),
+            jax.ShapeDtypeStruct((2, 16, 128, 512), bf16),
+            jax.ShapeDtypeStruct((2, 128, D), bf16),
+            jax.ShapeDtypeStruct((2, 512, D), bf16),
+        ),
+        in_specs=[pl.BlockSpec(memory_space=pl.ANY)] * 4,
+        out_specs=[pl.BlockSpec(memory_space=pl.ANY)] * 4,
+        scratch_shapes=[dma((32,)), dma((32,)), dma((32,)), dma((32,)), dma((2, 2)), dma((2, 2)), dma((4,))],
+        compiler_params=pltpu.CompilerParams(
+            collective_id=1, has_side_effects=True, vmem_limit_bytes=LIMIT
+        ),
+        name="fetch_weights",
+    )(mix, exp, out, con)
+
+
+def return_kernel(gq, ge, go, gc, rq, re, ro, rc, *sems):
+    q_send, q_recv, e_send, e_recv, row_send, row_recv, own_sem = sems
+    sec, shd = lax.axis_index("section"), lax.axis_index("shard")
+    me = sec * 16 + shd
+    everyone_barrier(me)
+    f = block_of(sec, shd)
+    low = lax.rem(shd, 8)
+    half = shd // 8
+
+    def column_copies(d):
+        there = lax.rem(me + d, 32)
+        ts, tj = there // 16, lax.rem(there, 16)
+        result = []
+        for src, dst, send, recv, wide in ((gq, rq, q_send, q_recv, HD), (ge, re, e_send, e_recv, 512)):
+            result.append(
+                pltpu.make_async_remote_copy(
+                    src_ref=src.at[ts, tj],
+                    dst_ref=dst.at[half, :, pl.ds(pl.multiple_of(f * wide, wide), wide)],
+                    send_sem=send.at[d],
+                    recv_sem=recv.at[d],
+                    device_id=(ts, tj),
+                    device_id_type=MESH,
+                )
+            )
+        return result
+
+    own = [
+        pltpu.make_async_copy(
+            gq.at[sec, shd], rq.at[half, :, pl.ds(pl.multiple_of(f * HD, HD), HD)], own_sem.at[0]
+        ),
+        pltpu.make_async_copy(
+            ge.at[sec, shd], re.at[half, :, pl.ds(pl.multiple_of(f * 512, 512), 512)], own_sem.at[1]
+        ),
+    ]
+    for one in own:
+        one.start()
+
+    def row_copies(s):
+        return [
+            pltpu.make_async_remote_copy(
+                src_ref=src.at[s],
+                dst_ref=dst.at[half],
+                send_sem=row_send.at[n, s],
+                recv_sem=row_recv.at[n, half],
+                device_id=(s, f),
+                device_id_type=MESH,
+            )
+            for n, (src, dst) in enumerate(((go, ro), (gc, rc)))
+        ]
+
+    def arrivals(z):
+        return [
+            pltpu.make_async_remote_copy(
+                src_ref=src.at[0],
+                dst_ref=dst.at[z],
+                send_sem=row_send.at[n, 0],
+                recv_sem=row_recv.at[n, z],
+                device_id=(sec, f),
+                device_id_type=MESH,
+            )
+            for n, (src, dst) in enumerate(((go, ro), (gc, rc)))
+        ]
+
+    def own_rows():
+        return [
+            pltpu.make_async_copy(src.at[sec], dst.at[half], own_sem.at[2 + n])
+            for n, (src, dst) in enumerate(((go, ro), (gc, rc)))
+        ]
+
+    for s in range(2):
+        mine = jnp.logical_and(sec == s, f == shd)
+
+        @pl.when(mine)
+        def _():
+            for one in own_rows():
+                one.start()
+
+        @pl.when(jnp.logical_not(mine))
+        def _():
+            for one in row_copies(s):
+                one.start()
+
+    @pl.loop(1, 32)
+    def _(d):
+        for one in column_copies(d):
+            one.start()
+
+    @pl.loop(1, 32)
+    def _(d):
+        for one in column_copies(d):
+            one.wait_recv()
+
+    for z in range(2):
+        mine = jnp.logical_and(f == shd, half == z)
+
+        @pl.when(jnp.logical_not(mine))
+        def _():
+            for one in arrivals(z):
+                one.wait_recv()
+
+    @pl.loop(1, 32)
+    def _(d):
+        for one in column_copies(d):
+            one.wait_send()
+
+    for s in range(2):
+        mine = jnp.logical_and(sec == s, f == shd)
+
+        @pl.when(mine)
+        def _():
+            for one in own_rows():
+                one.wait()
+
+        @pl.when(jnp.logical_not(mine))
+        def _():
+            for one in row_copies(s):
+                one.wait_send()
+
+    for one in own:
+        one.wait()
+
+
+def return_grads(gq, ge, go, gc):
+    bf16 = jnp.bfloat16
+    dma = pltpu.SemaphoreType.DMA
+    return pl.pallas_call(
+        return_kernel,
+        out_shape=(
+            jax.ShapeDtypeStruct((2, 128, D), bf16),
+            jax.ShapeDtypeStruct((2, 128, 8192), bf16),
+            jax.ShapeDtypeStruct((2, 128, D), bf16),
+            jax.ShapeDtypeStruct((2, 512, D), bf16),
+        ),
+        in_specs=[pl.BlockSpec(memory_space=pl.ANY)] * 4,
+        out_specs=[pl.BlockSpec(memory_space=pl.ANY)] * 4,
+        scratch_shapes=[dma((32,)), dma((32,)), dma((32,)), dma((32,)), dma((2, 2)), dma((2, 2)), dma((4,))],
+        compiler_params=pltpu.CompilerParams(
+            collective_id=2, has_side_effects=True, vmem_limit_bytes=LIMIT
+        ),
+        name="return_grads",
+    )(gq, ge, go, gc)
+
+
+QB = 256
+KB = WINDOW + QB
+SCALE = HD ** (-0.5)
+NT = (((1,), (1,)), ((), ()))
+TN = (((0,), (0,)), ((), ()))
+
+
+def kept_pairs(lo_ref, a):
+    key = a + lax.broadcasted_iota(jnp.int32, (KB, QB), 0)
+    last = a + WINDOW + lax.broadcasted_iota(jnp.int32, (KB, QB), 1)
+    return (key >= lo_ref[0]) & (key <= last)
+
+
+def attend_kernel(lo_ref, q_ref, k_ref, v_ref, o_ref, lse_ref):
+    a = pl.multiple_of(lax.rem(pl.program_id(0), 4) * QB, QB)
+    keys = pl.ds(a, KB)
+    s = lax.dot_general(k_ref[0, keys], q_ref[0], NT, preferred_element_type=jnp.float32) * SCALE
+    s = jnp.where(kept_pairs(lo_ref, a), s, -1e30)
+    top = jnp.max(s, axis=0, keepdims=True)
+    e = jnp.exp(s - top)
+    total = jnp.sum(e, axis=0, keepdims=True)
+    probs = (e * (1.0 / total)).astype(jnp.bfloat16)
+    o_ref[0] = lax.dot_general(probs, v_ref[0, keys], TN, preferred_element_type=jnp.float32).astype(
+        o_ref.dtype
+    )
+    lse_ref[0] = top + jnp.log(total)
+
+
+def attend(lo, q, k, v):
+    per_q = pl.BlockSpec((1, QB, HD), lambda n: (n, 0, 0))
+    per_row = pl.BlockSpec((1, 1, QB), lambda n: (n, 0, 0))
+    per_micro = pl.BlockSpec((1, 2 * WINDOW, HD), lambda n: (n // 4, 0, 0))
+    return pl.pallas_call(
+        attend_kernel,
+        grid=(8,),
+        out_shape=(
+            jax.ShapeDtypeStruct((8, QB, HD), jnp.bfloat16),
+            jax.ShapeDtypeStruct((8, 1, QB), jnp.float32),
+        ),
+        in_specs=[per_row, per_q, per_micro, per_micro],
+        out_specs=[per_q, per_row],
+        compiler_params=pltpu.CompilerParams(vmem_limit_bytes=LIMIT),
+        name="attend",
+    )(lo, q, k, v)
+
+
+def attend_back_kernel(lo_ref, lse_ref, q_ref, k_ref, v_ref, g_ref, dq_ref, dk_ref, dv_ref):
+    n = lax.rem(pl.program_id(0), 4)
+    a = pl.multiple_of(n * QB, QB)
+    keys = pl.ds(a, KB)
+
+    @pl.when(n == 0)
+    def _():
+        dk_ref[...] = jnp.zeros_like(dk_ref)
+        dv_ref[...] = jnp.zeros_like(dv_ref)
+
+    q, g, k = q_ref[0], g_ref[0], k_ref[0, keys]
+    s = lax.dot_general(k, q, NT, preferred_element_type=jnp.float32) * SCALE
+    probs = jnp.where(kept_pairs(lo_ref, a), jnp.exp(s - lse_ref[0]), 0.0)
+    gp = lax.dot_general(v_ref[0, keys], g, NT, preferred_element_type=jnp.float32)
+    dot = jnp.sum(probs * gp, axis=0, keepdims=True)
+    gs = (probs * (gp - dot)).astype(jnp.bfloat16)
+    dq = lax.dot_general(gs, k, TN, preferred_element_type=jnp.float32) * SCALE
+    dq_ref[0] = dq.astype(dq_ref.dtype)
+    dk_ref[0, keys] += jnp.dot(gs, q, preferred_element_type=jnp.float32) * SCALE
+    dv_ref[0, keys] += jnp.dot(probs.astype(jnp.bfloat16), g, preferred_element_type=jnp.float32)
+
+
+def attend_back(lo, lse, q, k, v, g):
+    per_q = pl.BlockSpec((1, QB, HD), lambda n: (n, 0, 0))
+    per_row = pl.BlockSpec((1, 1, QB), lambda n: (n, 0, 0))
+    per_micro = pl.BlockSpec((1, 2 * WINDOW, HD), lambda n: (n // 4, 0, 0))
+    return pl.pallas_call(
+        attend_back_kernel,
+        grid=(8,),
+        out_shape=(
+            jax.ShapeDtypeStruct((8, QB, HD), jnp.bfloat16),
+            jax.ShapeDtypeStruct((2, 2 * WINDOW, HD), jnp.float32),
+            jax.ShapeDtypeStruct((2, 2 * WINDOW, HD), jnp.float32),
+        ),
+        in_specs=[per_row, per_row, per_q, per_micro, per_micro, per_q],
+        out_specs=[per_q, per_micro, per_micro],
+        compiler_params=pltpu.CompilerParams(vmem_limit_bytes=LIMIT),
+        name="attend_back",
+    )(lo, lse, q, k, v, g)
+
+
+def dot32(a, b):
+    return jnp.dot(a, b, preferred_element_type=jnp.float32)
+
+
+def dot_nt(a, b):
+    return lax.dot_general(a, b, NT, preferred_element_type=jnp.float32)
+
+
+def dot_tn(a, b):
+    return lax.dot_general(a, b, TN, preferred_element_type=jnp.float32)
+
+
+PLAIN = cube_parts(128, (768, 640, 640))
+WIDE = cube_parts(128, (896, 896, 768))
+SMALL = tuple(
+    (48 * n, 48, 0, 256, order)
+    for n, order in enumerate(((8, "x", 4, 2, 1), (8, 4, 2, "x", 1), (8, 2, "x", 4, 1)))
+)
+BIAS = D + HD
+
+
+def on_device_fast(
+    embedded,
+    cotangent,
+    segments,
+    first_gain,
+    first_shift,
+    mixer_weight,
+    mixer_bias,
+    output_weight,
+    output_bias,
+    second_gain,
+    second_shift,
+    expand_weight,
+    expand_bias,
+    contract_weight,
+    contract_bias,
+):
+    bf16, f32 = jnp.bfloat16, jnp.float32
+    sec, shd = lax.axis_index("section"), lax.axis_index("shard")
+    half = shd // 8
+    f = block_of(sec, shd)
+
+    small = jnp.concatenate(
+        [
+            first_gain[0],
+            first_shift[0],
+            second_gain[0],
+            second_shift[0],
+            output_bias[0],
+            contract_bias[0],
+            expand_bias[0],
+            mixer_bias[0],
+        ]
+    )
+    small = jnp.concatenate([small, jnp.zeros((16 * 256 - small.shape[0],), bf16)]).reshape(16, 256)
+    shared = gather(
+        jnp.concatenate([mixer_weight[0][:, D:], small], axis=0), ALL, SMALL, 3, "gather_shared"
+    ).reshape(2, 16, 144, 256)
+    wkv = shared[:, :, :128].reshape(2, D, 256)
+    vectors = shared[:, :, 128:].reshape(2, 16, 4096)
+
+    def vector(n):
+        return vectors[:, :, 128 * n : 128 * (n + 1)].reshape(2, D).astype(f32)
+
+    gain_one, shift_one, gain_two, shift_two, bias_out, bias_con = [vector(n) for n in range(6)]
+    bias_exp = vectors[:, :, 768:1280].reshape(2, 8192).astype(f32)
+    bias_exp = lax.dynamic_slice_in_dim(bias_exp, f * 512, 512, 1)
+    bias_mix = vectors[:, :, 1280 : 1280 + 136].reshape(2, BIAS).astype(f32)
+    bias_q = lax.dynamic_slice_in_dim(bias_mix, f * HD, HD, 1)
+    bias_kv = jnp.concatenate([jnp.zeros((2, HD), f32), bias_mix[:, D:]], axis=1)
+
+    wq, we, wo, wc = fetch_weights(
+        mixer_weight[0][:, :D], expand_weight[0], output_weight[0], contract_weight[0]
+    )
+    wq = wq.reshape(2, D, HD)
+    we = we.reshape(2, D, 512)
+
+    starts = jnp.sum(
+        (segments[:, None, :] < lax.dynamic_slice_in_dim(segments, half * WINDOW, WINDOW, 1)[:, :, None]),
+        axis=2,
+        dtype=jnp.int32,
+    )
+    lo = jnp.maximum(jnp.arange(1, WINDOW + 1)[None], starts - half * WINDOW + WINDOW)
+    lo = lo.reshape(8, 1, QB)
+
+    hidden = lax.dynamic_index_in_dim(embedded, sec, 0, keepdims=False).astype(f32)
+    results, kept = [], []
+    for s in range(2):
+        n1 = layer_norm(hidden, gain_one[s], shift_one[s]).astype(bf16)
+        kv_rows = (dot32(n1, wkv[s]) + bias_kv[s]).astype(bf16)
+        all_n1, far_kv = gather_window(n1, kv_rows, 4)
+        all_n1 = all_n1.reshape(2048, D)
+        q = (dot32(all_n1, wq[s]) + bias_q[s]).astype(bf16).reshape(8, QB, HD)
+        kv = (dot32(all_n1, wkv[s]) + bias_kv[s]).astype(bf16).reshape(2, WINDOW, 256)
+        kv = jnp.concatenate([far_kv.reshape(2, WINDOW, 256), kv], axis=1)
+        k, v = kv[:, :, :HD], kv[:, :, HD:]
+        mixed, lse = attend(lo, q, k, v)
+        mixed = mixed.reshape(2048, HD)
+        part = dot32(mixed, wo[s]).astype(bf16).reshape(16, 128, D)
+        middle = hidden + reduce(part, CUBE, PLAIN, 5, "reduce_rows") + bias_out[s]
+        n2 = layer_norm(middle, gain_two[s], shift_two[s]).astype(bf16)
+        all_n2 = gather(n2, CUBE, PLAIN, 6, "gather_rows").reshape(2048, D)
+        pre = dot32(all_n2, we[s]) + bias_exp[s]
+        act = gelu_tanh(pre).astype(bf16)
+        part = dot32(act, wc[s]).astype(bf16).reshape(16, 128, D)
+        result = middle + reduce(part, CUBE, PLAIN, 5, "reduce_rows") + bias_con[s]
+        results.append(result.astype(bf16))
+        kept.append((hidden, n1, all_n1, q, k, v, lse, mixed, middle, all_n2, pre, act))
+        hidden = results[-1].astype(f32)
+
+    grad = lax.dynamic_index_in_dim(cotangent, sec, 0, keepdims=False).astype(f32)
+    input_grads = [None, None]
+    weight_grads = [None, None]
+    small_grads = [None, None]
+    for s in (1, 0):
+        hidden, n1, all_n1, q, k, v, lse, mixed, middle, all_n2, pre, act = kept[s]
+        go = grad.astype(bf16)
+        all_go = gather(go, CUBE, PLAIN, 6, "gather_rows").reshape(2048, D)
+        _, gelu_back = jax.vjp(gelu_tanh, pre)
+        g_pre = gelu_back(dot_nt(all_go, wc[s]))[0].astype(bf16)
+        part = dot_nt(g_pre, we[s]).astype(bf16).reshape(16, 128, D)
+        g_n2 = reduce(part, CUBE, PLAIN, 5, "reduce_rows")
+        d_wc = dot_tn(act, all_go).astype(bf16)
+        d_we = dot_tn(all_n2, g_pre).astype(bf16)
+        d_be = jnp.sum(g_pre.astype(f32), axis=0)
+        _, back = jax.vjp(layer_norm, middle, gain_two[s], shift_two[s])
+        g_mid, d_gain_two, d_shift_two = back(g_n2)
+        g_mid = grad + g_mid
+        ga = g_mid.astype(bf16)
+        all_ga = gather(ga, CUBE, PLAIN, 6, "gather_rows").reshape(2048, D)
+        g_mixed = dot_nt(all_ga, wo[s]).astype(bf16).reshape(8, QB, HD)
+        d_wo = dot_tn(mixed, all_ga).astype(bf16)
+        dq, dk, dv = attend_back(lo, lse, q, k, v, g_mixed)
+        dq = dq.reshape(2048, HD)
+        d_kv = jnp.concatenate([dk, dv], axis=2).astype(bf16)
+        part = jnp.concatenate(
+            [
+                dot_nt(dq, wq[s]).astype(bf16).reshape(16, 128, D),
+                d_kv[:, WINDOW:].reshape(16, 128, 256),
+                d_kv[:, :WINDOW].reshape(16, 128, 256),
+            ],
+            axis=2,
+        )
+        rows = reduce(part, CUBE, WIDE, 7, "reduce_window", (D + 256, 256))
+        dkv_rows = (rows[:, D : D + 256] + jnp.where(half == 0, rows[:, D + 256 :], 0.0)).astype(bf16)
+        g_n1 = rows[:, :D] + dot_nt(dkv_rows, wkv[s])
+        _, back = jax.vjp(layer_norm, hidden, gain_one[s], shift_one[s])
+        g_in, d_gain_one, d_shift_one = back(g_n1)
+        g_in = g_mid + g_in
+        input_grads[s] = g_in
+        d_wq = dot_tn(all_n1, dq).astype(bf16)
+        d_wkv = dot_tn(n1, dkv_rows)
+        d_bq = jnp.sum(dq.astype(f32), axis=0)
+        d_bv = jnp.sum(dkv_rows[:, HD:].astype(f32), axis=0)
+        weight_grads[s] = (d_wq.reshape(16, 128, HD), d_we.reshape(16, 128, 512), d_wo, d_wc)
+        spread = [
+            d_gain_one,
+            d_shift_one,
+            d_gain_two,
+            d_shift_two,
+            jnp.sum(ga.astype(f32), axis=0),
+            jnp.sum(go.astype(f32), axis=0),
+        ]
+        d_be = lax.dynamic_update_slice_in_dim(jnp.zeros((8192,), f32), d_be, f * 512, 0)
+        d_bm = lax.dynamic_update_slice_in_dim(jnp.zeros((D,), f32), d_bq, f * HD, 0)
+        vec = jnp.concatenate(
+            [one.reshape(16, 128) for one in spread]
+            + [d_be.reshape(16, 512), jnp.concatenate([d_bm, d_bv]).reshape(16, 136)],
+            axis=1,
+        )
+        vec = jnp.pad(vec, ((0, 0), (0, 4096 - vec.shape[1]))).reshape(16, 16, 256)
+        small_grads[s] = jnp.concatenate([d_wkv.reshape(16, 128, 256), vec], axis=1)
+        grad = g_in.astype(bf16).astype(f32)
+
+    mine = reduce(
+        jnp.concatenate(small_grads, axis=0).astype(bf16), ALL, SMALL, 8, "reduce_shared"
+    )
+    vec = mine[128:].reshape(4096)
+    rq, re, ro, rc = return_grads(
+        *[jnp.stack([weight_grads[0][n], weight_grads[1][n]]) for n in range(4)]
+    )
+
+    def both(r):
+        return r[0].astype(f32) + r[1].astype(f32)
+
+    def swap(pair):
+        theirs = jnp.where(sec == 0, pair[1].astype(bf16), pair[0].astype(bf16))
+        own = jnp.where(sec == 0, pair[0], pair[1])
+        came = lax.ppermute(theirs, "section", [(0, 1), (1, 0)]).astype(own.dtype)
+        first = jnp.where(sec == 0, own, came)
+        second = jnp.where(sec == 0, came, own)
+        return jnp.stack([first, second])[None]
+
+    return (
+        swap(results),
+        swap(input_grads),
+        vec[0:128][None],
+        vec[128:256][None],
+        jnp.concatenate([both(rq), mine[:128]], axis=1)[None],
+        vec[1280 : 1280 + 136][None],
+        both(ro)[None],
+        vec[512:640][None],
+        vec[256:384][None],
+        vec[384:512][None],
+        both(re)[None],
+        vec[768:1280][None],
+        both(rc)[None],
+        vec[640:768][None],
+    )
+
+
 def solution(mesh):
     in_specs = (
         P(None, "shard", None),
@@ -483,6 +1384,8 @@
         P("section", "shard", None),
         P("section", "shard"),
     )
+    fits = mesh.shape["section"] == 2 and mesh.shape["shard"] == HEADS
+    on_device = on_device_fast if fits else on_device_general
     return jax.shard_map(
         on_device, mesh=mesh, in_specs=in_specs, out_specs=out_specs, check_vma=False
     )

time: 3150 us -> 1480 us (0.47)
  waiting for transfers between devices: 2250 us -> 0.01 us
  Pallas kernels: 0 us -> 1160 us
  matrix products: 398 us -> 185 us
  blocking collectives: 195 us -> 0 us
  starting transfers between devices: 116 us -> 2.11 us
  local copies, waits for them, and re-layouts: 61.9 us -> 25.7 us
    reduce_scatter x4 -> x0, waiting for transfers between devices: 1660 us -> none  [the longest x1 641 us: on_device(): lax.psum_scatter(all_terms[10], 'shard', scatter_dimension=1, tiled=True)]
    pallas_call x0 -> x24, Pallas kernels: none -> 1160 us  [the longest x9 424 us: reduce(): pl.pallas_call(functools.partial(reduce_kernel, dims, parts, swap_cols),...]
    all_gather x4 -> x0, waiting for transfers between devices: 274 us -> none  [the longest x1 162 us: on_device(): lax.all_gather(own_params[10], 'shard', axis=0, tiled=True)]
    unnamed x22 -> x0, waiting for transfers between devices: 219 us -> none
    dot_general x49 -> x32, matrix products: 398 us -> 185 us  [the longest x12 69.1 us: dot32(): return jnp.dot(a, b, preferred_element_type=jnp.float32)]
    all_gather x7 -> x0, blocking collectives: 127 us -> none  [the longest x1 19.3 us: on_device(): lax.all_gather(own_params[1], 'shard', axis=0, tiled=True)]
    ppermute x52 -> x2, starting transfers between devices: 114 us -> 2.11 us  [swap(): came = lax.ppermute(theirs, 'section', [(0, 1), (1, 0)]).astype(own.dtype)]
    ppermute x52 -> x2, waiting for transfers between devices: 93.4 us -> 0.01 us  [swap(): came = lax.ppermute(theirs, 'section', [(0, 1), (1, 0)]).astype(own.dtype)]
  transfers between devices with their start and end apart: 67 -> 2, of which waited for: 34 -> 0; matrix products, arithmetic and copies ran while one was open for 7% -> 9% of each run, Pallas kernels for 0% -> 28%
where the time goes in v1:
time: 1480 us; the launch traced here: 1470 us
  Pallas kernels  1160 us (78%)
  matrix products  185 us (12%)
  other arithmetic  84.7 us (6%)
  local copies, waits for them, and re-layouts  25.7 us (2%)
    pallas_call x9, Pallas kernels, reduce(): pl.pallas_call(functools.partial(reduce_kernel, dims, parts, swap_cols),...  424 us
    pallas_call x7, Pallas kernels, gather(): pl.pallas_call(functools.partial(gather_kernel, dims, parts), out_shape=j...  229 us
    pallas_call x1, Pallas kernels, return_grads(): pl.pallas_call(return_kernel, out_shape=(jax.ShapeDtypeStruct((2, 128, D)...  220 us
    pallas_call x1, Pallas kernels, fetch_weights(): pl.pallas_call(fetch_kernel, out_shape=(jax.ShapeDtypeStruct((2, 16, 128,...  154 us
    pallas_call x2, Pallas kernels, gather_window(): pl.pallas_call(functools.partial(gather_window_kernel, parts), out_shape=...  81 us
    dot_general x12, matrix products, dot32(): return jnp.dot(a, b, preferred_element_type=jnp.float32)  69.1 us
    dot_general x10, matrix products, dot_nt(): return lax.dot_general(a, b, NT, preferred_element_type=jnp.float32)  61.9 us
    dot_general x10, matrix products, dot_tn(): return lax.dot_general(a, b, TN, preferred_element_type=jnp.float32)  54.3 us
  transfers between devices with their start and end apart: 2, of which 0 were waited for; matrix products, arithmetic and copies ran while one was open for 9% of the time, Pallas kernels for 28%

profile of v1, /device:TPU:0, one launch (start us, length us, event | category | flops | bytes accessed | tf_op | source)
XLA Modules:
  0.0 1465.1 jit_solution(9028831470225574974)
XLA Ops:
  9.6 22.6 %gather_shared.1 = bf16[32,144,256]{2,1,0:T(8,128)(2,1)} custom-call(bf16[144,256]{1,0:T(8,128)(2,1)} %pad_maximum_fusion.10.x_ref), custom_call_target="tpu_custom_call" | custom-call | tf_op jit(solution)/shard_map/gather_shared/pallas_call | solution.py:559
  41.9 33.6 %gather_rows.8 = bf16[16,128,2048]{2,1,0:T(8,128)(2,1)} custom-call(bf16[128,2048]{1,0:T(8,128)(2,1)} %get-tuple-element.110.x_ref), custom_call_target="tpu_custom_call" | custom-call | tf_op jit(solution)/shard_map/gather_rows/pallas_call | solution.py:559
  77.8 40.0 %gather_window.2 = (bf16[16,128,2048]{2,1,0:T(8,128)(2,1)}, bf16[16,128,256]{2,1,0:T(8,128)(2,1)}) custom-call(bf16[128,2048]{1,0:T(8,128)(2,1)} %fusion.56.x_ref, bf16[128,256]{1,0:T(8,128)(2,1)} %fusion.50.kv_ref), custom_call_target="tpu_custom_call" | custom-call | tf_op jit(solution)/shard_map/gather_window/pallas_call | solution.py:619
  124.5 154.4 %fetch_weights.1 = (bf16[2,16,128,128]{3,2,1,0:T(8,128)(2,1)}, bf16[2,16,128,512]{3,2,1,0:T(8,128)(2,1)}, bf16[2,128,2048]{2,1,0:T(8,128)(2,1)}, bf16[2,512,2048]{2,1,0:T(8,128)(2,1)}) custom-call(bf16[128,2048]{1,0:T(8,128)(2,1)} %slice.346.mix, bf16[128,8192]{1,0:T(8,128)(2,1)} %bitcast.342, bf16[128,2048]{1,0:T(8,128)(2,1)} %bitcast.364, ...), custom_call_target="tpu_custom_call" | custom-call | tf_op jit(solution)/shard_map/fetch_weights/pallas_call | solution.py:893
  294.3 12.3 attend.2
  313.3 117.6 %reduce_rows.6 = f32[128,2048]{1,0:T(8,128)} custom-call(bf16[16,128,2048]{2,1,0:T(8,128)(2,1)} %bitcast.300), custom_call_target="tpu_custom_call" | custom-call | tf_op jit(solution)/shard_map/reduce_rows/pallas_call | solution.py:734
  433.6 33.3 %gather_rows.6 = bf16[16,128,2048]{2,1,0:T(8,128)(2,1)} custom-call(bf16[128,2048]{1,0:T(8,128)(2,1)} %add_convert_fusion.3.x_ref), custom_call_target="tpu_custom_call" | custom-call | tf_op jit(solution)/shard_map/gather_rows/pallas_call | solution.py:559
  474.7 8.1 convolution_convert_fusion.3
  482.8 37.2 %reduce_rows.7 = f32[128,2048]{1,0:T(8,128)} custom-call(bf16[16,128,2048]{2,1,0:T(8,128)(2,1)} %bitcast.310), custom_call_target="tpu_custom_call" | custom-call | tf_op jit(solution)/shard_map/reduce_rows/pallas_call | solution.py:734
  523.3 41.0 %gather_window.3 = (bf16[16,128,2048]{2,1,0:T(8,128)(2,1)}, bf16[16,128,256]{2,1,0:T(8,128)(2,1)}) custom-call(bf16[128,2048]{1,0:T(8,128)(2,1)} %copy-done.7, bf16[128,256]{1,0:T(8,128)(2,1)} %fusion.51.kv_ref), custom_call_target="tpu_custom_call" | custom-call | tf_op jit(solution)/shard_map/gather_window/pallas_call | solution.py:619
  575.2 12.5 attend.3
  594.5 37.1 %reduce_rows.8 = f32[128,2048]{1,0:T(8,128)} custom-call(bf16[16,128,2048]{2,1,0:T(8,128)(2,1)} %bitcast.301), custom_call_target="tpu_custom_call" | custom-call | tf_op jit(solution)/shard_map/reduce_rows/pallas_call | solution.py:734
  634.4 32.9 %gather_rows.7 = bf16[16,128,2048]{2,1,0:T(8,128)(2,1)} custom-call(bf16[128,2048]{1,0:T(8,128)(2,1)} %add_convert_fusion.1.x_ref), custom_call_target="tpu_custom_call" | custom-call | tf_op jit(solution)/shard_map/gather_rows/pallas_call | solution.py:559
  675.0 7.9 convolution_convert_fusion.2
  683.0 9.7 convert_reduce_fusion.1
  692.7 37.2 %reduce_rows.9 = f32[128,2048]{1,0:T(8,128)} custom-call(bf16[16,128,2048]{2,1,0:T(8,128)(2,1)} %bitcast.307), custom_call_target="tpu_custom_call" | custom-call | tf_op jit(solution)/shard_map/reduce_rows/pallas_call | solution.py:734
  730.0 10.0 convolution_convert_fusion.1
  740.0 36.8 %reduce_rows.10 = f32[128,2048]{1,0:T(8,128)} custom-call(bf16[16,128,2048]{2,1,0:T(8,128)(2,1)} %bitcast.308), custom_call_target="tpu_custom_call" | custom-call | tf_op jit(solution)/shard_map/reduce_rows/pallas_call | solution.py:734
  782.1 33.2 %gather_rows.9 = bf16[16,128,2048]{2,1,0:T(8,128)(2,1)} custom-call(bf16[128,2048]{1,0:T(8,128)(2,1)} %get-tuple-element.78.x_ref), custom_call_target="tpu_custom_call" | custom-call | tf_op jit(solution)/shard_map/gather_rows/pallas_call | solution.py:559
  821.9 15.8 %attend_back.2 = (bf16[8,256,128]{2,1,0:T(8,128)(2,1)}, f32[2,2048,128]{2,1,0:T(8,128)}, f32[2,2048,128]{2,1,0:T(8,128)}) custom-call(s32[8,1,256]{2,1,0:T(1,128)} %max.19.lo_ref, f32[8,1,256]{2,1,0:T(1,128)} %get-tuple-element.46.lse_ref, bf16[8,256,128]{2,1,0:T(8,128)(2,1)} %bitcast.347, bf16[2,2048,128]{2,1,0:T(8,128)(2,1)} %get-tuple-element.104.k_ref, ...), custom_call_target="tpu_custom_call" | custom-call | tf_op jit(solution)/shard_map/attend_back/pallas_call | solution.py:1126
  850.3 49.8 %reduce_window.2 = f32[128,2560]{1,0:T(8,128)} custom-call(bf16[16,128,2560]{2,1,0:T(8,128)(2,1)} %pad_maximum_fusion.x_ref), custom_call_target="tpu_custom_call" | custom-call | tf_op jit(solution)/shard_map/reduce_window/pallas_call | solution.py:734
  907.0 40.3 %gather_rows.10 = bf16[16,128,2048]{2,1,0:T(8,128)(2,1)} custom-call(bf16[128,2048]{1,0:T(8,128)(2,1)} %get-tuple-element.73.x_ref), custom_call_target="tpu_custom_call" | custom-call | tf_op jit(solution)/shard_map/gather_rows/pallas_call | solution.py:559
  947.4 12.7 convert_reduce_fusion.2
  967.5 37.2 %reduce_rows.11 = f32[128,2048]{1,0:T(8,128)} custom-call(bf16[16,128,2048]{2,1,0:T(8,128)(2,1)} %bitcast.309), custom_call_target="tpu_custom_call" | custom-call | tf_op jit(solution)/shard_map/reduce_rows/pallas_call | solution.py:734
  1009.1 33.0 %gather_rows.11 = bf16[16,128,2048]{2,1,0:T(8,128)(2,1)} custom-call(bf16[128,2048]{1,0:T(8,128)(2,1)} %get-tuple-element.76.x_ref), custom_call_target="tpu_custom_call" | custom-call | tf_op jit(solution)/shard_map/gather_rows/pallas_call | solution.py:559
  1048.6 15.8 %attend_back.3 = (bf16[8,256,128]{2,1,0:T(8,128)(2,1)}, f32[2,2048,128]{2,1,0:T(8,128)}, f32[2,2048,128]{2,1,0:T(8,128)}) custom-call(s32[8,1,256]{2,1,0:T(1,128)} %max.19.lo_ref, f32[8,1,256]{2,1,0:T(1,128)} %get-tuple-element.50.lse_ref, bf16[8,256,128]{2,1,0:T(8,128)(2,1)} %bitcast.345, bf16[2,2048,128]{2,1,0:T(8,128)(2,1)} %get-tuple-element.106.k_ref, ...), custom_call_target="tpu_custom_call" | custom-call | tf_op jit(solution)/shard_map/attend_back/pallas_call | solution.py:1126
  1077.3 49.8 %reduce_window.3 = f32[128,2560]{1,0:T(8,128)} custom-call(bf16[16,128,2560]{2,1,0:T(8,128)(2,1)} %pad_maximum_fusion.1.x_ref), custom_call_target="tpu_custom_call" | custom-call | tf_op jit(solution)/shard_map/reduce_window/pallas_call | solution.py:734
  1134.8 11.4 fusion.15
  1146.2 9.8 convolution_convert_fusion.10
  1168.4 8.5 fusion.14
  1194.6 21.4 %reduce_shared.1 = f32[144,256]{1,0:T(8,128)} custom-call(bf16[32,144,256]{2,1,0:T(8,128)(2,1)} %maximum_maximum_fusion.x_ref), custom_call_target="tpu_custom_call" | custom-call | tf_op jit(solution)/shard_map/reduce_shared/pallas_call | solution.py:734
  1226.8 219.8 %return_grads.1 = (bf16[2,128,2048]{2,1,0:T(8,128)(2,1)}, bf16[2,128,8192]{2,1,0:T(8,128)(2,1)}, bf16[2,128,2048]{2,1,0:T(8,128)(2,1)}, bf16[2,512,2048]{2,1,0:T(8,128)(2,1)}) custom-call(bf16[2,16,128,128]{3,2,1,0:T(8,128)(2,1)} %pad_maximum_fusion.8.gq, bf16[2,16,128,512]{3,2,1,0:T(8,128)(2,1)} %pad_maximum_fusion.2.ge, ...), custom_call_target="tpu_custom_call" | custom-call | tf_op jit(solution)/shard_map/return_grads/pallas_call | solution.py:1036
  (313 shorter events, 219.8 us)
Async XLA Ops:
  3.4 32.7 %copy-start = (bf16[2,128,2048]{2,1,0:T(8,128)(2,1)S(1)}, bf16[2,128,2048]{2,1,0:T(8,128)(2,1)}, u32[]{:S(2)}) copy-start(bf16[2,128,2048]{2,1,0:T(8,128)(2,1)} %param.15) | copy-start | bytes 3145732
  9.6 27.4 %copy-start.46 = (s32[2,2048]{1,0:T(2,128)S(1)}, s32[2,2048]{1,0:T(2,128)}, u32[]{:S(2)}) copy-start(s32[2,2048]{1,0:T(2,128)} %param.17) | copy-start | bytes 49156
  35.9 82.0 %copy-start.15 = (bf16[1,16,128,256]{3,2,1,0:T(8,128)(2,1)}, bf16[1,16,128,256]{3,2,1,0:T(8,128)(2,1)S(1)}, u32[]{:S(2)}) copy-start(bf16[1,16,128,256]{3,2,1,0:T(8,128)(2,1)S(1)} %get-tuple-element.98) | copy-start | bytes 3145732
  36.3 40.5 %copy-start.41 = (f32[128]{0:T(128)}, f32[128]{0:T(128)S(1)}, u32[]{:S(2)}) copy-start(f32[128]{0:T(128)S(1)} %broadcast_multiply_fusion.3) | copy-start | bytes 1540
  36.6 40.2 %copy-start.44 = (f32[128]{0:T(128)}, f32[128]{0:T(128)S(1)}, u32[]{:S(2)}) copy-start(f32[128]{0:T(128)S(1)} %fusion.93) | copy-start | bytes 1540
  75.6 49.0 %copy-start.37 = (f32[2048]{0:T(1024)}, f32[2048]{0:T(1024)S(1)}, u32[]{:S(2)}) copy-start(f32[2048]{0:T(1024)S(1)} %get-tuple-element.157) | copy-start | bytes 24580
  75.6 49.0 %copy-start.39 = (f32[2048]{0:T(1024)}, f32[2048]{0:T(1024)S(1)}, u32[]{:S(2)}) copy-start(f32[2048]{0:T(1024)S(1)} %get-tuple-element.138) | copy-start | bytes 24580
  280.3 289.9 %copy-start.27 = (bf16[1,16,128,128]{3,2,1,0:T(8,128)(2,1)}, bf16[1,16,128,128]{3,2,1,0:T(8,128)(2,1)S(1)}, u32[]{:S(2)}) copy-start(bf16[1,16,128,128]{3,2,1,0:T(8,128)(2,1)S(1)} %get-tuple-element.111) | copy-start | bytes 1572868
  287.7 19.0 %copy-start.33 = (bf16[2,128,2048]{2,1,0:T(8,128)(2,1)S(1)}, bf16[2,128,2048]{2,1,0:T(8,128)(2,1)}, u32[]{:S(2)}) copy-start(bf16[2,128,2048]{2,1,0:T(8,128)(2,1)} %get-tuple-element.40) | copy-start | bytes 3145732
  474.6 8.2 copy-start.53
  667.3 15.7 %slice-start.2 = ((s8[8388608]{0:T(1024)(128)(4,1)}), s8[4194304]{0:T(1024)(128)(4,1)S(1)}, s32[]{:S(2)}) async-start(s8[8388608]{0:T(1024)(128)(4,1)} %bitcast.312), calls=%async_computation.2 | async-start | bytes 8388608
  675.0 8.0 copy-start.54
  675.0 7.9 slice-start.3
  906.0 553.6 %collective-permute-start = (bf16[128,2048]{1,0:T(8,128)(2,1)}, bf16[128,2048]{1,0:T(8,128)(2,1)}, u32[]{:S(2)}, u32[]{:S(2)}) collective-permute-start(bf16[128,2048]{1,0:T(8,128)(2,1)} %get-tuple-element.113), channel_id=1, source_target_pairs={{0,16},{16,0},{1,17},{17,1},{2,18},{18,2},{3,19},{19,3},{4,20},{20... | collective-permute-start | bytes 1572872 | tf_op jit(solution)/shard_map/ppermute | solution.py:1330
  947.4 12.8 copy-start.22
  1009.1 33.0 %copy-start.34 = (bf16[2,128,2048]{2,1,0:T(8,128)(2,1)S(1)}, bf16[2,128,2048]{2,1,0:T(8,128)(2,1)}, u32[]{:S(2)}) copy-start(bf16[2,128,2048]{2,1,0:T(8,128)(2,1)} %get-tuple-element.40) | copy-start | bytes 3145732
  1077.2 50.8 %copy-start.1 = (bf16[2,128,2048]{2,1,0:T(8,128)(2,1)S(1)}, bf16[2,128,2048]{2,1,0:T(8,128)(2,1)}, u32[]{:S(2)}) copy-start(bf16[2,128,2048]{2,1,0:T(8,128)(2,1)} %param.15) | copy-start | bytes 3145732
  1077.2 50.8 %copy-start.38 = (f32[2048]{0:T(1024)S(1)}, f32[2048]{0:T(1024)}, u32[]{:S(2)}) copy-start(f32[2048]{0:T(1024)} %copy-done.37) | copy-start | bytes 24580
  1077.2 50.8 %copy-start.42 = (f32[128]{0:T(128)S(1)}, f32[128]{0:T(128)}, u32[]{:S(2)}) copy-start(f32[128]{0:T(128)} %copy-done.41) | copy-start | bytes 1540
  1077.2 52.9 %copy-start.49 = (f32[128]{0:T(128)S(1)}, f32[128]{0:T(128)}, u32[]{:S(2)}) copy-start(f32[128]{0:T(128)} %copy-done.48) | copy-start | bytes 1540
  1077.2 53.0 %copy-start.45 = (f32[128]{0:T(128)S(1)}, f32[128]{0:T(128)}, u32[]{:S(2)}) copy-start(f32[128]{0:T(128)} %copy-done.44) | copy-start | bytes 1540
  1132.6 329.2 %collective-permute-start.1 = (bf16[128,2048]{1,0:T(8,128)(2,1)}, bf16[128,2048]{1,0:T(8,128)(2,1)}, u32[]{:S(2)}, u32[]{:S(2)}) collective-permute-start(bf16[128,2048]{1,0:T(8,128)(2,1)} %get-tuple-element.79), channel_id=1, source_target_pairs={{0,16},{16,0},{1,17},{17,1},{2,18},{18,2},{3,19},{19,3},{4,20},{20... | collective-permute-start | bytes 1572872 | tf_op jit(solution)/shard_map/ppermute | solution.py:1330
  1134.8 11.4 copy-start.55
  1146.2 9.8 copy-start.10
  1146.2 22.2 %slice-start.6 = ((s8[8388608]{0:T(1024)(128)(4,1)}), s8[4194304]{0:T(1024)(128)(4,1)S(1)}, s32[]{:S(2)}) async-start(s8[8388608]{0:T(1024)(128)(4,1)} %bitcast.322), calls=%async_computation.6 | async-start | bytes 8388608
  1156.0 12.4 slice-start.7
  1160.8 16.1 %slice-start.4 = ((s8[8388608]{0:T(1024)(128)(4,1)}), s8[4194304]{0:T(1024)(128)(4,1)S(1)}, s32[]{:S(2)}) async-start(s8[8388608]{0:T(1024)(128)(4,1)} %bitcast.316), calls=%async_computation.4 | async-start | bytes 8388608
  1160.8 23.8 %slice-start = ((s8[8388608]{0:T(1024)(128)(4,1)}), s8[4194304]{0:T(1024)(128)(4,1)S(1)}, s32[]{:S(2)}) async-start(s8[8388608]{0:T(1024)(128)(4,1)} %bitcast.295), calls=%async_computation | async-start | bytes 8388608
  1168.4 8.5 slice-start.5
  1168.4 16.2 %slice-start.1 = ((s8[8388608]{0:T(1024)(128)(4,1)}), s8[4194304]{0:T(1024)(128)(4,1)S(1)}, s32[]{:S(2)}) async-start(s8[8388608]{0:T(1024)(128)(4,1)} %bitcast.295), calls=%async_computation.1 | async-start | bytes 8388608
  1168.4 17.6 %slice-start.9 = ((s8[8388608]{0:T(1024)(128)(4,1)}), s8[4194304]{0:T(1024)(128)(4,1)S(1)}, s32[]{:S(2)}) async-start(s8[8388608]{0:T(1024)(128)(4,1)} %bitcast.396), calls=%async_computation.9 | async-start | bytes 8388608
  1176.9 9.1 slice-start.10
  (38 other events, 163.4 us)

commit v2 on v1

--- a/solution.py
+++ b/solution.py
@@ -459,6 +459,16 @@
 ALL = ("x", 8, 4, 2, 1)
 
 
+def columns(n, wide):
+    return pl.ds(pl.multiple_of(n * wide, wide), wide)
+
+
+def remote(src, dst, send, recv, there):
+    return pltpu.make_async_remote_copy(
+        src_ref=src, dst_ref=dst, send_sem=send, recv_sem=recv, device_id=there, device_id_type=MESH
+    )
+
+
 class Hyper:
     def __init__(self, dims):
         sec = lax.axis_index("section")
@@ -573,25 +583,47 @@
     )(x)
 
 
-def gather_window_kernel(parts, x_ref, kv_ref, o_ref, okv_ref, far, *sems):
-    send_sem, recv_sem, kv_send, kv_recv, own_sem, swap_send, swap_recv = sems
+def gather_window_kernel(parts, weights, *refs):
+    if weights:
+        x_ref, kv_ref, exp, con, o_ref, okv_ref, we, wc, far = refs[:9]
+        sems = refs[9:]
+        spread_sems = sems[7:]
+    else:
+        x_ref, kv_ref, o_ref, okv_ref, far = refs[:5]
+        sems = refs[5:]
+    send_sem, recv_sem, kv_send, kv_recv, own_sem, swap_send, swap_recv = sems[:7]
     h = Hyper(CUBE)
     sec, shd = lax.axis_index("section"), lax.axis_index("shard")
+    low = lax.rem(shd, 8)
     other = (sec, shd + 8 * (1 - 2 * lax.rem(shd // 8, 2)))
-    h.barrier((other,))
-    swap = pltpu.make_async_remote_copy(
-        src_ref=kv_ref,
-        dst_ref=far,
-        send_sem=swap_send,
-        recv_sem=swap_recv,
-        device_id=other,
-        device_id_type=MESH,
-    )
+    if weights:
+        w_send, w_recv, con_send, con_recv, w_own = spread_sems
+
+        def pieces(ts, tj):
+            for n in range(2):
+                yield (
+                    exp.at[:, columns(2 * (8 * n + lax.rem(tj, 8)) + ts, 256)],
+                    we.at[sec, low, :, pl.ds(256 * n, 256)],
+                )
+
+        spread = Spread(pieces, w_own, w_send, w_recv)
+        spread.barrier()
+    else:
+        h.barrier((other,))
+    swap = remote(kv_ref, far, swap_send, swap_recv, other)
     swap.start()
     own = pltpu.make_async_copy(x_ref, o_ref.at[h.pos], own_sem.at[0])
     own.start()
     g = Gather(h, parts, x_ref, o_ref, send_sem, recv_sem)
     g.start(range(3))
+    if weights:
+        spread.start()
+        own_rows = pltpu.make_async_copy(con.at[pl.ds(256 * sec, 256)], wc.at[sec], w_own.at[2])
+        own_rows.start()
+        rows = remote(
+            con.at[pl.ds(256 * (1 - sec), 256)], wc.at[sec], con_send, con_recv, (1 - sec, shd)
+        )
+        rows.start()
     swap.wait_recv()
     own_kv = pltpu.make_async_copy(far, okv_ref.at[h.pos], own_sem.at[1])
     own_kv.start()
@@ -600,12 +632,19 @@
     gkv.start(range(1))
     k = len(CUBE)
     for j in range(k):
-        for low in range(1 << j):
+        for n in range(1 << j):
             for one, chosen in ((g, range(3)), (gkv, range(1))):
                 for p in chosen:
-                    one.copy(p, low, j).wait_recv()
+                    one.copy(p, n, j).wait_recv()
                     for later in range(j + 1, k):
-                        one.copy(p, low | 1 << j, later).start()
+                        one.copy(p, n | 1 << j, later).start()
+    if weights:
+        spread.wait()
+        remote(
+            con.at[pl.ds(0, 256)], wc.at[1 - sec], con_send, con_recv, (1 - sec, shd)
+        ).wait_recv()
+        rows.wait_send()
+        own_rows.wait()
     g.finish()
     gkv.finish()
     swap.wait_send()
@@ -613,418 +652,368 @@
     own_kv.wait()
 
 
-def gather_window(x, kv, collective_id):
+def gather_window(x, kv, collective_id, weights=()):
     parts = cube_parts(x.shape[0], (768, 640, 640))
     n = 16
+    dma = pltpu.SemaphoreType.DMA
+    out = [
+        jax.ShapeDtypeStruct((n,) + x.shape, x.dtype),
+        jax.ShapeDtypeStruct((n,) + kv.shape, kv.dtype),
+    ]
+    sems = [dma((3, n)), dma((3, n)), dma((1, n)), dma((1, n)), dma((2,)), dma, dma]
+    if weights:
+        out += [
+            jax.ShapeDtypeStruct((2, 8, 128, 512), kv.dtype),
+            jax.ShapeDtypeStruct((2, 256, D), kv.dtype),
+        ]
+        sems += [dma((2, 16)), dma((2, 16)), dma, dma, dma((3,))]
     return pl.pallas_call(
-        functools.partial(gather_window_kernel, parts),
-        out_shape=(
-            jax.ShapeDtypeStruct((n,) + x.shape, x.dtype),
-            jax.ShapeDtypeStruct((n,) + kv.shape, kv.dtype),
-        ),
-        in_specs=[pl.BlockSpec(memory_space=pl.ANY)] * 2,
-        out_specs=[pl.BlockSpec(memory_space=pl.ANY)] * 2,
-        scratch_shapes=[
-            pltpu.VMEM(kv.shape, kv.dtype),
-            pltpu.SemaphoreType.DMA((3, n)),
-            pltpu.SemaphoreType.DMA((3, n)),
-            pltpu.SemaphoreType.DMA((1, n)),
-            pltpu.SemaphoreType.DMA((1, n)),
-            pltpu.SemaphoreType.DMA((2,)),
-            pltpu.SemaphoreType.DMA,
-            pltpu.SemaphoreType.DMA,
-        ],
+        functools.partial(gather_window_kernel, parts, bool(weights)),
+        out_shape=out,
+        in_specs=[pl.BlockSpec(memory_space=pl.ANY)] * (2 + len(weights)),
+        out_specs=[pl.BlockSpec(memory_space=pl.ANY)] * len(out),
+        scratch_shapes=[pltpu.VMEM(kv.shape, kv.dtype)] + sems,
         compiler_params=pltpu.CompilerParams(
             collective_id=collective_id, has_side_effects=True, vmem_limit_bytes=LIMIT
         ),
         name="gather_window",
-    )(x, kv)
-
-
-def reduce_kernel(dims, parts, swap_cols, x_ref, o_ref, *scratch):
-    if swap_cols:
-        buf, send_sem, recv_sem, swapped, swap_send, swap_recv = scratch
-    else:
-        buf, send_sem, recv_sem = scratch
+    )(x, kv, *weights)
+
+
+class Reduce:
+    def __init__(self, h, parts, src, buf, send_sem, recv_sem):
+        self.h, self.parts, self.src, self.buf = h, parts, src, buf
+        self.send_sem, self.recv_sem = send_sem, recv_sem
+
+    def window(self, p):
+        r0, rn, c0, cn, order = self.parts[p]
+        return pl.ds(r0, rn), pl.ds(c0, cn)
+
+    def held(self, p, j, offset):
+        if j == len(self.h.dims) - 1:
+            return self.src.at[(self.h.at(self.parts[p][4], offset),) + self.window(p)]
+        return self.buf.at[((1 << (j + 1)) | offset,) + self.window(p)]
+
+    def copy(self, p, j, low):
+        n = (1 << j) | low
+        return remote(
+            self.held(p, j, low | 1 << j),
+            self.buf.at[(n,) + self.window(p)],
+            self.send_sem.at[p, n],
+            self.recv_sem.at[p, n],
+            self.h.partner[self.parts[p][4][j]],
+        )
+
+    def add(self, p, j, low, out=None):
+        self.copy(p, j, low).wait_recv()
+        r0, rn, c0, cn, order = self.parts[p]
+        mine = self.held(p, j, low)
+        came = self.buf.at[((1 << j) | low,) + self.window(p)]
+        step = 16
+
+        @pl.loop(0, rn // step)
+        def _(i):
+            rows = pl.ds(pl.multiple_of(i * step, step), step)
+            total = mine[rows, :].astype(jnp.float32) + came[rows, :].astype(jnp.float32)
+            if j > 0:
+                came[rows, :] = total.astype(came.dtype)
+            else:
+                out[pl.ds(pl.multiple_of(r0 + i * step, step), step), pl.ds(c0, cn)] = total
+
+        if j > 0 and low >> (j - 1) & 1:
+            self.copy(p, j - 1, low ^ (1 << (j - 1))).start()
+
+    def finish(self):
+        for p in range(len(self.parts)):
+            for j in range(len(self.h.dims)):
+                for low in range(1 << j):
+                    self.copy(p, j, low).wait_send()
+
+
+def reduce_kernel(dims, all_parts, swapped, *refs):
+    count = len(all_parts)
+    xs, outs, bufs = refs[:count], refs[count : 2 * count], refs[2 * count : 3 * count]
+    sems = refs[3 * count :]
     h = Hyper(dims)
     k = len(dims)
     sec, shd = lax.axis_index("section"), lax.axis_index("shard")
     other = (sec, shd + 8 * (1 - 2 * lax.rem(shd // 8, 2)))
-    h.barrier((other,) if swap_cols else ())
-
-    def window(p):
-        r0, rn, c0, cn, order = parts[p]
-        return pl.ds(r0, rn), pl.ds(c0, cn)
-
-    def held(p, j, offset):
-        if j == k - 1:
-            return x_ref.at[(h.at(parts[p][4], offset),) + window(p)]
-        return buf.at[((1 << (j + 1)) | offset,) + window(p)]
-
-    def copy(p, j, low):
-        n = (1 << j) | low
-        return pltpu.make_async_remote_copy(
-            src_ref=held(p, j, low | 1 << j),
-            dst_ref=buf.at[(n,) + window(p)],
-            send_sem=send_sem.at[p, n],
-            recv_sem=recv_sem.at[p, n],
-            device_id=h.partner[parts[p][4][j]],
-            device_id_type=MESH,
-        )
-
+    h.barrier((other,) if swapped else ())
+    sums = [
+        Reduce(h, parts, xs[n], bufs[n], sems[2 * n], sems[2 * n + 1])
+        for n, parts in enumerate(all_parts)
+    ]
+    every = [(r, p, outs[n]) for n, r in enumerate(sums) for p in range(len(all_parts[n]))]
     for low in reversed(range(1 << (k - 1))):
-        for p in range(len(parts)):
-            copy(p, k - 1, low).start()
-    step = 16
+        for r, p, _ in every:
+            r.copy(p, k - 1, low).start()
     for j in reversed(range(k)):
         for low in reversed(range(1 << j)):
-            for p in range(len(parts)):
-                r0, rn, c0, cn, order = parts[p]
-                copy(p, j, low).wait_recv()
-                mine = held(p, j, low)
-                came = buf.at[((1 << j) | low,) + window(p)]
-
-                @pl.loop(0, rn // step)
-                def _(i):
-                    rows = pl.ds(pl.multiple_of(i * step, step), step)
-                    total = mine[rows, :].astype(jnp.float32) + came[rows, :].astype(jnp.float32)
-                    if j > 0:
-                        came[rows, :] = total.astype(came.dtype)
-                    else:
-                        out_rows = pl.ds(pl.multiple_of(r0 + i * step, step), step)
-                        o_ref[out_rows, pl.ds(c0, cn)] = total
-
-                if j > 0 and low >> (j - 1) & 1:
-                    copy(p, j - 1, low ^ (1 << (j - 1))).start()
-    if swap_cols:
-        c0, cn = swap_cols
-        rows = x_ref.shape[1]
-        swapped[0] = o_ref[:, c0 : c0 + cn].astype(swapped.dtype)
-        swap = pltpu.make_async_remote_copy(
-            src_ref=swapped.at[0],
-            dst_ref=swapped.at[1],
-            send_sem=swap_send,
-            recv_sem=swap_recv,
-            device_id=other,
-            device_id_type=MESH,
-        )
+            for r, p, out in every:
+                r.add(p, j, low, out)
+    if swapped:
+        sent, swap_send, swap_recv = sems[2 * count :]
+        out = outs[-1]
+        sent[0] = out[...].astype(sent.dtype)
+        swap = remote(sent.at[0], sent.at[1], swap_send, swap_recv, other)
         swap.start()
         swap.wait()
-        o_ref[:, c0 : c0 + cn] = swapped[1].astype(jnp.float32)
-    for p in range(len(parts)):
-        for j in range(k):
-            for low in range(1 << j):
-                copy(p, j, low).wait_send()
-
-
-def reduce(x, dims, parts, collective_id, name, swap_cols=None):
+        out[...] = sent[1].astype(jnp.float32)
+    for r in sums:
+        r.finish()
+
+
+def reduce(xs, dims, all_parts, collective_id, name, swapped=False):
     n = 1 << len(dims)
-    block = x.shape[1:]
-    scratch = [
-        pltpu.VMEM((n,) + block, x.dtype),
-        pltpu.SemaphoreType.DMA((len(parts), n)),
-        pltpu.SemaphoreType.DMA((len(parts), n)),
-    ]
-    if swap_cols:
-        scratch += [
-            pltpu.VMEM((2, block[0], swap_cols[1]), x.dtype),
-            pltpu.SemaphoreType.DMA,
-            pltpu.SemaphoreType.DMA,
-        ]
+    dma = pltpu.SemaphoreType.DMA
+    vmem = pl.BlockSpec(memory_space=pltpu.VMEM)
+    scratch = [pltpu.VMEM(x.shape, x.dtype) for x in xs]
+    for parts in all_parts:
+        scratch += [dma((len(parts), n))] * 2
+    if swapped:
+        scratch += [pltpu.VMEM((2,) + xs[-1].shape[1:], xs[-1].dtype), dma, dma]
     return pl.pallas_call(
-        functools.partial(reduce_kernel, dims, parts, swap_cols),
-        out_shape=jax.ShapeDtypeStruct(block, jnp.float32),
-        in_specs=[pl.BlockSpec(memory_space=pltpu.VMEM)],
-        out_specs=pl.BlockSpec(memory_space=pltpu.VMEM),
+        functools.partial(reduce_kernel, dims, all_parts, swapped),
+        out_shape=[jax.ShapeDtypeStruct(x.shape[1:], jnp.float32) for x in xs],
+        in_specs=[vmem] * len(xs),
+        out_specs=[vmem] * len(xs),
         scratch_shapes=scratch,
         compiler_params=pltpu.CompilerParams(
             collective_id=collective_id, has_side_effects=True, vmem_limit_bytes=LIMIT
         ),
         name=name,
-    )(x)
+    )(*xs)
 
 
 def block_of(sec, shd):
     return 8 * lax.rem(sec + lax.rem(shd, 2), 2) + lax.rem(shd, 8)
 
 
-def everyone_barrier(me):
+def half_group(sec, shd):
+    first = 8 * (shd // 8)
+    return 8 * sec + lax.rem(shd, 8), lambda n: (n // 8, first + lax.rem(n, 8))
+
+
+def half_barrier(me, place, sec, shd):
     sem = pltpu.get_barrier_semaphore()
 
-    @pl.loop(1, 32)
+    @pl.loop(1, 16)
     def _(d):
-        there = lax.rem(me + d, 32)
         pl.semaphore_signal(
-            sem, inc=1, device_id=(there // 16, lax.rem(there, 16)), device_id_type=MESH
+            sem, inc=1, device_id=place(lax.rem(me + d, 16)), device_id_type=MESH
         )
 
-    pl.semaphore_wait(sem, 31)
-
-
-def fetch_kernel(mix, exp, out, con, wq, we, wo, wc, *sems):
-    q_send, q_recv, e_send, e_recv, row_send, row_recv, own_sem = sems
+    across = shd + 8 * (1 - 2 * (shd // 8))
+    for s in range(2):
+        pl.semaphore_signal(sem, inc=1, device_id=(s, across), device_id_type=MESH)
+    pl.semaphore_wait(sem, 17)
+
+
+class Spread:
+    def __init__(self, pieces, own_sem, send, recv):
+        self.sec, self.shd = lax.axis_index("section"), lax.axis_index("shard")
+        self.me, self.place = half_group(self.sec, self.shd)
+        self.pieces, self.own_sem, self.send, self.recv = pieces, own_sem, send, recv
+
+    def barrier(self):
+        half_barrier(self.me, self.place, self.sec, self.shd)
+
+    def copies(self, d):
+        there = self.place(lax.rem(self.me + d, 16))
+        return [
+            remote(src, dst, self.send.at[n, d], self.recv.at[n, d], there)
+            for n, (src, dst) in enumerate(self.pieces(*there))
+        ]
+
+    def own(self):
+        return [
+            pltpu.make_async_copy(src, dst, self.own_sem.at[n])
+            for n, (src, dst) in enumerate(self.pieces(self.sec, self.shd))
+        ]
+
+    def start(self):
+        @pl.loop(1, 16)
+        def _(d):
+            for one in self.copies(d):
+                one.start()
+
+        for one in self.own():
+            one.start()
+
+    def wait(self):
+        @pl.loop(1, 16)
+        def _(d):
+            for one in self.copies(d):
+                one.wait_recv()
+
+        @pl.loop(1, 16)
+        def _(d):
+            for one in self.copies(d):
+                one.wait_send()
+
+        for one in self.own():
+            one.wait()
+
+
+def first_kernel(block, mix, out, shared, wq, wo, *sems):
+    send, recv, out_send, out_recv, own_sem, sh_send, sh_recv = sems
     sec, shd = lax.axis_index("section"), lax.axis_index("shard")
-    me = sec * 16 + shd
-    everyone_barrier(me)
-    f = block_of(sec, shd)
-
-    def column_copies(d):
-        there = lax.rem(me + d, 32)
-        ts, tj = there // 16, lax.rem(there, 16)
-        tf = block_of(ts, tj)
-        result = []
-        for src, dst, send, recv, wide in ((mix, wq, q_send, q_recv, HD), (exp, we, e_send, e_recv, 512)):
-            result.append(
-                pltpu.make_async_remote_copy(
-                    src_ref=src.at[:, pl.ds(pl.multiple_of(tf * wide, wide), wide)],
-                    dst_ref=dst.at[sec, shd],
-                    send_sem=send.at[d],
-                    recv_sem=recv.at[d],
-                    device_id=(ts, tj),
-                    device_id_type=MESH,
-                )
-            )
-        return result
-
-    own = [
-        pltpu.make_async_copy(
-            mix.at[:, pl.ds(pl.multiple_of(f * HD, HD), HD)], wq.at[sec, shd], own_sem.at[0]
-        ),
-        pltpu.make_async_copy(
-            exp.at[:, pl.ds(pl.multiple_of(f * 512, 512), 512)], we.at[sec, shd], own_sem.at[1]
-        ),
-    ]
-    for one in own:
-        one.start()
-
-    @pl.loop(1, 32)
-    def _(d):
-        for one in column_copies(d):
-            one.start()
-
-    low = lax.rem(shd, 8)
-    half = shd // 8
+    low, half = lax.rem(shd, 8), shd // 8
+
+    def pieces(ts, tj):
+        yield mix.at[:, columns(block_of(ts, tj), HD)], wq.at[sec, low]
+
+    spread = Spread(pieces, own_sem, send, recv)
+    spread.barrier()
+    h = Hyper(ALL)
+    own_block = pltpu.make_async_copy(block, shared.at[h.pos], own_sem.at[1])
+    own_block.start()
+    g = Gather(h, SMALL, block, shared, sh_send, sh_recv)
+    g.start(range(3))
+    spread.start()
+
     to_x = lax.rem(half + lax.rem(shd, 2), 2)
     from_half = lax.rem(sec + lax.rem(shd, 2), 2)
-
-    def row_copies(z):
-        return [
-            pltpu.make_async_remote_copy(
-                src_ref=src,
-                dst_ref=dst.at[sec],
-                send_sem=row_send.at[n, z],
-                recv_sem=row_recv.at[n, sec],
-                device_id=(to_x, 8 * z + low),
-                device_id_type=MESH,
-            )
-            for n, (src, dst) in enumerate(((out, wo), (con, wc)))
-        ]
-
-    def arrivals(s):
-        return [
-            pltpu.make_async_remote_copy(
-                src_ref=src,
-                dst_ref=dst.at[s],
-                send_sem=row_send.at[n, 0],
-                recv_sem=row_recv.at[n, s],
-                device_id=(to_x, low),
-                device_id_type=MESH,
-            )
-            for n, (src, dst) in enumerate(((out, wo), (con, wc)))
-        ]
-
-    def own_rows():
-        return [
-            pltpu.make_async_copy(src, dst.at[sec], own_sem.at[2 + n])
-            for n, (src, dst) in enumerate(((out, wo), (con, wc)))
-        ]
-
+    own_out = pltpu.make_async_copy(out, wo.at[sec], own_sem.at[2])
     for z in range(2):
         mine = jnp.logical_and(to_x == sec, half == z)
+        there = remote(out, wo.at[sec], out_send.at[z], out_recv.at[sec], (to_x, 8 * z + low))
 
         @pl.when(mine)
         def _():
-            for one in own_rows():
-                one.start()
+            own_out.start()
 
         @pl.when(jnp.logical_not(mine))
         def _():
-            for one in row_copies(z):
-                one.start()
-
-    @pl.loop(1, 32)
-    def _(d):
-        for one in column_copies(d):
-            one.wait_recv()
-
+            there.start()
+
+    g.forward(range(3))
+    spread.wait()
     for s in range(2):
         mine = jnp.logical_and(sec == s, from_half == half)
 
         @pl.when(jnp.logical_not(mine))
         def _():
-            for one in arrivals(s):
-                one.wait_recv()
-
-    @pl.loop(1, 32)
-    def _(d):
-        for one in column_copies(d):
-            one.wait_send()
+            remote(out, wo.at[s], out_send.at[0], out_recv.at[s], (1 - sec, shd)).wait_recv()
 
     for z in range(2):
         mine = jnp.logical_and(to_x == sec, half == z)
+        there = remote(out, wo.at[sec], out_send.at[z], out_recv.at[sec], (to_x, 8 * z + low))
 
         @pl.when(mine)
         def _():
-            for one in own_rows():
-                one.wait()
+            own_out.wait()
 
         @pl.when(jnp.logical_not(mine))
         def _():
-            for one in row_copies(z):
-                one.wait_send()
-
-    for one in own:
-        one.wait()
-
-
-def fetch_weights(mix, exp, out, con):
+            there.wait_send()
+
+    g.finish()
+    own_block.wait()
+
+
+def fetch_first(block, mix, out):
     bf16 = jnp.bfloat16
     dma = pltpu.SemaphoreType.DMA
     return pl.pallas_call(
-        fetch_kernel,
+        first_kernel,
         out_shape=(
-            jax.ShapeDtypeStruct((2, 16, 128, HD), bf16),
-            jax.ShapeDtypeStruct((2, 16, 128, 512), bf16),
+            jax.ShapeDtypeStruct((32,) + block.shape, bf16),
+            jax.ShapeDtypeStruct((2, 8, 128, HD), bf16),
             jax.ShapeDtypeStruct((2, 128, D), bf16),
-            jax.ShapeDtypeStruct((2, 512, D), bf16),
         ),
-        in_specs=[pl.BlockSpec(memory_space=pl.ANY)] * 4,
-        out_specs=[pl.BlockSpec(memory_space=pl.ANY)] * 4,
-        scratch_shapes=[dma((32,)), dma((32,)), dma((32,)), dma((32,)), dma((2, 2)), dma((2, 2)), dma((4,))],
+        in_specs=[pl.BlockSpec(memory_space=pl.ANY)] * 3,
+        out_specs=[pl.BlockSpec(memory_space=pl.ANY)] * 3,
+        scratch_shapes=[dma((1, 16)), dma((1, 16)), dma((2,)), dma((2,)), dma((3,)), dma((3, 32)), dma((3, 32))],
         compiler_params=pltpu.CompilerParams(
             collective_id=1, has_side_effects=True, vmem_limit_bytes=LIMIT
         ),
-        name="fetch_weights",
-    )(mix, exp, out, con)
+        name="fetch_first",
+    )(block, mix, out)
 
 
 def return_kernel(gq, ge, go, gc, rq, re, ro, rc, *sems):
-    q_send, q_recv, e_send, e_recv, row_send, row_recv, own_sem = sems
+    send, recv, con_send, con_recv, out_send, out_recv, own_sem = sems
     sec, shd = lax.axis_index("section"), lax.axis_index("shard")
-    me = sec * 16 + shd
-    everyone_barrier(me)
+    me, place = half_group(sec, shd)
+    half_barrier(me, place, sec, shd)
+    low, half = lax.rem(shd, 8), shd // 8
     f = block_of(sec, shd)
-    low = lax.rem(shd, 8)
-    half = shd // 8
-
-    def column_copies(d):
-        there = lax.rem(me + d, 32)
-        ts, tj = there // 16, lax.rem(there, 16)
-        result = []
-        for src, dst, send, recv, wide in ((gq, rq, q_send, q_recv, HD), (ge, re, e_send, e_recv, 512)):
-            result.append(
-                pltpu.make_async_remote_copy(
-                    src_ref=src.at[ts, tj],
-                    dst_ref=dst.at[half, :, pl.ds(pl.multiple_of(f * wide, wide), wide)],
-                    send_sem=send.at[d],
-                    recv_sem=recv.at[d],
-                    device_id=(ts, tj),
-                    device_id_type=MESH,
-                )
+
+    def pieces(ts, tj):
+        tlow = lax.rem(tj, 8)
+        yield gq.at[ts, tlow], rq.at[:, columns(f, HD)]
+        for h in range(2):
+            yield (
+                ge.at[ts, tlow, :, pl.ds(256 * h, 256)],
+                re.at[:, columns(2 * (8 * h + low) + sec, 256)],
             )
-        return result
+
+    def spread(d):
+        there = place(lax.rem(me + d, 16))
+        return [
+            remote(src, dst, send.at[n, d], recv.at[n, d], there)
+            for n, (src, dst) in enumerate(pieces(*there))
+        ]
+
+    @pl.loop(1, 16)
+    def _(d):
+        for one in spread(d):
+            one.start()
 
     own = [
-        pltpu.make_async_copy(
-            gq.at[sec, shd], rq.at[half, :, pl.ds(pl.multiple_of(f * HD, HD), HD)], own_sem.at[0]
-        ),
-        pltpu.make_async_copy(
-            ge.at[sec, shd], re.at[half, :, pl.ds(pl.multiple_of(f * 512, 512), 512)], own_sem.at[1]
-        ),
+        pltpu.make_async_copy(src, dst, own_sem.at[n])
+        for n, (src, dst) in enumerate(pieces(sec, shd))
     ]
+    own.append(pltpu.make_async_copy(gc.at[sec], rc.at[pl.ds(256 * sec, 256)], own_sem.at[3]))
     for one in own:
         one.start()
-
-    def row_copies(s):
-        return [
-            pltpu.make_async_remote_copy(
-                src_ref=src.at[s],
-                dst_ref=dst.at[half],
-                send_sem=row_send.at[n, s],
-                recv_sem=row_recv.at[n, half],
-                device_id=(s, f),
-                device_id_type=MESH,
-            )
-            for n, (src, dst) in enumerate(((go, ro), (gc, rc)))
-        ]
-
-    def arrivals(z):
-        return [
-            pltpu.make_async_remote_copy(
-                src_ref=src.at[0],
-                dst_ref=dst.at[z],
-                send_sem=row_send.at[n, 0],
-                recv_sem=row_recv.at[n, z],
-                device_id=(sec, f),
-                device_id_type=MESH,
-            )
-            for n, (src, dst) in enumerate(((go, ro), (gc, rc)))
-        ]
-
-    def own_rows():
-        return [
-            pltpu.make_async_copy(src.at[sec], dst.at[half], own_sem.at[2 + n])
-            for n, (src, dst) in enumerate(((go, ro), (gc, rc)))
-        ]
-
+    rows = remote(gc.at[1 - sec], rc.at[pl.ds(256 * sec, 256)], con_send, con_recv, (1 - sec, shd))
+    rows.start()
+
+    own_out = pltpu.make_async_copy(go.at[sec], ro.at[half], own_sem.at[4])
     for s in range(2):
         mine = jnp.logical_and(sec == s, f == shd)
+        there = remote(go.at[s], ro.at[half], out_send.at[s], out_recv.at[half], (s, f))
 
         @pl.when(mine)
         def _():
-            for one in own_rows():
-                one.start()
+            own_out.start()
 
         @pl.when(jnp.logical_not(mine))
         def _():
-            for one in row_copies(s):
-                one.start()
-
-    @pl.loop(1, 32)
+            there.start()
+
+    @pl.loop(1, 16)
     def _(d):
-        for one in column_copies(d):
-            one.start()
-
-    @pl.loop(1, 32)
-    def _(d):
-        for one in column_copies(d):
+        for one in spread(d):
             one.wait_recv()
 
+    remote(gc.at[0], rc.at[pl.ds(256 * (1 - sec), 256)], con_send, con_recv, (1 - sec, shd)).wait_recv()
     for z in range(2):
         mine = jnp.logical_and(f == shd, half == z)
 
         @pl.when(jnp.logical_not(mine))
         def _():
-            for one in arrivals(z):
-                one.wait_recv()
-
-    @pl.loop(1, 32)
+            remote(go.at[0], ro.at[z], out_send.at[0], out_recv.at[z], (1 - sec, shd)).wait_recv()
+
+    @pl.loop(1, 16)
     def _(d):
-        for one in column_copies(d):
+        for one in spread(d):
             one.wait_send()
 
+    rows.wait_send()
     for s in range(2):
         mine = jnp.logical_and(sec == s, f == shd)
+        there = remote(go.at[s], ro.at[half], out_send.at[s], out_recv.at[half], (s, f))
 
         @pl.when(mine)
         def _():
-            for one in own_rows():
-                one.wait()
+            own_out.wait()
 
         @pl.when(jnp.logical_not(mine))
         def _():
-            for one in row_copies(s):
-                one.wait_send()
+            there.wait_send()
 
     for one in own:
         one.wait()
@@ -1036,14 +1025,14 @@
     return pl.pallas_call(
         return_kernel,
         out_shape=(
+            jax.ShapeDtypeStruct((128, D), bf16),
+            jax.ShapeDtypeStruct((128, 8192), bf16),
             jax.ShapeDtypeStruct((2, 128, D), bf16),
-            jax.ShapeDtypeStruct((2, 128, 8192), bf16),
-            jax.ShapeDtypeStruct((2, 128, D), bf16),
-            jax.ShapeDtypeStruct((2, 512, D), bf16),
+            jax.ShapeDtypeStruct((512, D), bf16),
         ),
         in_specs=[pl.BlockSpec(memory_space=pl.ANY)] * 4,
         out_specs=[pl.BlockSpec(memory_space=pl.ANY)] * 4,
-        scratch_shapes=[dma((32,)), dma((32,)), dma((32,)), dma((32,)), dma((2, 2)), dma((2, 2)), dma((4,))],
+        scratch_shapes=[dma((3, 16)), dma((3, 16)), dma, dma, dma((2,)), dma((2,)), dma((5,))],
         compiler_params=pltpu.CompilerParams(
             collective_id=2, has_side_effects=True, vmem_limit_bytes=LIMIT
         ),
@@ -1051,11 +1040,256 @@
     )(gq, ge, go, gc)
 
 
+HALVES = [[n, n + 8] for n in range(8)]
+
+
+def from_halves(x):
+    return lax.all_gather(x, "shard", axis=0, tiled=True, axis_index_groups=HALVES)
+
+
+def to_halves(x):
+    return lax.psum_scatter(x, "shard", scatter_dimension=0, tiled=True, axis_index_groups=HALVES)
+
+
+NT = (((1,), (1,)), ((), ()))
+TN = (((0,), (0,)), ((), ()))
+
+
+def dot32(a, b):
+    return jnp.dot(a, b, preferred_element_type=jnp.float32)
+
+
+def dot_nt(a, b):
+    return lax.dot_general(a, b, NT, preferred_element_type=jnp.float32)
+
+
+def dot_tn(a, b):
+    return lax.dot_general(a, b, TN, preferred_element_type=jnp.float32)
+
+
+PLAIN = cube_parts(128, (768, 640, 640))
+TRIO = ("x", 4, 2)
+CHUNK = 64
+
+
+def spaced(many, few):
+    result = []
+    for n, step in enumerate(many):
+        result.append(step)
+        done = len(few) * (n + 1) // len(many)
+        result.extend(few[len(few) * n // len(many) : done])
+    return result
+
+
+def chunk_gather_steps(g, count):
+    k = len(g.h.dims)
+
+    def step(j, low):
+        for p in range(count):
+            g.copy(p, low, j).wait_recv()
+            for later in range(j + 1, k):
+                g.copy(p, low | 1 << j, later).start()
+
+    return [functools.partial(step, j, low) for j in range(k) for low in range(1 << j)]
+
+
+def chunk_reduce_steps(r, out):
+    k = len(r.h.dims)
+    return [
+        functools.partial(r.add, p, j, low, out)
+        for j in reversed(range(k))
+        for low in reversed(range(1 << j))
+        for p in range(len(r.parts))
+    ]
+
+
+GELU_K = (2.0 / 3.141592653589793) ** 0.5
+
+
+def gelu_pair(u):
+    square = u * u
+    t = jnp.tanh(GELU_K * (u + 0.044715 * u * square))
+    half = 0.5 * (1.0 + t)
+    slope = half + 0.5 * u * (1.0 - t * t) * (GELU_K * (1.0 + 3 * 0.044715 * square))
+    return u * half, slope
+
+
+def hidden_kernel(back, *refs):
+    if back:
+        x_ref, we_hbm, wc_hbm, slope_hbm, o_ref, x_out, h_out = refs[:7]
+        scratch = refs[7:]
+    else:
+        x_ref, we_hbm, wc_hbm, be_ref, o_ref, x_out, h_out, slope_out = refs[:8]
+        scratch = refs[8:]
+    x_all, we, wc, h_all, slope, part, came, buf = scratch[:8]
+    g_send, g_recv, c_send, c_recv, r_send, r_recv, own_sem, load_sem, out_sem = scratch[8:]
+    h = Hyper(CUBE)
+    trio = Hyper(TRIO)
+    h.barrier()
+    loads = [pltpu.make_async_copy(we_hbm, we, load_sem.at[0]), pltpu.make_async_copy(wc_hbm, wc, load_sem.at[1])]
+    if back:
+        loads.append(pltpu.make_async_copy(slope_hbm, slope, load_sem.at[2]))
+    parts = tuple((0, CHUNK, c0, cn, order) for _, _, c0, cn, order in PLAIN)
+    gathers, sums = [], []
+    for n in range(2):
+        mine = x_ref.at[pl.ds(CHUNK * n, CHUNK)]
+        own = pltpu.make_async_copy(mine, x_all.at[n, h.pos], own_sem.at[n])
+        own.start()
+        loads.append(own)
+        gathers.append(Gather(h, parts, mine, x_all.at[n], g_send.at[n], g_recv.at[n]))
+        sums.append(
+            Reduce(
+                trio,
+                tuple((0, CHUNK, c0, cn, order[:3]) for _, _, c0, cn, order in PLAIN),
+                came.at[n],
+                buf.at[n],
+                r_send.at[n],
+                r_recv.at[n],
+            )
+        )
+        gathers[n].start(range(3))
+    for one in loads[:-2]:
+        one.start()
+    core = 1 - lax.rem(lax.axis_index("shard"), 2)
+
+    def quad(r):
+        return 4 * (h.pos // 4) + (h.delta["x"] if r & 2 else 0) + (h.delta[4] if r & 1 else 0)
+
+    def pair(r, y):
+        return quad(r) + 2 * (lax.rem(h.pos, 4) // 2) + (h.delta[2] if y else 0)
+
+    def compute(n, r):
+        four = pl.ds(quad(r), 4)
+        x = x_all[n, four].reshape(4 * CHUNK, D)
+        if back:
+            inner = dot_nt(x, wc[...]).reshape(4, CHUNK, 512)
+            mid = (inner * slope[n, four].astype(jnp.float32)).astype(jnp.bfloat16)
+        else:
+            inner = dot32(x, we[...]) + be_ref[...]
+            act, grad = gelu_pair(inner)
+            mid = act.astype(jnp.bfloat16).reshape(4, CHUNK, 512)
+            slope[n, four] = grad.astype(jnp.bfloat16).reshape(4, CHUNK, 512)
+        h_all[n, four] = mid
+        mid = mid.reshape(4 * CHUNK, 512)
+        for c in range(4):
+            cols = pl.ds(512 * c, 512)
+            tile = dot_nt(mid, we[cols, :]) if back else dot32(mid, wc[:, cols])
+            part[n, four, :, cols] = tile.astype(jnp.bfloat16).reshape(4, CHUNK, 512)
+        for y in reversed(range(2)):
+            core_copy(n, r, y).start()
+
+    def core_copy(n, r, y):
+        at = pair(r, y)
+        return remote(
+            part.at[n, at + core],
+            came.at[n, at // 2],
+            c_send.at[n, 2 * r + y],
+            c_recv.at[n, 2 * r + y],
+            h.partner[1],
+        )
+
+    def core_add(n, r):
+        for y in reversed(range(2)):
+            core_copy(n, r, y).wait_recv()
+            at = pair(r, y)
+
+            @pl.loop(0, CHUNK // 16)
+            def _(i):
+                rows = pl.ds(pl.multiple_of(i * 16, 16), 16)
+                total = part[n, at + 1 - core, rows, :].astype(jnp.float32) + came[
+                    n, at // 2, rows, :
+                ].astype(jnp.float32)
+                came[n, at // 2, rows, :] = total.astype(jnp.bfloat16)
+
+            offset = ((r >> 1) & 1, r & 1, y)
+            for p, (_, _, _, _, order) in enumerate(sums[n].parts):
+                bits = [offset[TRIO.index(d)] for d in order]
+                if bits[2]:
+                    sums[n].copy(p, 2, bits[0] | bits[1] << 1).start()
+
+    def compute_steps(n):
+        steps = []
+        for r in (3, 2, 1, 0):
+            steps.append(functools.partial(compute, n, r))
+            if r < 3:
+                steps.append(functools.partial(core_add, n, r + 1))
+        return steps + [functools.partial(core_add, n, 0)]
+
+    for step in chunk_gather_steps(gathers[0], 3):
+        step()
+    for one in loads:
+        one.wait()
+    for step in spaced(chunk_gather_steps(gathers[1], 3), compute_steps(0)):
+        step()
+    outs = [pltpu.make_async_copy(x_all, x_out, out_sem.at[0])]
+    outs[0].start()
+    out_rows = [o_ref.at[pl.ds(CHUNK * n, CHUNK)] for n in range(2)]
+    first = chunk_reduce_steps(sums[0], out_rows[0])
+    for step in spaced(first, compute_steps(1)):
+        step()
+    outs.append(pltpu.make_async_copy(h_all, h_out, out_sem.at[1]))
+    if not back:
+        outs.append(pltpu.make_async_copy(slope, slope_out, out_sem.at[2]))
+    for one in outs[1:]:
+        one.start()
+    for step in chunk_reduce_steps(sums[1], out_rows[1]):
+        step()
+    for n in range(2):
+        gathers[n].finish()
+        sums[n].finish()
+        for r in range(4):
+            for y in range(2):
+                core_copy(n, r, y).wait_send()
+    for one in outs:
+        one.wait()
+
+
+def hidden_layer(back, x, we, wc, last, collective_id, name):
+    bf16, f32 = jnp.bfloat16, jnp.float32
+    dma = pltpu.SemaphoreType.DMA
+    hbm, vmem = pl.BlockSpec(memory_space=pl.ANY), pl.BlockSpec(memory_space=pltpu.VMEM)
+    wide, narrow = (2, 16, CHUNK, D), (2, 16, CHUNK, 512)
+    out = [
+        jax.ShapeDtypeStruct((128, D), f32),
+        jax.ShapeDtypeStruct(wide, bf16),
+        jax.ShapeDtypeStruct(narrow, bf16),
+    ]
+    if not back:
+        out.append(jax.ShapeDtypeStruct(narrow, bf16))
+    return pl.pallas_call(
+        functools.partial(hidden_kernel, back),
+        out_shape=out,
+        in_specs=[hbm, hbm, hbm, hbm if back else vmem],
+        out_specs=[vmem] + [hbm] * (len(out) - 1),
+        scratch_shapes=[
+            pltpu.VMEM(wide, bf16),
+            pltpu.VMEM((D, 512), bf16),
+            pltpu.VMEM((512, D), bf16),
+            pltpu.VMEM(narrow, bf16),
+            pltpu.VMEM(narrow, bf16),
+            pltpu.VMEM(wide, bf16),
+            pltpu.VMEM((2, 8, CHUNK, D), bf16),
+            pltpu.VMEM((2, 8, CHUNK, D), bf16),
+            dma((2, 3, 16)),
+            dma((2, 3, 16)),
+            dma((2, 8)),
+            dma((2, 8)),
+            dma((2, 3, 8)),
+            dma((2, 3, 8)),
+            dma((2,)),
+            dma((3,)),
+            dma((3,)),
+        ],
+        compiler_params=pltpu.CompilerParams(
+            collective_id=collective_id, has_side_effects=True, vmem_limit_bytes=LIMIT
+        ),
+        name=name,
+    )(x, we, wc, last)
+
+
 QB = 256
 KB = WINDOW + QB
 SCALE = HD ** (-0.5)
-NT = (((1,), (1,)), ((), ()))
-TN = (((0,), (0,)), ((), ()))
 
 
 def kept_pairs(lo_ref, a):
@@ -1097,7 +1331,7 @@
     )(lo, q, k, v)
 
 
-def attend_back_kernel(lo_ref, lse_ref, q_ref, k_ref, v_ref, g_ref, dq_ref, dk_ref, dv_ref):
+def attend_back_kernel(lo_ref, lse_ref, q_ref, k_ref, v_ref, g_ref, dq_ref, far_ref, own_ref, dk_ref, dv_ref):
     n = lax.rem(pl.program_id(0), 4)
     a = pl.multiple_of(n * QB, QB)
     keys = pl.ds(a, KB)
@@ -1115,43 +1349,39 @@
     gs = (probs * (gp - dot)).astype(jnp.bfloat16)
     dq = lax.dot_general(gs, k, TN, preferred_element_type=jnp.float32) * SCALE
     dq_ref[0] = dq.astype(dq_ref.dtype)
-    dk_ref[0, keys] += jnp.dot(gs, q, preferred_element_type=jnp.float32) * SCALE
-    dv_ref[0, keys] += jnp.dot(probs.astype(jnp.bfloat16), g, preferred_element_type=jnp.float32)
+    dk_ref[keys] += jnp.dot(gs, q, preferred_element_type=jnp.float32) * SCALE
+    dv_ref[keys] += jnp.dot(probs.astype(jnp.bfloat16), g, preferred_element_type=jnp.float32)
+
+    @pl.when(n == 3)
+    def _():
+        for out, first in ((far_ref, 0), (own_ref, WINDOW)):
+            rows = pl.ds(first, WINDOW)
+            out[0, :, :HD] = dk_ref[rows].astype(out.dtype)
+            out[0, :, HD:] = dv_ref[rows].astype(out.dtype)
 
 
 def attend_back(lo, lse, q, k, v, g):
     per_q = pl.BlockSpec((1, QB, HD), lambda n: (n, 0, 0))
     per_row = pl.BlockSpec((1, 1, QB), lambda n: (n, 0, 0))
     per_micro = pl.BlockSpec((1, 2 * WINDOW, HD), lambda n: (n // 4, 0, 0))
+    per_half = pl.BlockSpec((1, WINDOW, 2 * HD), lambda n: (n // 4, 0, 0))
     return pl.pallas_call(
         attend_back_kernel,
         grid=(8,),
         out_shape=(
             jax.ShapeDtypeStruct((8, QB, HD), jnp.bfloat16),
-            jax.ShapeDtypeStruct((2, 2 * WINDOW, HD), jnp.float32),
-            jax.ShapeDtypeStruct((2, 2 * WINDOW, HD), jnp.float32),
+            jax.ShapeDtypeStruct((2, WINDOW, 2 * HD), jnp.bfloat16),
+            jax.ShapeDtypeStruct((2, WINDOW, 2 * HD), jnp.bfloat16),
         ),
         in_specs=[per_row, per_row, per_q, per_micro, per_micro, per_q],
-        out_specs=[per_q, per_micro, per_micro],
+        out_specs=[per_q, per_half, per_half],
+        scratch_shapes=[pltpu.VMEM((2 * WINDOW, HD), jnp.float32)] * 2,
         compiler_params=pltpu.CompilerParams(vmem_limit_bytes=LIMIT),
         name="attend_back",
     )(lo, lse, q, k, v, g)
 
 
-def dot32(a, b):
-    return jnp.dot(a, b, preferred_element_type=jnp.float32)
-
-
-def dot_nt(a, b):
-    return lax.dot_general(a, b, NT, preferred_element_type=jnp.float32)
-
-
-def dot_tn(a, b):
-    return lax.dot_general(a, b, TN, preferred_element_type=jnp.float32)
-
-
-PLAIN = cube_parts(128, (768, 640, 640))
-WIDE = cube_parts(128, (896, 896, 768))
+BESIDE = ((0, 128, 0, 256, (4, 2, "x", 1)),), ((0, 128, 0, 256, (2, "x", 4, 1)),)
 SMALL = tuple(
     (48 * n, 48, 0, 256, order)
     for n, order in enumerate(((8, "x", 4, 2, 1), (8, 4, 2, "x", 1), (8, 2, "x", 4, 1)))
@@ -1194,9 +1424,11 @@
         ]
     )
     small = jnp.concatenate([small, jnp.zeros((16 * 256 - small.shape[0],), bf16)]).reshape(16, 256)
-    shared = gather(
-        jnp.concatenate([mixer_weight[0][:, D:], small], axis=0), ALL, SMALL, 3, "gather_shared"
-    ).reshape(2, 16, 144, 256)
+    shared, wq, wo = fetch_first(
+        jnp.concatenate([mixer_weight[0][:, D:], small], axis=0), mixer_weight[0], output_weight[0]
+    )
+    shared = shared.reshape(2, 16, 144, 256)
+    wq = from_halves(wq.reshape(2, 8 * 128, HD).transpose(1, 0, 2)).transpose(1, 0, 2)
     wkv = shared[:, :, :128].reshape(2, D, 256)
     vectors = shared[:, :, 128:].reshape(2, 16, 4096)
 
@@ -1205,16 +1437,13 @@
 
     gain_one, shift_one, gain_two, shift_two, bias_out, bias_con = [vector(n) for n in range(6)]
     bias_exp = vectors[:, :, 768:1280].reshape(2, 8192).astype(f32)
-    bias_exp = lax.dynamic_slice_in_dim(bias_exp, f * 512, 512, 1)
+    hidden_units = [512 * (8 * h + lax.rem(shd, 8)) + 256 * sec for h in range(2)]
+    bias_exp = jnp.concatenate(
+        [lax.dynamic_slice_in_dim(bias_exp, first, 256, 1) for first in hidden_units], axis=1
+    )
     bias_mix = vectors[:, :, 1280 : 1280 + 136].reshape(2, BIAS).astype(f32)
     bias_q = lax.dynamic_slice_in_dim(bias_mix, f * HD, HD, 1)
     bias_kv = jnp.concatenate([jnp.zeros((2, HD), f32), bias_mix[:, D:]], axis=1)
-
-    wq, we, wo, wc = fetch_weights(
-        mixer_weight[0][:, :D], expand_weight[0], output_weight[0], contract_weight[0]
-    )
-    wq = wq.reshape(2, D, HD)
-    we = we.reshape(2, D, 512)
 
     starts = jnp.sum(
         (segments[:, None, :] < lax.dynamic_slice_in_dim(segments, half * WINDOW, WINDOW, 1)[:, :, None]),
@@ -1229,7 +1458,14 @@
     for s in range(2):
         n1 = layer_norm(hidden, gain_one[s], shift_one[s]).astype(bf16)
         kv_rows = (dot32(n1, wkv[s]) + bias_kv[s]).astype(bf16)
-        all_n1, far_kv = gather_window(n1, kv_rows, 4)
+        if s == 0:
+            all_n1, far_kv, we, wc = gather_window(
+                n1, kv_rows, 3, (expand_weight[0], contract_weight[0])
+            )
+            we = [from_halves(we[n].reshape(8 * 128, 512)) for n in range(2)]
+            wc = [from_halves(wc[n]) for n in range(2)]
+        else:
+            all_n1, far_kv = gather_window(n1, kv_rows, 4)
         all_n1 = all_n1.reshape(2048, D)
         q = (dot32(all_n1, wq[s]) + bias_q[s]).astype(bf16).reshape(8, QB, HD)
         kv = (dot32(all_n1, wkv[s]) + bias_kv[s]).astype(bf16).reshape(2, WINDOW, 256)
@@ -1238,15 +1474,12 @@
         mixed, lse = attend(lo, q, k, v)
         mixed = mixed.reshape(2048, HD)
         part = dot32(mixed, wo[s]).astype(bf16).reshape(16, 128, D)
-        middle = hidden + reduce(part, CUBE, PLAIN, 5, "reduce_rows") + bias_out[s]
+        middle = hidden + reduce([part], CUBE, [PLAIN], 5, "reduce_rows")[0] + bias_out[s]
         n2 = layer_norm(middle, gain_two[s], shift_two[s]).astype(bf16)
-        all_n2 = gather(n2, CUBE, PLAIN, 6, "gather_rows").reshape(2048, D)
-        pre = dot32(all_n2, we[s]) + bias_exp[s]
-        act = gelu_tanh(pre).astype(bf16)
-        part = dot32(act, wc[s]).astype(bf16).reshape(16, 128, D)
-        result = middle + reduce(part, CUBE, PLAIN, 5, "reduce_rows") + bias_con[s]
+        rows, all_n2, act, slope = hidden_layer(False, n2, we[s], wc[s], bias_exp[s][None], 9, "hidden")
+        result = middle + rows + bias_con[s]
         results.append(result.astype(bf16))
-        kept.append((hidden, n1, all_n1, q, k, v, lse, mixed, middle, all_n2, pre, act))
+        kept.append((hidden, n1, all_n1, q, k, v, lse, mixed, middle, all_n2, act, slope))
         hidden = results[-1].astype(f32)
 
     grad = lax.dynamic_index_in_dim(cotangent, sec, 0, keepdims=False).astype(f32)
@@ -1254,15 +1487,13 @@
     weight_grads = [None, None]
     small_grads = [None, None]
     for s in (1, 0):
-        hidden, n1, all_n1, q, k, v, lse, mixed, middle, all_n2, pre, act = kept[s]
+        hidden, n1, all_n1, q, k, v, lse, mixed, middle, all_n2, act, slope = kept[s]
         go = grad.astype(bf16)
-        all_go = gather(go, CUBE, PLAIN, 6, "gather_rows").reshape(2048, D)
-        _, gelu_back = jax.vjp(gelu_tanh, pre)
-        g_pre = gelu_back(dot_nt(all_go, wc[s]))[0].astype(bf16)
-        part = dot_nt(g_pre, we[s]).astype(bf16).reshape(16, 128, D)
-        g_n2 = reduce(part, CUBE, PLAIN, 5, "reduce_rows")
-        d_wc = dot_tn(act, all_go).astype(bf16)
-        d_we = dot_tn(all_n2, g_pre).astype(bf16)
+        g_n2, all_go, g_pre = hidden_layer(True, go, we[s], wc[s], slope, 10, "hidden_back")
+        all_go, all_n2 = all_go.reshape(2048, D), all_n2.reshape(2048, D)
+        act, g_pre = act.reshape(2048, 512), g_pre.reshape(2048, 512)
+        d_wc = to_halves(dot_tn(act, all_go).astype(bf16))
+        d_we = to_halves(dot_tn(all_n2, g_pre).astype(bf16))
         d_be = jnp.sum(g_pre.astype(f32), axis=0)
         _, back = jax.vjp(layer_norm, middle, gain_two[s], shift_two[s])
         g_mid, d_gain_two, d_shift_two = back(g_n2)
@@ -1271,29 +1502,33 @@
         all_ga = gather(ga, CUBE, PLAIN, 6, "gather_rows").reshape(2048, D)
         g_mixed = dot_nt(all_ga, wo[s]).astype(bf16).reshape(8, QB, HD)
         d_wo = dot_tn(mixed, all_ga).astype(bf16)
-        dq, dk, dv = attend_back(lo, lse, q, k, v, g_mixed)
+        dq, d_far, d_own = attend_back(lo, lse, q, k, v, g_mixed)
         dq = dq.reshape(2048, HD)
-        d_kv = jnp.concatenate([dk, dv], axis=2).astype(bf16)
-        part = jnp.concatenate(
-            [
-                dot_nt(dq, wq[s]).astype(bf16).reshape(16, 128, D),
-                d_kv[:, WINDOW:].reshape(16, 128, 256),
-                d_kv[:, :WINDOW].reshape(16, 128, 256),
-            ],
-            axis=2,
+        d_wq = to_halves(dot_tn(all_n1, dq).astype(bf16))
+        part = dot_nt(dq, wq[s]).astype(bf16).reshape(16, 128, D)
+        rows, kv_own, kv_far = reduce(
+            [part, d_own.reshape(16, 128, 256), d_far.reshape(16, 128, 256)],
+            CUBE,
+            (PLAIN,) + BESIDE,
+            7,
+            "reduce_window",
+            True,
         )
-        rows = reduce(part, CUBE, WIDE, 7, "reduce_window", (D + 256, 256))
-        dkv_rows = (rows[:, D : D + 256] + jnp.where(half == 0, rows[:, D + 256 :], 0.0)).astype(bf16)
-        g_n1 = rows[:, :D] + dot_nt(dkv_rows, wkv[s])
+        dkv_rows = (kv_own + jnp.where(half == 0, kv_far, 0.0)).astype(bf16)
+        g_n1 = rows + dot_nt(dkv_rows, wkv[s])
         _, back = jax.vjp(layer_norm, hidden, gain_one[s], shift_one[s])
         g_in, d_gain_one, d_shift_one = back(g_n1)
         g_in = g_mid + g_in
         input_grads[s] = g_in
-        d_wq = dot_tn(all_n1, dq).astype(bf16)
         d_wkv = dot_tn(n1, dkv_rows)
         d_bq = jnp.sum(dq.astype(f32), axis=0)
         d_bv = jnp.sum(dkv_rows[:, HD:].astype(f32), axis=0)
-        weight_grads[s] = (d_wq.reshape(16, 128, HD), d_we.reshape(16, 128, 512), d_wo, d_wc)
+        weight_grads[s] = (
+            d_wq.reshape(8, 128, HD),
+            d_we.reshape(8, 128, 512),
+            d_wo,
+            d_wc,
+        )
         spread = [
             d_gain_one,
             d_shift_one,
@@ -1302,11 +1537,13 @@
             jnp.sum(ga.astype(f32), axis=0),
             jnp.sum(go.astype(f32), axis=0),
         ]
-        d_be = lax.dynamic_update_slice_in_dim(jnp.zeros((8192,), f32), d_be, f * 512, 0)
+        placed = jnp.zeros((8192,), f32)
+        for h, first in enumerate(hidden_units):
+            placed = lax.dynamic_update_slice_in_dim(placed, d_be[256 * h : 256 * (h + 1)], first, 0)
         d_bm = lax.dynamic_update_slice_in_dim(jnp.zeros((D,), f32), d_bq, f * HD, 0)
         vec = jnp.concatenate(
             [one.reshape(16, 128) for one in spread]
-            + [d_be.reshape(16, 512), jnp.concatenate([d_bm, d_bv]).reshape(16, 136)],
+            + [placed.reshape(16, 512), jnp.concatenate([d_bm, d_bv]).reshape(16, 136)],
             axis=1,
         )
         vec = jnp.pad(vec, ((0, 0), (0, 4096 - vec.shape[1]))).reshape(16, 16, 256)
@@ -1314,8 +1551,8 @@
         grad = g_in.astype(bf16).astype(f32)
 
     mine = reduce(
-        jnp.concatenate(small_grads, axis=0).astype(bf16), ALL, SMALL, 8, "reduce_shared"
-    )
+        [jnp.concatenate(small_grads, axis=0).astype(bf16)], ALL, [SMALL], 8, "reduce_shared"
+    )[0]
     vec = mine[128:].reshape(4096)
     rq, re, ro, rc = return_grads(
         *[jnp.stack([weight_grads[0][n], weight_grads[1][n]]) for n in range(4)]
@@ -1337,15 +1574,15 @@
         swap(input_grads),
         vec[0:128][None],
         vec[128:256][None],
-        jnp.concatenate([both(rq), mine[:128]], axis=1)[None],
+        jnp.concatenate([rq.astype(f32), mine[:128]], axis=1)[None],
         vec[1280 : 1280 + 136][None],
         both(ro)[None],
         vec[512:640][None],
         vec[256:384][None],
         vec[384:512][None],
-        both(re)[None],
+        re.astype(f32)[None],
         vec[768:1280][None],
-        both(rc)[None],
+        rc.astype(f32)[None],
         vec[640:768][None],
     )
 

time: 1480 us -> 1260 us (0.85)
  Pallas kernels: 1160 us -> 930 us
  waiting for transfers between devices: 0.01 us -> 81.4 us
  matrix products: 185 us -> 133 us
  other arithmetic: 84.7 us -> 68 us
    pallas_call x7 -> x2, Pallas kernels: 229 us -> 65.5 us  [gather(): pl.pallas_call(functools.partial(gather_kernel, dims, parts), out_shape=j...]
    pallas_call x13, Pallas kernels: 879 us -> 808 us  [the longest x4 311 us: hidden_layer(): pl.pallas_call(functools.partial(hidden_kernel, back), out_shape=out, in_...]
    reduce_scatter x0 -> x6, waiting for transfers between devices: none -> 64 us  [to_halves(): lax.psum_scatter(x, 'shard', scatter_dimension=0, tiled=True, axis_index_...]
    dot_general x12 -> x8, matrix products: 69.1 us -> 37.5 us  [dot32(): return jnp.dot(a, b, preferred_element_type=jnp.float32)]
    dot_general x10 -> x6, matrix products: 61.9 us -> 30.8 us  [dot_nt(): return lax.dot_general(a, b, NT, preferred_element_type=jnp.float32)]
    concatenate x4 -> x1, other arithmetic: 15.6 us -> 0.59 us  [on_device_fast(): jnp.concatenate([lax.dynamic_slice_in_dim(bias_exp, first, 256, 1) for fi...]
  transfers between devices with their start and end apart: 2 -> 13, of which waited for: 0 -> 4; matrix products, arithmetic and copies ran while one was open for 9% -> 14% of each run, Pallas kernels for 28% -> 51%
where the time goes in v2:
time: 1260 us; the launch traced here: 1250 us
  Pallas kernels  930 us (74%)
  matrix products  133 us (11%)
  waiting for transfers between devices  81.4 us (6%)
  other arithmetic  68 us (5%)
  local copies, waits for them, and re-layouts  24.3 us (2%)
  between operations  15 us (1%)
    pallas_call x4, Pallas kernels, hidden_layer(): pl.pallas_call(functools.partial(hidden_kernel, back), out_shape=out, in_...  311 us
    pallas_call x5, Pallas kernels, reduce(): pl.pallas_call(functools.partial(reduce_kernel, dims, all_parts, swapped)...  261 us
    pallas_call x2, Pallas kernels, gather_window(): pl.pallas_call(functools.partial(gather_window_kernel, parts, bool(weight...  128 us
    pallas_call x1, Pallas kernels, return_grads(): pl.pallas_call(return_kernel, out_shape=(jax.ShapeDtypeStruct((128, D), b...  66.1 us
    pallas_call x2, Pallas kernels, gather(): pl.pallas_call(functools.partial(gather_kernel, dims, parts), out_shape=j...  65.5 us
    dot_general x10, matrix products, dot_tn(): return lax.dot_general(a, b, TN, preferred_element_type=jnp.float32)  64.7 us
    reduce_scatter x6, waiting for transfers between devices, to_halves(): lax.psum_scatter(x, 'shard', scatter_dimension=0, tiled=True, axis_index_...  64 us
    pallas_call x1, Pallas kernels, fetch_first(): pl.pallas_call(first_kernel, out_shape=(jax.ShapeDtypeStruct((32,) + bloc...  41.1 us
  transfers between devices with their start and end apart: 13, of which 4 were waited for; matrix products, arithmetic and copies ran while one was open for 14% of the time, Pallas kernels for 51%

profile of v2, /device:TPU:0, one launch (start us, length us, event | category | flops | bytes accessed | tf_op | source)
XLA Modules:
  0.0 1254.0 jit_solution(8937319375905016344)
XLA Ops:
  14.2 41.1 %fetch_first.1 = (bf16[32,144,256]{2,1,0:T(8,128)(2,1)}, bf16[2,8,128,128]{3,2,1,0:T(8,128)(2,1)}, bf16[2,128,2048]{2,1,0:T(8,128)(2,1)}) custom-call(bf16[144,256]{1,0:T(8,128)(2,1)} %pad_maximum_fusion.6.block, bf16[128,2304]{1,0:T(8,128)(2,1)} %bitcast.337, bf16[128,2048]{1,0:T(8,128)(2,1)} %bitcast.338), custom_call_target="tpu_custom_call" | custom-call | tf_op jit(solution)/shard_map/fetch_first/pallas_call | solution.py:918
  63.6 79.6 %gather_window.2 = (bf16[16,128,2048]{2,1,0:T(8,128)(2,1)}, bf16[16,128,256]{2,1,0:T(8,128)(2,1)}, bf16[2,8,128,512]{3,2,1,0:T(8,128)(2,1)}, bf16[2,256,2048]{2,1,0:T(8,128)(2,1)}) custom-call(bf16[128,2048]{1,0:T(8,128)(2,1)} %fusion.26.refs_0_, bf16[128,256]{1,0:T(8,128)(2,1)} %fusion.20.refs_1_, bf16[128,8192]{1,0:T(8,128)(2,1)} %bitcast.313, ...), custom_call_target="tpu_custom_call" | custom-call | tf_op jit(solution)/shard_map/gather_window/pallas_call | solution.py:670
  159.1 6.7 fusion
  176.6 12.6 %attend.2 = (bf16[8,256,128]{2,1,0:T(8,128)(2,1)}, f32[8,1,256]{2,1,0:T(1,128)}) custom-call(s32[8,1,256]{2,1,0:T(1,128)} %max.19.lo_ref, bf16[8,256,128]{2,1,0:T(8,128)(2,1)} %bitcast.316, bf16[2,2048,128]{2,1,0:T(8,128)(2,1)} %get-tuple-element.146.k_ref, bf16[2,2048,128]{2,1,0:T(8,128)(2,1)} %get-tuple-element.145.v_ref), custom_call_target="tpu_custom_call" | custom-call | tf_op jit(solution)/shard_map/attend/pallas_call | solution.py:1320
  189.2 6.6 convolution_convert_fusion.3
  195.8 53.9 %reduce_rows.2 = f32[128,2048]{1,0:T(8,128)} custom-call(bf16[16,128,2048]{2,1,0:T(8,128)(2,1)} %bitcast.288), custom_call_target="tpu_custom_call" | custom-call | tf_op jit(solution)/shard_map/reduce_rows/pallas_call | solution.py:775
  258.5 96.0 %hidden.2 = (f32[128,2048]{1,0:T(8,128)}, bf16[2,16,64,2048]{3,2,1,0:T(8,128)(2,1)}, bf16[2,16,64,512]{3,2,1,0:T(8,128)(2,1)}, bf16[2,16,64,512]{3,2,1,0:T(8,128)(2,1)}) custom-call(bf16[128,2048]{1,0:T(8,128)(2,1)} %add_convert_fusion.3.refs_0_, bf16[2048,512]{1,0:T(8,128)(2,1)} %all-gather.10.cloned.1.call-done.refs_1_, bf16[512,2048]{1,0:T(8,128)(2,1)} %bitcast.293, ...), custom_call_target="tpu_custom_call" | custom-call | tf_op jit(solution)/shard_map/hidden/pallas_call | solution.py:1259
  357.6 48.7 %gather_window.3 = (bf16[16,128,2048]{2,1,0:T(8,128)(2,1)}, bf16[16,128,256]{2,1,0:T(8,128)(2,1)}) custom-call(bf16[128,2048]{1,0:T(8,128)(2,1)} %copy-done.8, bf16[128,256]{1,0:T(8,128)(2,1)} %fusion.21.refs_1_), custom_call_target="tpu_custom_call" | custom-call | tf_op jit(solution)/shard_map/gather_window/pallas_call | solution.py:670
  417.4 12.4 attend.3
  436.4 38.1 %reduce_rows.3 = f32[128,2048]{1,0:T(8,128)} custom-call(bf16[16,128,2048]{2,1,0:T(8,128)(2,1)} %bitcast.289), custom_call_target="tpu_custom_call" | custom-call | tf_op jit(solution)/shard_map/reduce_rows/pallas_call | solution.py:775
  477.4 68.0 %hidden.3 = (f32[128,2048]{1,0:T(8,128)}, bf16[2,16,64,2048]{3,2,1,0:T(8,128)(2,1)}, bf16[2,16,64,512]{3,2,1,0:T(8,128)(2,1)}, bf16[2,16,64,512]{3,2,1,0:T(8,128)(2,1)}) custom-call(bf16[128,2048]{1,0:T(8,128)(2,1)} %add_convert_fusion.1.refs_0_, bf16[2048,512]{1,0:T(8,128)(2,1)} %all-gather.12.cloned.1.call-done.refs_1_, bf16[512,2048]{1,0:T(8,128)(2,1)} %bitcast.295, ...), custom_call_target="tpu_custom_call" | custom-call | tf_op jit(solution)/shard_map/hidden/pallas_call | solution.py:1259
  545.4 67.4 %hidden_back.2 = (f32[128,2048]{1,0:T(8,128)}, bf16[2,16,64,2048]{3,2,1,0:T(8,128)(2,1)}, bf16[2,16,64,512]{3,2,1,0:T(8,128)(2,1)}) custom-call(bf16[128,2048]{1,0:T(8,128)(2,1)} %get-tuple-element.150.refs_0_, bf16[2048,512]{1,0:T(8,128)(2,1)} %all-gather.12.cloned.1.call-done.refs_1_, bf16[512,2048]{1,0:T(8,128)(2,1)} %bitcast.296, ...), custom_call_target="tpu_custom_call" | custom-call | tf_op jit(solution)/shard_map/hidden_back/pallas_call | solution.py:1259
  617.0 32.6 %gather_rows.2 = bf16[16,128,2048]{2,1,0:T(8,128)(2,1)} custom-call(bf16[128,2048]{1,0:T(8,128)(2,1)} %get-tuple-element.120.x_ref), custom_call_target="tpu_custom_call" | custom-call | tf_op jit(solution)/shard_map/gather_rows/pallas_call | solution.py:569
  649.6 6.6 convolution_convert_fusion.10
  656.2 15.9 %attend_back.2 = (bf16[8,256,128]{2,1,0:T(8,128)(2,1)}, bf16[2,1024,256]{2,1,0:T(8,128)(2,1)}, bf16[2,1024,256]{2,1,0:T(8,128)(2,1)}) custom-call(s32[8,1,256]{2,1,0:T(1,128)} %max.19.lo_ref, f32[8,1,256]{2,1,0:T(1,128)} %get-tuple-element.72.lse_ref, bf16[8,256,128]{2,1,0:T(8,128)(2,1)} %bitcast.319, bf16[2,2048,128]{2,1,0:T(8,128)(2,1)} %get-tuple-element.144.k_ref, ...), custom_call_target="tpu_custom_call" | custom-call | tf_op jit(solution)/shard_map/attend_back/pallas_call | solution.py:1368
  673.4 6.6 convolution_convert_fusion.7
  680.0 6.9 convolution_convert_fusion.1
  687.6 52.2 %reduce_window.2 = (f32[128,2048]{1,0:T(8,128)}, f32[128,256]{1,0:T(8,128)}, f32[128,256]{1,0:T(8,128)}) custom-call(bf16[16,128,2048]{2,1,0:T(8,128)(2,1)} %bitcast.286, bf16[16,128,256]{2,1,0:T(8,128)(2,1)} %bitcast.323, bf16[16,128,256]{2,1,0:T(8,128)(2,1)} %bitcast.322), custom_call_target="tpu_custom_call" | custom-call | tf_op jit(solution)/shard_map/reduce_window/pallas_call | solution.py:775
  751.1 79.4 %hidden_back.3 = (f32[128,2048]{1,0:T(8,128)}, bf16[2,16,64,2048]{3,2,1,0:T(8,128)(2,1)}, bf16[2,16,64,512]{3,2,1,0:T(8,128)(2,1)}) custom-call(bf16[128,2048]{1,0:T(8,128)(2,1)} %get-tuple-element.115.refs_0_, bf16[2048,512]{1,0:T(8,128)(2,1)} %all-gather.10.cloned.1.call-done.refs_1_, bf16[512,2048]{1,0:T(8,128)(2,1)} %bitcast.294, ...), custom_call_target="tpu_custom_call" | custom-call | tf_op jit(solution)/shard_map/hidden_back/pallas_call | solution.py:1259
  833.8 32.9 %gather_rows.3 = bf16[16,128,2048]{2,1,0:T(8,128)(2,1)} custom-call(bf16[128,2048]{1,0:T(8,128)(2,1)} %get-tuple-element.118.x_ref), custom_call_target="tpu_custom_call" | custom-call | tf_op jit(solution)/shard_map/gather_rows/pallas_call | solution.py:569
  873.2 15.9 %attend_back.3 = (bf16[8,256,128]{2,1,0:T(8,128)(2,1)}, bf16[2,1024,256]{2,1,0:T(8,128)(2,1)}, bf16[2,1024,256]{2,1,0:T(8,128)(2,1)}) custom-call(s32[8,1,256]{2,1,0:T(1,128)} %max.19.lo_ref, f32[8,1,256]{2,1,0:T(1,128)} %get-tuple-element.81.lse_ref, bf16[8,256,128]{2,1,0:T(8,128)(2,1)} %bitcast.317, bf16[2,2048,128]{2,1,0:T(8,128)(2,1)} %get-tuple-element.146.k_ref, ...), custom_call_target="tpu_custom_call" | custom-call | tf_op jit(solution)/shard_map/attend_back/pallas_call | solution.py:1368
  889.1 6.6 convolution_convert_fusion.8
  895.9 9.9 bitcast_convert_fusion
  914.4 72.4 %reduce_window.3 = (f32[128,2048]{1,0:T(8,128)}, f32[128,256]{1,0:T(8,128)}, f32[128,256]{1,0:T(8,128)}) custom-call(bf16[16,128,2048]{2,1,0:T(8,128)(2,1)} %bitcast.287, bf16[16,128,256]{2,1,0:T(8,128)(2,1)} %bitcast.321, bf16[16,128,256]{2,1,0:T(8,128)(2,1)} %bitcast.320), custom_call_target="tpu_custom_call" | custom-call | tf_op jit(solution)/shard_map/reduce_window/pallas_call | solution.py:775
  987.9 9.9 bitcast_convert_fusion.1
  1004.2 9.4 bitcast_convert_fusion.2
  1016.7 44.7 %reduce_shared.1 = f32[144,256]{1,0:T(8,128)} custom-call(bf16[32,144,256]{2,1,0:T(8,128)(2,1)} %maximum_maximum_fusion.refs_0_), custom_call_target="tpu_custom_call" | custom-call | tf_op jit(solution)/shard_map/reduce_shared/pallas_call | solution.py:775
  1067.4 9.4 bitcast_convert_fusion.3
  1087.6 10.1 collective-permute-done.1
  1104.5 6.8 reduce-scatter.13.cloned.1.call-done
  1111.2 57.2 %reduce-scatter.11.cloned.1.call-done = bf16[1024,512]{1,0:T(8,128)(2,1)} async-done(((bf16[2048,512]{1,0:T(8,128)(2,1)}), bf16[1024,512]{1,0:T(8,128)(2,1)}) %reduce-scatter.11.cloned.1.call-update) | async-done | bytes 1048592 | tf_op jit(solution)/shard_map/reduce_scatter | solution.py:1051
  1171.5 66.1 %return_grads.1 = (bf16[128,2048]{1,0:T(8,128)(2,1)}, bf16[128,8192]{1,0:T(8,128)(2,1)}, bf16[2,128,2048]{2,1,0:T(8,128)(2,1)}, bf16[512,2048]{1,0:T(8,128)(2,1)}) custom-call(bf16[2,8,128,128]{3,2,1,0:T(8,128)(2,1)} %pad_maximum_fusion.5.gq, bf16[2,8,128,512]{3,2,1,0:T(8,128)(2,1)} %pad_maximum_fusion.ge, bf16[2,128,2048]{2,1,0:T(8,128)(2,1)} %pad_maximum_fusion.4.go, ...), custom_call_target="tpu_custom_call" | custom-call | tf_op jit(solution)/shard_map/return_grads/pallas_call | solution.py:1025
  (267 shorter events, 156.3 us)
Async XLA Ops:
  7.2 162.8 %all-gather.8.cloned.1.call-start = ((), (), s32[]{:S(2)}) async-start(), calls=%async_computation.6 | async-start | bytes 1572864 | tf_op jit(solution)/shard_map/all_gather | solution.py:1047
  55.3 197.1 %all-gather.10.cloned.1.call-start = ((), (), s32[]{:S(2)}) async-start(), calls=%async_computation.7 | async-start | bytes 3145728 | tf_op jit(solution)/shard_map/all_gather | solution.py:1047
  56.4 4.3 copy-start
  58.2 100.9 %copy-start.18 = (bf16[1,16,128,256]{3,2,1,0:T(8,128)(2,1)}, bf16[1,16,128,256]{3,2,1,0:T(8,128)(2,1)S(1)}, u32[]{:S(2)}) copy-start(bf16[1,16,128,256]{3,2,1,0:T(8,128)(2,1)S(1)} %get-tuple-element.138) | copy-start | bytes 3145732
  58.2 348.2 %copy-start.5 = (bf16[1,16,128,256]{3,2,1,0:T(8,128)(2,1)}, bf16[1,16,128,256]{3,2,1,0:T(8,128)(2,1)S(1)}, u32[]{:S(2)}) copy-start(bf16[1,16,128,256]{3,2,1,0:T(8,128)(2,1)S(1)} %get-tuple-element.137) | copy-start | bytes 3145732
  146.2 112.3 %all-gather.14.cloned.1.call-start = ((), (), s32[]{:S(2)}) async-start(), calls=%async_computation.15 | async-start | bytes 3145728 | tf_op jit(solution)/shard_map/all_gather | solution.py:1047
  149.5 3.5 copy-start.35
  149.5 327.9 %all-gather.12.cloned.1.call-start = ((), (), s32[]{:S(2)}) async-start(), calls=%async_computation.8 | async-start | bytes 3145728 | tf_op jit(solution)/shard_map/all_gather | solution.py:1047
  150.1 327.3 %all-gather.16.cloned.1.call-start = ((), (), s32[]{:S(2)}) async-start(), calls=%async_computation.16 | async-start | bytes 3145728 | tf_op jit(solution)/shard_map/all_gather | solution.py:1047
  150.6 948.8 %reduce-scatter.9.cloned.1.call-start = ((), (), s32[]{:S(2)}) async-start(), calls=%async_computation.10 | async-start | bytes 786432 | tf_op jit(solution)/shard_map/reduce_scatter | solution.py:1051
  176.5 12.6 %copy-start.31 = (bf16[2,128,2048]{2,1,0:T(8,128)(2,1)S(1)}, bf16[2,128,2048]{2,1,0:T(8,128)(2,1)}, u32[]{:S(2)}) copy-start(bf16[2,128,2048]{2,1,0:T(8,128)(2,1)} %get-tuple-element.62) | copy-start | bytes 3145732
  406.4 5.9 copy-start.29
  406.4 6.1 copy-start.36
  412.5 3.2 copy-start.28
  417.4 12.4 copy-start.32
  680.0 6.9 copy-start.23
  687.5 412.0 %reduce-scatter.7.cloned.1.call-start = ((), (), s32[]{:S(2)}) async-start(), calls=%async_computation.9 | async-start | bytes 786432 | tf_op jit(solution)/shard_map/reduce_scatter | solution.py:1051
  749.6 335.7 %collective-permute-start = (bf16[128,2048]{1,0:T(8,128)(2,1)}, bf16[128,2048]{1,0:T(8,128)(2,1)}, u32[]{:S(2)}, u32[]{:S(2)}) collective-permute-start(bf16[128,2048]{1,0:T(8,128)(2,1)} %get-tuple-element.151), channel_id=1, source_target_pairs={{0,16},{16,0},{1,17},{17,1},{2,18},{18,2},{3,19},{19,3},{4,20},{20... | collective-permute-start | bytes 1572872 | tf_op jit(solution)/shard_map/ppermute | solution.py:1567
  833.8 32.9 %copy-start.33 = (bf16[2,128,2048]{2,1,0:T(8,128)(2,1)S(1)}, bf16[2,128,2048]{2,1,0:T(8,128)(2,1)}, u32[]{:S(2)}) copy-start(bf16[2,128,2048]{2,1,0:T(8,128)(2,1)} %get-tuple-element.62) | copy-start | bytes 3145732
  895.7 205.7 %reduce-scatter.17.cloned.1.call-start = ((), (), s32[]{:S(2)}) async-start(), calls=%async_computation.14 | async-start | bytes 3145728 | tf_op jit(solution)/shard_map/reduce_scatter | solution.py:1051
  908.0 193.4 %reduce-scatter.15.cloned.1.call-start = ((), (), s32[]{:S(2)}) async-start(), calls=%async_computation.13 | async-start | bytes 3145728 | tf_op jit(solution)/shard_map/reduce_scatter | solution.py:1051
  997.9 113.4 %reduce-scatter.13.cloned.1.call-start = ((), (), s32[]{:S(2)}) async-start(), calls=%async_computation.12 | async-start | bytes 3145728 | tf_op jit(solution)/shard_map/reduce_scatter | solution.py:1051
  999.1 3.7 copy-start.9
  1013.6 154.8 %reduce-scatter.11.cloned.1.call-start = ((), (), s32[]{:S(2)}) async-start(), calls=%async_computation.11 | async-start | bytes 3145728 | tf_op jit(solution)/shard_map/reduce_scatter | solution.py:1051
  1016.7 44.7 %copy-start.13 = (bf16[8,256,128]{2,1,0:T(8,128)(2,1)S(1)}, bf16[8,256,128]{2,1,0:T(8,128)(2,1)}, u32[]{:S(2)}) copy-start(bf16[8,256,128]{2,1,0:T(8,128)(2,1)} %get-tuple-element.68) | copy-start | bytes 1572868
  1061.4 6.0 copy-start.25
  1067.4 9.5 copy-start.34
  1076.9 5.0 copy-start.7
  1076.9 5.0 copy-start.11
  1083.7 14.0 %collective-permute-start.1 = (bf16[128,2048]{1,0:T(8,128)(2,1)S(1)}, bf16[128,2048]{1,0:T(8,128)(2,1)S(1)}, u32[]{:S(2)}, u32[]{:S(2)}) collective-permute-start(bf16[128,2048]{1,0:T(8,128)(2,1)S(1)} %get-tuple-element.121), channel_id=1, source_target_pairs={{0,16},{16,0},{1,17},{17,1},{2,18},{18,2},{3,19},{19,3},{4,20},{20... | collective-permute-start | bytes 1572872 | tf_op jit(solution)/shard_map/ppermute | solution.py:1567
  1085.3 12.4 copy-start.14
  1237.6 3.6 copy-start.21
  (19 other events, 38.0 us)
Sparse Core Ops, SparseCore 0:
  55.5 34.1 all-gather.7
  146.4 54.9 all-gather.9
  202.9 55.5 all-gather.13
  260.5 55.5 all-gather.11
  318.1 58.4 all-gather.15
  687.6 19.1 reduce-scatter.8
  895.8 19.1 reduce-scatter.6
  917.3 53.2 reduce-scatter.16
  998.0 54.1 reduce-scatter.14
  1054.8 56.3 reduce-scatter.12
  1114.2 54.2 reduce-scatter.10

commit v3 on v2

--- a/solution.py
+++ b/solution.py
@@ -583,103 +583,6 @@
     )(x)
 
 
-def gather_window_kernel(parts, weights, *refs):
-    if weights:
-        x_ref, kv_ref, exp, con, o_ref, okv_ref, we, wc, far = refs[:9]
-        sems = refs[9:]
-        spread_sems = sems[7:]
-    else:
-        x_ref, kv_ref, o_ref, okv_ref, far = refs[:5]
-        sems = refs[5:]
-    send_sem, recv_sem, kv_send, kv_recv, own_sem, swap_send, swap_recv = sems[:7]
-    h = Hyper(CUBE)
-    sec, shd = lax.axis_index("section"), lax.axis_index("shard")
-    low = lax.rem(shd, 8)
-    other = (sec, shd + 8 * (1 - 2 * lax.rem(shd // 8, 2)))
-    if weights:
-        w_send, w_recv, con_send, con_recv, w_own = spread_sems
-
-        def pieces(ts, tj):
-            for n in range(2):
-                yield (
-                    exp.at[:, columns(2 * (8 * n + lax.rem(tj, 8)) + ts, 256)],
-                    we.at[sec, low, :, pl.ds(256 * n, 256)],
-                )
-
-        spread = Spread(pieces, w_own, w_send, w_recv)
-        spread.barrier()
-    else:
-        h.barrier((other,))
-    swap = remote(kv_ref, far, swap_send, swap_recv, other)
-    swap.start()
-    own = pltpu.make_async_copy(x_ref, o_ref.at[h.pos], own_sem.at[0])
-    own.start()
-    g = Gather(h, parts, x_ref, o_ref, send_sem, recv_sem)
-    g.start(range(3))
-    if weights:
-        spread.start()
-        own_rows = pltpu.make_async_copy(con.at[pl.ds(256 * sec, 256)], wc.at[sec], w_own.at[2])
-        own_rows.start()
-        rows = remote(
-            con.at[pl.ds(256 * (1 - sec), 256)], wc.at[sec], con_send, con_recv, (1 - sec, shd)
-        )
-        rows.start()
-    swap.wait_recv()
-    own_kv = pltpu.make_async_copy(far, okv_ref.at[h.pos], own_sem.at[1])
-    own_kv.start()
-    kv_parts = tuple((0, kv_ref.shape[0], 0, kv_ref.shape[1], order) for order in (CUBE,))
-    gkv = Gather(h, kv_parts, far, okv_ref, kv_send, kv_recv)
-    gkv.start(range(1))
-    k = len(CUBE)
-    for j in range(k):
-        for n in range(1 << j):
-            for one, chosen in ((g, range(3)), (gkv, range(1))):
-                for p in chosen:
-                    one.copy(p, n, j).wait_recv()
-                    for later in range(j + 1, k):
-                        one.copy(p, n | 1 << j, later).start()
-    if weights:
-        spread.wait()
-        remote(
-            con.at[pl.ds(0, 256)], wc.at[1 - sec], con_send, con_recv, (1 - sec, shd)
-        ).wait_recv()
-        rows.wait_send()
-        own_rows.wait()
-    g.finish()
-    gkv.finish()
-    swap.wait_send()
-    own.wait()
-    own_kv.wait()
-
-
-def gather_window(x, kv, collective_id, weights=()):
-    parts = cube_parts(x.shape[0], (768, 640, 640))
-    n = 16
-    dma = pltpu.SemaphoreType.DMA
-    out = [
-        jax.ShapeDtypeStruct((n,) + x.shape, x.dtype),
-        jax.ShapeDtypeStruct((n,) + kv.shape, kv.dtype),
-    ]
-    sems = [dma((3, n)), dma((3, n)), dma((1, n)), dma((1, n)), dma((2,)), dma, dma]
-    if weights:
-        out += [
-            jax.ShapeDtypeStruct((2, 8, 128, 512), kv.dtype),
-            jax.ShapeDtypeStruct((2, 256, D), kv.dtype),
-        ]
-        sems += [dma((2, 16)), dma((2, 16)), dma, dma, dma((3,))]
-    return pl.pallas_call(
-        functools.partial(gather_window_kernel, parts, bool(weights)),
-        out_shape=out,
-        in_specs=[pl.BlockSpec(memory_space=pl.ANY)] * (2 + len(weights)),
-        out_specs=[pl.BlockSpec(memory_space=pl.ANY)] * len(out),
-        scratch_shapes=[pltpu.VMEM(kv.shape, kv.dtype)] + sems,
-        compiler_params=pltpu.CompilerParams(
-            collective_id=collective_id, has_side_effects=True, vmem_limit_bytes=LIMIT
-        ),
-        name="gather_window",
-    )(x, kv, *weights)
-
-
 class Reduce:
     def __init__(self, h, parts, src, buf, send_sem, recv_sem):
         self.h, self.parts, self.src, self.buf = h, parts, src, buf
@@ -855,26 +758,43 @@
             one.wait()
 
 
-def first_kernel(block, mix, out, shared, wq, wo, *sems):
-    send, recv, out_send, out_recv, own_sem, sh_send, sh_recv = sems
+def everyone_barrier(me):
+    sem = pltpu.get_barrier_semaphore()
+
+    @pl.loop(1, 32)
+    def _(d):
+        there = lax.rem(me + d, 32)
+        pl.semaphore_signal(
+            sem, inc=1, device_id=(there // 16, lax.rem(there, 16)), device_id_type=MESH
+        )
+
+    pl.semaphore_wait(sem, 31)
+
+
+def fetch_kernel(block, mix, out, exp, con, shared, wq, wo, we, wc, *sems):
+    q_send, q_recv, send, recv, con_send, con_recv, out_send, out_recv, own_sem, sh_send, sh_recv = sems
     sec, shd = lax.axis_index("section"), lax.axis_index("shard")
     low, half = lax.rem(shd, 8), shd // 8
-
-    def pieces(ts, tj):
-        yield mix.at[:, columns(block_of(ts, tj), HD)], wq.at[sec, low]
-
-    spread = Spread(pieces, own_sem, send, recv)
-    spread.barrier()
+    me = 16 * sec + shd
+    everyone_barrier(me)
     h = Hyper(ALL)
-    own_block = pltpu.make_async_copy(block, shared.at[h.pos], own_sem.at[1])
-    own_block.start()
     g = Gather(h, SMALL, block, shared, sh_send, sh_recv)
     g.start(range(3))
-    spread.start()
+
+    def query(d):
+        there = lax.rem(me + d, 32)
+        ts, tj = there // 16, lax.rem(there, 16)
+        return remote(
+            mix.at[:, columns(block_of(ts, tj), HD)], wq.at[sec, shd], q_send.at[d], q_recv.at[d], (ts, tj)
+        )
+
+    @pl.loop(1, 32)
+    def _(d):
+        query(d).start()
 
     to_x = lax.rem(half + lax.rem(shd, 2), 2)
     from_half = lax.rem(sec + lax.rem(shd, 2), 2)
-    own_out = pltpu.make_async_copy(out, wo.at[sec], own_sem.at[2])
+    own_out = pltpu.make_async_copy(out, wo.at[sec], own_sem.at[5])
     for z in range(2):
         mine = jnp.logical_and(to_x == sec, half == z)
         there = remote(out, wo.at[sec], out_send.at[z], out_recv.at[sec], (to_x, 8 * z + low))
@@ -887,8 +807,31 @@
         def _():
             there.start()
 
+    own = [
+        pltpu.make_async_copy(block, shared.at[h.pos], own_sem.at[2]),
+        pltpu.make_async_copy(mix.at[:, columns(block_of(sec, shd), HD)], wq.at[sec, shd], own_sem.at[3]),
+        pltpu.make_async_copy(con.at[pl.ds(256 * sec, 256)], wc.at[sec], own_sem.at[4]),
+    ]
+    for one in own:
+        one.start()
+
+    def pieces(ts, tj):
+        for n in range(2):
+            yield (
+                exp.at[:, columns(2 * (8 * n + lax.rem(tj, 8)) + ts, 256)],
+                we.at[sec, low, :, pl.ds(256 * n, 256)],
+            )
+
+    spread = Spread(pieces, own_sem, send, recv)
+    spread.start()
+    rows = remote(con.at[pl.ds(256 * (1 - sec), 256)], wc.at[sec], con_send, con_recv, (1 - sec, shd))
+    rows.start()
     g.forward(range(3))
-    spread.wait()
+
+    @pl.loop(1, 32)
+    def _(d):
+        query(d).wait_recv()
+
     for s in range(2):
         mine = jnp.logical_and(sec == s, from_half == half)
 
@@ -896,6 +839,14 @@
         def _():
             remote(out, wo.at[s], out_send.at[0], out_recv.at[s], (1 - sec, shd)).wait_recv()
 
+    spread.wait()
+    remote(con.at[pl.ds(0, 256)], wc.at[1 - sec], con_send, con_recv, (1 - sec, shd)).wait_recv()
+    rows.wait_send()
+
+    @pl.loop(1, 32)
+    def _(d):
+        query(d).wait_send()
+
     for z in range(2):
         mine = jnp.logical_and(to_x == sec, half == z)
         there = remote(out, wo.at[sec], out_send.at[z], out_recv.at[sec], (to_x, 8 * z + low))
@@ -909,27 +860,42 @@
             there.wait_send()
 
     g.finish()
-    own_block.wait()
-
-
-def fetch_first(block, mix, out):
+    for one in own:
+        one.wait()
+
+
+def fetch_weights(block, mix, out, exp, con):
     bf16 = jnp.bfloat16
     dma = pltpu.SemaphoreType.DMA
     return pl.pallas_call(
-        first_kernel,
+        fetch_kernel,
         out_shape=(
             jax.ShapeDtypeStruct((32,) + block.shape, bf16),
-            jax.ShapeDtypeStruct((2, 8, 128, HD), bf16),
+            jax.ShapeDtypeStruct((2, 16, 128, HD), bf16),
             jax.ShapeDtypeStruct((2, 128, D), bf16),
+            jax.ShapeDtypeStruct((2, 8, 128, 512), bf16),
+            jax.ShapeDtypeStruct((2, 256, D), bf16),
         ),
-        in_specs=[pl.BlockSpec(memory_space=pl.ANY)] * 3,
-        out_specs=[pl.BlockSpec(memory_space=pl.ANY)] * 3,
-        scratch_shapes=[dma((1, 16)), dma((1, 16)), dma((2,)), dma((2,)), dma((3,)), dma((3, 32)), dma((3, 32))],
+        in_specs=[pl.BlockSpec(memory_space=pl.ANY)] * 5,
+        out_specs=[pl.BlockSpec(memory_space=pl.ANY)] * 5,
+        scratch_shapes=[
+            dma((32,)),
+            dma((32,)),
+            dma((2, 16)),
+            dma((2, 16)),
+            dma,
+            dma,
+            dma((2,)),
+            dma((2,)),
+            dma((6,)),
+            dma((3, 32)),
+            dma((3, 32)),
+        ],
         compiler_params=pltpu.CompilerParams(
             collective_id=1, has_side_effects=True, vmem_limit_bytes=LIMIT
         ),
-        name="fetch_first",
-    )(block, mix, out)
+        name="fetch_weights",
+    )(block, mix, out, exp, con)
 
 
 def return_kernel(gq, ge, go, gc, rq, re, ro, rc, *sems):
@@ -1047,6 +1013,11 @@
     return lax.all_gather(x, "shard", axis=0, tiled=True, axis_index_groups=HALVES)
 
 
+def with_other(x, came):
+    mine = lax.dynamic_index_in_dim(x, lax.axis_index("shard") // 8, 0, keepdims=False)
+    return (mine.astype(jnp.float32) + came.astype(jnp.float32)).astype(x.dtype)
+
+
 def to_halves(x):
     return lax.psum_scatter(x, "shard", scatter_dimension=0, tiled=True, axis_index_groups=HALVES)
 
@@ -1067,7 +1038,8 @@
     return lax.dot_general(a, b, TN, preferred_element_type=jnp.float32)
 
 
-PLAIN = cube_parts(128, (768, 640, 640))
+EVEN = cube_parts(128, (768, 640, 640))
+LIGHT = cube_parts(128, (896, 896, 256))
 TRIO = ("x", 4, 2)
 CHUNK = 64
 
@@ -1114,10 +1086,11 @@
     return u * half, slope
 
 
-def hidden_kernel(back, *refs):
+def hidden_kernel(back, plan, *refs):
     if back:
-        x_ref, we_hbm, wc_hbm, slope_hbm, o_ref, x_out, h_out = refs[:7]
-        scratch = refs[7:]
+        x_ref, we_hbm, wc_hbm, slope_hbm, act_hbm, n2_hbm, o_ref, dc_out, de_out, be_ref = refs[:10]
+        act_all, n2_all, d_tile = refs[10:13]
+        scratch = refs[13:]
     else:
         x_ref, we_hbm, wc_hbm, be_ref, o_ref, x_out, h_out, slope_out = refs[:8]
         scratch = refs[8:]
@@ -1129,7 +1102,11 @@
     loads = [pltpu.make_async_copy(we_hbm, we, load_sem.at[0]), pltpu.make_async_copy(wc_hbm, wc, load_sem.at[1])]
     if back:
         loads.append(pltpu.make_async_copy(slope_hbm, slope, load_sem.at[2]))
-    parts = tuple((0, CHUNK, c0, cn, order) for _, _, c0, cn, order in PLAIN)
+        late = [
+            pltpu.make_async_copy(act_hbm, act_all, load_sem.at[3]),
+            pltpu.make_async_copy(n2_hbm, n2_all, load_sem.at[4]),
+        ]
+    parts = tuple((0, CHUNK, c0, cn, order) for _, _, c0, cn, order in plan)
     gathers, sums = [], []
     for n in range(2):
         mine = x_ref.at[pl.ds(CHUNK * n, CHUNK)]
@@ -1140,14 +1117,14 @@
         sums.append(
             Reduce(
                 trio,
-                tuple((0, CHUNK, c0, cn, order[:3]) for _, _, c0, cn, order in PLAIN),
+                tuple((0, CHUNK, c0, cn, order[:3]) for _, _, c0, cn, order in plan),
                 came.at[n],
                 buf.at[n],
                 r_send.at[n],
                 r_recv.at[n],
             )
         )
-        gathers[n].start(range(3))
+        gathers[n].start(range(len(plan)))
     for one in loads[:-2]:
         one.start()
     core = 1 - lax.rem(lax.axis_index("shard"), 2)
@@ -1171,6 +1148,8 @@
             slope[n, four] = grad.astype(jnp.bfloat16).reshape(4, CHUNK, 512)
         h_all[n, four] = mid
         mid = mid.reshape(4 * CHUNK, 512)
+        if back:
+            be_ref[...] += jnp.sum(mid.astype(jnp.float32), axis=0, keepdims=True)
         for c in range(4):
             cols = pl.ds(512 * c, 512)
             tile = dot_nt(mid, we[cols, :]) if back else dot32(mid, wc[:, cols])
@@ -1215,25 +1194,60 @@
                 steps.append(functools.partial(core_add, n, r + 1))
         return steps + [functools.partial(core_add, n, 0)]
 
-    for step in chunk_gather_steps(gathers[0], 3):
+    for step in chunk_gather_steps(gathers[0], len(plan)):
         step()
     for one in loads:
         one.wait()
-    for step in spaced(chunk_gather_steps(gathers[1], 3), compute_steps(0)):
+    if back:
+        for one in late:
+            one.start()
+        be_ref[...] = jnp.zeros_like(be_ref)
+
+    tiles = []
+
+    def product(left, right, c, n, dst, slot):
+        if len(tiles) >= 2:
+            tiles[-2].wait()
+        if left is act_all:
+            x = right[:, :, :, pl.ds(512 * c, 512)].reshape(D, 512)
+            d_tile[slot] = dot_tn(left[...].reshape(D, 512), x).astype(jnp.bfloat16)
+        else:
+            x = left[:, :, :, pl.ds(512 * c, 512)].reshape(D, 512)
+            d_tile[slot] = dot_tn(x, right[...].reshape(D, 512)).astype(jnp.bfloat16)
+        tiles.append(pltpu.make_async_copy(d_tile.at[slot], dst, out_sem.at[slot]))
+        tiles[-1].start()
+
+    for step in spaced(chunk_gather_steps(gathers[1], len(plan)), compute_steps(0)):
         step()
-    outs = [pltpu.make_async_copy(x_all, x_out, out_sem.at[0])]
-    outs[0].start()
     out_rows = [o_ref.at[pl.ds(CHUNK * n, CHUNK)] for n in range(2)]
     first = chunk_reduce_steps(sums[0], out_rows[0])
+    outs = []
+    if back:
+        wait_late = [one.wait for one in late]
+        of_wc = [
+            functools.partial(product, act_all, x_all, c, n, dc_out.at[:, pl.ds(512 * c, 512)], c % 2)
+            for n, c in enumerate(range(4))
+        ]
+        of_we = [
+            functools.partial(product, n2_all, h_all, c, n, de_out.at[pl.ds(512 * c, 512)], c % 2)
+            for n, c in enumerate(range(4))
+        ]
+    else:
+        outs = [pltpu.make_async_copy(x_all, x_out, out_sem.at[0])]
+        outs[0].start()
     for step in spaced(first, compute_steps(1)):
         step()
-    outs.append(pltpu.make_async_copy(h_all, h_out, out_sem.at[1]))
-    if not back:
+    last_steps = chunk_reduce_steps(sums[1], out_rows[1])
+    if back:
+        last_steps = spaced(last_steps, wait_late + of_wc + of_we)
+    else:
+        outs.append(pltpu.make_async_copy(h_all, h_out, out_sem.at[1]))
         outs.append(pltpu.make_async_copy(slope, slope_out, out_sem.at[2]))
-    for one in outs[1:]:
-        one.start()
-    for step in chunk_reduce_steps(sums[1], out_rows[1]):
+        for one in outs[1:]:
+            one.start()
+    for step in last_steps:
         step()
+    outs += tiles[-2:]
     for n in range(2):
         gathers[n].finish()
         sums[n].finish()
@@ -1244,24 +1258,35 @@
         one.wait()
 
 
-def hidden_layer(back, x, we, wc, last, collective_id, name):
+def hidden_layer(back, x, we, wc, rest, plan, collective_id, name):
     bf16, f32 = jnp.bfloat16, jnp.float32
     dma = pltpu.SemaphoreType.DMA
     hbm, vmem = pl.BlockSpec(memory_space=pl.ANY), pl.BlockSpec(memory_space=pltpu.VMEM)
     wide, narrow = (2, 16, CHUNK, D), (2, 16, CHUNK, 512)
-    out = [
-        jax.ShapeDtypeStruct((128, D), f32),
-        jax.ShapeDtypeStruct(wide, bf16),
-        jax.ShapeDtypeStruct(narrow, bf16),
-    ]
-    if not back:
-        out.append(jax.ShapeDtypeStruct(narrow, bf16))
+    out = [jax.ShapeDtypeStruct((128, D), f32)]
+    more = []
+    if back:
+        out += [
+            jax.ShapeDtypeStruct((512, D), bf16),
+            jax.ShapeDtypeStruct((D, 512), bf16),
+            jax.ShapeDtypeStruct((1, 512), f32),
+        ]
+        out_specs = [vmem, hbm, hbm, vmem]
+        more = [pltpu.VMEM(narrow, bf16), pltpu.VMEM(wide, bf16), pltpu.VMEM((2, 512, 512), bf16)]
+    else:
+        out += [
+            jax.ShapeDtypeStruct(wide, bf16),
+            jax.ShapeDtypeStruct(narrow, bf16),
+            jax.ShapeDtypeStruct(narrow, bf16),
+        ]
+        out_specs = [vmem, hbm, hbm, hbm]
     return pl.pallas_call(
-        functools.partial(hidden_kernel, back),
+        functools.partial(hidden_kernel, back, plan),
         out_shape=out,
-        in_specs=[hbm, hbm, hbm, hbm if back else vmem],
-        out_specs=[vmem] + [hbm] * (len(out) - 1),
-        scratch_shapes=[
+        in_specs=[hbm, hbm, hbm] + ([hbm] * 3 if back else [vmem]),
+        out_specs=out_specs,
+        scratch_shapes=more
+        + [
             pltpu.VMEM(wide, bf16),
             pltpu.VMEM((D, 512), bf16),
             pltpu.VMEM((512, D), bf16),
@@ -1277,108 +1302,436 @@
             dma((2, 3, 8)),
             dma((2, 3, 8)),
             dma((2,)),
-            dma((3,)),
+            dma((5,)),
             dma((3,)),
         ],
         compiler_params=pltpu.CompilerParams(
             collective_id=collective_id, has_side_effects=True, vmem_limit_bytes=LIMIT
         ),
         name=name,
-    )(x, we, wc, last)
+    )(x, we, wc, *rest)
 
 
 QB = 256
 KB = WINDOW + QB
 SCALE = HD ** (-0.5)
-
-
-def kept_pairs(lo_ref, a):
+NEAR = (2, 4, "x")
+
+
+def kept_pairs(lo, a):
     key = a + lax.broadcasted_iota(jnp.int32, (KB, QB), 0)
     last = a + WINDOW + lax.broadcasted_iota(jnp.int32, (KB, QB), 1)
-    return (key >= lo_ref[0]) & (key <= last)
-
-
-def attend_kernel(lo_ref, q_ref, k_ref, v_ref, o_ref, lse_ref):
-    a = pl.multiple_of(lax.rem(pl.program_id(0), 4) * QB, QB)
-    keys = pl.ds(a, KB)
-    s = lax.dot_general(k_ref[0, keys], q_ref[0], NT, preferred_element_type=jnp.float32) * SCALE
-    s = jnp.where(kept_pairs(lo_ref, a), s, -1e30)
-    top = jnp.max(s, axis=0, keepdims=True)
-    e = jnp.exp(s - top)
-    total = jnp.sum(e, axis=0, keepdims=True)
-    probs = (e * (1.0 / total)).astype(jnp.bfloat16)
-    o_ref[0] = lax.dot_general(probs, v_ref[0, keys], TN, preferred_element_type=jnp.float32).astype(
-        o_ref.dtype
-    )
-    lse_ref[0] = top + jnp.log(total)
-
-
-def attend(lo, q, k, v):
-    per_q = pl.BlockSpec((1, QB, HD), lambda n: (n, 0, 0))
-    per_row = pl.BlockSpec((1, 1, QB), lambda n: (n, 0, 0))
-    per_micro = pl.BlockSpec((1, 2 * WINDOW, HD), lambda n: (n // 4, 0, 0))
+    return (key >= lo) & (key <= last)
+
+
+class PairSum:
+    def __init__(self, h, trio, plan, part, came, buf, sems):
+        self.c_send, self.c_recv, r_send, r_recv = sems
+        self.h, self.trio, self.part, self.came = h, trio, part, came
+        parts = tuple((0, 128, c0, cn, order[:3]) for _, _, c0, cn, order in plan)
+        self.sums = Reduce(trio, parts, came, buf, r_send, r_recv)
+        self.core = lax.rem(lax.axis_index("shard"), 2)
+
+    def pair(self, o):
+        return self.trio.at(NEAR, o)
+
+    def core_copy(self, o):
+        n = self.pair(o)
+        return remote(
+            self.part.at[2 * n + 1 - self.core],
+            self.came.at[n],
+            self.c_send.at[o],
+            self.c_recv.at[o],
+            self.h.partner[1],
+        )
+
+    def core_add(self, o):
+        self.core_copy(o).wait_recv()
+        n = self.pair(o)
+
+        @pl.loop(0, 8)
+        def _(i):
+            rows = pl.ds(pl.multiple_of(i * 16, 16), 16)
+            total = self.part[2 * n + self.core, rows, :].astype(jnp.float32) + self.came[
+                n, rows, :
+            ].astype(jnp.float32)
+            self.came[n, rows, :] = total.astype(jnp.bfloat16)
+
+        for p, (_, _, _, _, order) in enumerate(self.sums.parts):
+            bits = [o >> NEAR.index(d) & 1 for d in order]
+            if bits[2]:
+                self.sums.copy(p, 2, bits[0] | bits[1] << 1).start()
+
+    def schedule(self, compute, out, lag=2):
+        steps, waiting, made = [], [], []
+        for n, o in enumerate(range(7, -1, -1)):
+            steps.append(functools.partial(compute, o))
+            if n:
+                steps.append(functools.partial(self.core_add, o + 1))
+                made.append(o + 1)
+            for p, (_, _, _, _, order) in enumerate(self.sums.parts):
+                for low in range(4):
+                    own = sum((low >> b & 1) << NEAR.index(order[b]) for b in range(2))
+                    if own in made and made.index(own) <= len(made) - 1 - lag and (p, low) not in waiting:
+                        waiting.append((p, low))
+                        steps.append(functools.partial(self.sums.add, p, 2, low, out))
+        steps.append(functools.partial(self.core_add, 0))
+        rest = [
+            functools.partial(self.sums.add, p, j, low, out)
+            for j in reversed(range(3))
+            for low in reversed(range(1 << j))
+            for p in range(len(self.sums.parts))
+            if j < 2 or (p, low) not in waiting
+        ]
+        return steps, rest
+
+    def finish(self):
+        self.sums.finish()
+        for o in range(8):
+            self.core_copy(o).wait_send()
+
+
+def pair_gather_steps(g, used):
+    def number(o, order):
+        return sum((o >> NEAR.index(d) & 1) << n for n, d in enumerate(order[:3]))
+
+    def link(j, low):
+        for p in range(len(g.parts)):
+            g.copy(p, low, j).wait_recv()
+            for later in range(j + 1, 4):
+                g.copy(p, low | 1 << j, later).start()
+
+    def pair(o):
+        for p, part in enumerate(g.parts):
+            g.copy(p, number(o, part[4]), 3).wait_recv()
+        used(o)
+
+    steps = []
+    for j in range(3):
+        for low in range(1 << j):
+            steps.append(functools.partial(link, j, low))
+            for o in range(8):
+                if max(1, *[number(o, part[4]) for part in g.parts]) == low | 1 << j:
+                    steps.append(functools.partial(pair, o))
+    return steps
+
+
+def attend_kernel(plan, *refs):
+    ins, refs = refs[:8], refs[8:]
+    x_ref, kv_ref, wq_hbm, wkv_hbm, wo_hbm, bq_ref, bkv_ref, lo_ref = ins
+    o_ref, x_out, q_out, kv_out, mixed_out, lse_ref = refs[:6]
+    refs = refs[6:]
+    x_all, wq, wkv, wo, far, far_all, q_all, kv_all, mixed, part, came, buf = refs[:12]
+    g_send, g_recv, k_send, k_recv, swap_send, swap_recv, own_sem, load_sem, out_sem = refs[12:21]
+    pair_sems = refs[21:]
+    h, trio = Hyper(CUBE), Hyper(TRIO)
+    sec, shd = lax.axis_index("section"), lax.axis_index("shard")
+    other = (sec, shd + 8 * (1 - 2 * (shd // 8)))
+    h.barrier((other,))
+    swap = remote(kv_ref, far, swap_send, swap_recv, other)
+    swap.start()
+    loads = [
+        pltpu.make_async_copy(x_ref, x_all.at[h.pos], own_sem),
+        pltpu.make_async_copy(wq_hbm, wq, load_sem.at[0]),
+        pltpu.make_async_copy(wkv_hbm, wkv, load_sem.at[1]),
+        pltpu.make_async_copy(wo_hbm, wo, load_sem.at[2]),
+    ]
+    for one in loads:
+        one.start()
+    g = Gather(h, plan, x_ref, x_all, g_send, g_recv)
+    g.start(range(len(plan)))
+    swap.wait_recv()
+    far_all[h.pos] = far[...]
+    gkv = Gather(h, ((0, 128, 0, 2 * HD, CUBE),), far, far_all, k_send, k_recv)
+    gkv.start(range(1))
+    for one in loads:
+        one.wait()
+    sums = PairSum(h, trio, plan, part, came, buf, pair_sems)
+
+    def project(o):
+        n = sums.pair(o)
+        x = x_all[pl.ds(2 * n, 2)].reshape(QB, D)
+        q_all[n] = (dot32(x, wq[...]) + bq_ref[...]).astype(jnp.bfloat16)
+        at = pl.ds(pl.multiple_of(WINDOW + QB * lax.rem(n, 4), QB), QB)
+        kv_all[n // 4, at] = (dot32(x, wkv[...]) + bkv_ref[...]).astype(jnp.bfloat16)
+
+    far_steps = chunk_gather_steps(gkv, 1)
+    for step in spaced(pair_gather_steps(g, project), far_steps):
+        step()
+    kv_all[:, :WINDOW] = far_all[...].reshape(2, WINDOW, 2 * HD)
+
+    def compute(o):
+        n = sums.pair(o)
+        m, a = n // 4, pl.multiple_of(QB * lax.rem(n, 4), QB)
+        keys = pl.ds(a, KB)
+        s = dot_nt(kv_all[m, keys, :HD], q_all[n]) * SCALE
+        s = jnp.where(kept_pairs(lo_ref[n], a), s, -1e30)
+        top = jnp.max(s, axis=0, keepdims=True)
+        e = jnp.exp(s - top)
+        total = jnp.sum(e, axis=0, keepdims=True)
+        probs = (e * (1.0 / total)).astype(jnp.bfloat16)
+        mix = dot_tn(probs, kv_all[m, keys, HD:]).astype(jnp.bfloat16)
+        mixed[n] = mix
+        lse_ref[n] = top + jnp.log(total)
+        for c in range(4):
+            cols = pl.ds(512 * c, 512)
+            part[pl.ds(2 * n, 2), :, cols] = (
+                dot32(mix, wo[:, cols]).astype(jnp.bfloat16).reshape(2, 128, 512)
+            )
+        sums.core_copy(o).start()
+
+    outs = [
+        pltpu.make_async_copy(x_all, x_out, out_sem.at[0]),
+        pltpu.make_async_copy(q_all, q_out, out_sem.at[1]),
+        pltpu.make_async_copy(kv_all, kv_out, out_sem.at[2]),
+    ]
+    for one in outs:
+        one.start()
+    steps, rest = sums.schedule(compute, o_ref)
+    for step in steps:
+        step()
+    outs.append(pltpu.make_async_copy(mixed, mixed_out, out_sem.at[3]))
+    outs[-1].start()
+    for step in rest:
+        step()
+    g.finish()
+    gkv.finish()
+    swap.wait_send()
+    sums.finish()
+    for one in outs:
+        one.wait()
+
+
+def attend_layer(x, kv, wq, wkv, wo, bq, bkv, lo, plan, collective_id):
+    bf16, f32 = jnp.bfloat16, jnp.float32
+    dma = pltpu.SemaphoreType.DMA
+    hbm, vmem = pl.BlockSpec(memory_space=pl.ANY), pl.BlockSpec(memory_space=pltpu.VMEM)
+    out = [
+        jax.ShapeDtypeStruct((128, D), f32),
+        jax.ShapeDtypeStruct((16, 128, D), bf16),
+        jax.ShapeDtypeStruct((8, QB, HD), bf16),
+        jax.ShapeDtypeStruct((2, 2 * WINDOW, 2 * HD), bf16),
+        jax.ShapeDtypeStruct((8, QB, HD), bf16),
+        jax.ShapeDtypeStruct((8, 1, QB), f32),
+    ]
+    out_specs = [vmem, hbm, hbm, hbm, hbm, vmem]
     return pl.pallas_call(
-        attend_kernel,
-        grid=(8,),
-        out_shape=(
-            jax.ShapeDtypeStruct((8, QB, HD), jnp.bfloat16),
-            jax.ShapeDtypeStruct((8, 1, QB), jnp.float32),
+        functools.partial(attend_kernel, plan),
+        out_shape=out,
+        in_specs=[hbm] * 5 + [vmem] * 3,
+        out_specs=out_specs,
+        scratch_shapes=[
+            pltpu.VMEM((16, 128, D), bf16),
+            pltpu.VMEM((D, HD), bf16),
+            pltpu.VMEM((D, 2 * HD), bf16),
+            pltpu.VMEM((HD, D), bf16),
+            pltpu.VMEM((128, 2 * HD), bf16),
+            pltpu.VMEM((16, 128, 2 * HD), bf16),
+            pltpu.VMEM((8, QB, HD), bf16),
+            pltpu.VMEM((2, 2 * WINDOW, 2 * HD), bf16),
+            pltpu.VMEM((8, QB, HD), bf16),
+            pltpu.VMEM((16, 128, D), bf16),
+            pltpu.VMEM((8, 128, D), bf16),
+            pltpu.VMEM((8, 128, D), bf16),
+            dma((3, 16)),
+            dma((3, 16)),
+            dma((1, 16)),
+            dma((1, 16)),
+            dma,
+            dma,
+            dma,
+            dma((3,)),
+            dma((4,)),
+            dma((8,)),
+            dma((8,)),
+            dma((3, 8)),
+            dma((3, 8)),
+        ],
+        compiler_params=pltpu.CompilerParams(
+            collective_id=collective_id, has_side_effects=True, vmem_limit_bytes=LIMIT
         ),
-        in_specs=[per_row, per_q, per_micro, per_micro],
-        out_specs=[per_q, per_row],
-        compiler_params=pltpu.CompilerParams(vmem_limit_bytes=LIMIT),
         name="attend",
-    )(lo, q, k, v)
-
-
-def attend_back_kernel(lo_ref, lse_ref, q_ref, k_ref, v_ref, g_ref, dq_ref, far_ref, own_ref, dk_ref, dv_ref):
-    n = lax.rem(pl.program_id(0), 4)
-    a = pl.multiple_of(n * QB, QB)
-    keys = pl.ds(a, KB)
-
-    @pl.when(n == 0)
-    def _():
-        dk_ref[...] = jnp.zeros_like(dk_ref)
-        dv_ref[...] = jnp.zeros_like(dv_ref)
-
-    q, g, k = q_ref[0], g_ref[0], k_ref[0, keys]
-    s = lax.dot_general(k, q, NT, preferred_element_type=jnp.float32) * SCALE
-    probs = jnp.where(kept_pairs(lo_ref, a), jnp.exp(s - lse_ref[0]), 0.0)
-    gp = lax.dot_general(v_ref[0, keys], g, NT, preferred_element_type=jnp.float32)
-    dot = jnp.sum(probs * gp, axis=0, keepdims=True)
-    gs = (probs * (gp - dot)).astype(jnp.bfloat16)
-    dq = lax.dot_general(gs, k, TN, preferred_element_type=jnp.float32) * SCALE
-    dq_ref[0] = dq.astype(dq_ref.dtype)
-    dk_ref[keys] += jnp.dot(gs, q, preferred_element_type=jnp.float32) * SCALE
-    dv_ref[keys] += jnp.dot(probs.astype(jnp.bfloat16), g, preferred_element_type=jnp.float32)
-
-    @pl.when(n == 3)
-    def _():
-        for out, first in ((far_ref, 0), (own_ref, WINDOW)):
-            rows = pl.ds(first, WINDOW)
-            out[0, :, :HD] = dk_ref[rows].astype(out.dtype)
-            out[0, :, HD:] = dv_ref[rows].astype(out.dtype)
-
-
-def attend_back(lo, lse, q, k, v, g):
-    per_q = pl.BlockSpec((1, QB, HD), lambda n: (n, 0, 0))
-    per_row = pl.BlockSpec((1, 1, QB), lambda n: (n, 0, 0))
-    per_micro = pl.BlockSpec((1, 2 * WINDOW, HD), lambda n: (n // 4, 0, 0))
-    per_half = pl.BlockSpec((1, WINDOW, 2 * HD), lambda n: (n // 4, 0, 0))
+    )(x, kv, wq, wkv, wo, bq, bkv, lo)
+
+
+def attend_back_kernel(plan, *refs):
+    x_ref, n1_hbm, wq_hbm, wo_hbm, q_hbm, kv_hbm, mixed_hbm, lse_ref, lo_ref, gc, ge = refs[:11]
+    o_ref, own_ref, far_ref, wo_ref, wq_ref, bq_ref, rc, re = refs[11:19]
+    x_all, n1, wq, wo, q_all, kv_all, mixed, dq_all, g_all, dk, dv, part, came, buf = refs[19:33]
+    kv_parts, kv_bufs, sent = refs[33:35], refs[35:37], refs[37]
+    g_send, g_recv, swap_send, swap_recv, own_sem, load_sem, bg_send, bg_recv = refs[38:46]
+    pair_sems, kv_sems = refs[46:50], refs[50:54]
+    h, trio = Hyper(CUBE), Hyper(TRIO)
+    sec, shd = lax.axis_index("section"), lax.axis_index("shard")
+    half = shd // 8
+    other = (sec, shd + 8 * (1 - 2 * half))
+    h.barrier((other,))
+
+    def beside(n):
+        if n < 8:
+            rows = pl.ds(32 * n, 32)
+            src, dst = gc.at[1 - half, rows], rc.at[rows]
+        else:
+            rows = pl.ds(128 * (n - 8), 128)
+            src, dst = ge.at[1 - half, rows], re.at[rows]
+        return remote(src, dst, bg_send.at[n], bg_recv.at[n], other)
+
+    pending = list(range(16))
+
+    def feed(steps, every):
+        for n, step in enumerate(steps):
+            step()
+            if pending and n % every == 0:
+                beside(pending.pop(0)).start()
+
+    own = pltpu.make_async_copy(x_ref, x_all.at[h.pos], own_sem)
+    own.start()
+    g = Gather(h, plan, x_ref, x_all, g_send, g_recv)
+    g.start(range(len(plan)))
+    pairs = ((wq_hbm, wq), (wo_hbm, wo), (q_hbm, q_all), (kv_hbm, kv_all), (mixed_hbm, mixed), (n1_hbm, n1))
+    loads = [pltpu.make_async_copy(src, dst, load_sem.at[n]) for n, (src, dst) in enumerate(pairs)]
+    for one in loads:
+        one.start()
+    own.wait()
+    for one in loads[:5]:
+        one.wait()
+    sums = PairSum(h, trio, plan, part, came, buf, pair_sems)
+
+    def project(o):
+        n = sums.pair(o)
+        g_all[n] = dot_nt(x_all[pl.ds(2 * n, 2)].reshape(QB, D), wo[...]).astype(jnp.bfloat16)
+
+    feed(pair_gather_steps(g, project), 3)
+    bq_ref[...] = jnp.zeros_like(bq_ref)
+
+    def compute(o):
+        n = sums.pair(o)
+        m, a = n // 4, pl.multiple_of(QB * lax.rem(n, 4), QB)
+        keys = pl.ds(a, KB)
+        if o % 4 == 3:
+            dk[...] = jnp.zeros_like(dk)
+            dv[...] = jnp.zeros_like(dv)
+        q, gm, k = q_all[n], g_all[n], kv_all[m, keys, :HD]
+        s = dot_nt(k, q) * SCALE
+        probs = jnp.where(kept_pairs(lo_ref[n], a), jnp.exp(s - lse_ref[n]), 0.0)
+        gp = dot_nt(kv_all[m, keys, HD:], gm)
+        row = jnp.sum(probs * gp, axis=0, keepdims=True)
+        gs = (probs * (gp - row)).astype(jnp.bfloat16)
+        dq = (dot_tn(gs, k) * SCALE).astype(jnp.bfloat16)
+        dq_all[n] = dq
+        bq_ref[...] += jnp.sum(dq.astype(jnp.float32), axis=0, keepdims=True)
+        for c in range(4):
+            rows = pl.ds(512 * c, 512)
+            part[pl.ds(2 * n, 2), :, rows] = (
+                dot_nt(dq, wq[rows, :]).astype(jnp.bfloat16).reshape(2, 128, 512)
+            )
+        sums.core_copy(o).start()
+        dk[keys] += dot32(gs, q) * SCALE
+        dv[keys] += dot32(probs.astype(jnp.bfloat16), gm)
+        if o % 4 == 0:
+            eight = pl.ds(8 * m, 8)
+            for one, first in zip(kv_parts, (WINDOW, 0)):
+                rows = pl.ds(first, WINDOW)
+                one[eight, :, :HD] = dk[rows].astype(jnp.bfloat16).reshape(8, 128, HD)
+                one[eight, :, HD:] = dv[rows].astype(jnp.bfloat16).reshape(8, 128, HD)
+
+    steps, rest = sums.schedule(compute, o_ref)
+    feed(steps, 3)
+    kv_sums = [
+        Reduce(h, BESIDE[n], kv_parts[n], kv_bufs[n], kv_sems[2 * n], kv_sems[2 * n + 1]) for n in range(2)
+    ]
+    for n in reversed(range(8)):
+        for r in kv_sums:
+            r.copy(0, 3, n).start()
+
+    def product(out, left, right, c):
+        cols = pl.ds(512 * c, 512)
+        out[:, cols] = dot_tn(left[...].reshape(D, HD), right[:, :, cols].reshape(D, 512)).astype(out.dtype)
+
+    products = [functools.partial(product, wo_ref, mixed, x_all, c) for c in range(4)]
+    products += [loads[5].wait] + [functools.partial(product, wq_ref, dq_all, n1, c) for c in range(4)]
+    kv_steps = [
+        step
+        for pair in zip(chunk_reduce_steps(kv_sums[0], own_ref), chunk_reduce_steps(kv_sums[1], far_ref))
+        for step in pair
+    ]
+    feed(spaced(spaced(rest, kv_steps), products), 3)
+    while pending:
+        beside(pending.pop(0)).start()
+    sent[0] = far_ref[...].astype(sent.dtype)
+    swap = remote(sent.at[0], sent.at[1], swap_send, swap_recv, other)
+    swap.start()
+    g.finish()
+    sums.finish()
+    for r in kv_sums:
+        r.finish()
+    swap.wait()
+    far_ref[...] = sent[1].astype(jnp.float32)
+    for n in range(16):
+        beside(n).wait()
+
+
+def attend_back_layer(x, n1, wq, wo, q, kv, mixed, lse, lo, gc, ge, plan, collective_id):
+    bf16, f32 = jnp.bfloat16, jnp.float32
+    dma = pltpu.SemaphoreType.DMA
+    hbm, vmem = pl.BlockSpec(memory_space=pl.ANY), pl.BlockSpec(memory_space=pltpu.VMEM)
+    pair = pltpu.VMEM((16, 128, 2 * HD), bf16)
     return pl.pallas_call(
-        attend_back_kernel,
-        grid=(8,),
-        out_shape=(
-            jax.ShapeDtypeStruct((8, QB, HD), jnp.bfloat16),
-            jax.ShapeDtypeStruct((2, WINDOW, 2 * HD), jnp.bfloat16),
-            jax.ShapeDtypeStruct((2, WINDOW, 2 * HD), jnp.bfloat16),
+        functools.partial(attend_back_kernel, plan),
+        out_shape=[
+            jax.ShapeDtypeStruct((128, D), f32),
+            jax.ShapeDtypeStruct((128, 2 * HD), f32),
+            jax.ShapeDtypeStruct((128, 2 * HD), f32),
+            jax.ShapeDtypeStruct((HD, D), bf16),
+            jax.ShapeDtypeStruct((HD, D), bf16),
+            jax.ShapeDtypeStruct((1, HD), f32),
+            jax.ShapeDtypeStruct((256, D), bf16),
+            jax.ShapeDtypeStruct((1024, 512), bf16),
+        ],
+        in_specs=[hbm] * 7 + [vmem] * 2 + [hbm] * 2,
+        out_specs=[vmem] * 6 + [hbm] * 2,
+        scratch_shapes=[
+            pltpu.VMEM((16, 128, D), bf16),
+            pltpu.VMEM((16, 128, D), bf16),
+            pltpu.VMEM((D, HD), bf16),
+            pltpu.VMEM((HD, D), bf16),
+            pltpu.VMEM((8, QB, HD), bf16),
+            pltpu.VMEM((2, 2 * WINDOW, 2 * HD), bf16),
+            pltpu.VMEM((8, QB, HD), bf16),
+            pltpu.VMEM((8, QB, HD), bf16),
+            pltpu.VMEM((8, QB, HD), bf16),
+            pltpu.VMEM((2 * WINDOW, HD), f32),
+            pltpu.VMEM((2 * WINDOW, HD), f32),
+            pltpu.VMEM((16, 128, D), bf16),
+            pltpu.VMEM((8, 128, D), bf16),
+            pltpu.VMEM((8, 128, D), bf16),
+            pair,
+            pair,
+            pair,
+            pair,
+            pltpu.VMEM((2, 128, 2 * HD), bf16),
+            dma((3, 16)),
+            dma((3, 16)),
+            dma,
+            dma,
+            dma,
+            dma((6,)),
+            dma((16,)),
+            dma((16,)),
+            dma((8,)),
+            dma((8,)),
+            dma((3, 8)),
+            dma((3, 8)),
+            dma((1, 16)),
+            dma((1, 16)),
+            dma((1, 16)),
+            dma((1, 16)),
+        ],
+        compiler_params=pltpu.CompilerParams(
+            collective_id=collective_id, has_side_effects=True, vmem_limit_bytes=LIMIT
         ),
-        in_specs=[per_row, per_row, per_q, per_micro, per_micro, per_q],
-        out_specs=[per_q, per_half, per_half],
-        scratch_shapes=[pltpu.VMEM((2 * WINDOW, HD), jnp.float32)] * 2,
-        compiler_params=pltpu.CompilerParams(vmem_limit_bytes=LIMIT),
         name="attend_back",
-    )(lo, lse, q, k, v, g)
+    )(x, n1, wq, wo, q, kv, mixed, lse, lo, gc, ge)
 
 
 BESIDE = ((0, 128, 0, 256, (4, 2, "x", 1)),), ((0, 128, 0, 256, (2, "x", 4, 1)),)
@@ -1424,11 +1777,19 @@
         ]
     )
     small = jnp.concatenate([small, jnp.zeros((16 * 256 - small.shape[0],), bf16)]).reshape(16, 256)
-    shared, wq, wo = fetch_first(
-        jnp.concatenate([mixer_weight[0][:, D:], small], axis=0), mixer_weight[0], output_weight[0]
-    )
+    shared, wq, wo, we, wc = fetch_weights(
+        jnp.concatenate([mixer_weight[0][:, D:], small], axis=0),
+        mixer_weight[0],
+        output_weight[0],
+        expand_weight[0],
+        contract_weight[0],
+    )
+    we = [we[s].reshape(8 * 128, 512) for s in range(2)]
+    for s in range(2):
+        we[s] = from_halves(we[s])
+    wc = [from_halves(wc[s]) for s in range(2)]
+    wq = wq.reshape(2, D, HD)
     shared = shared.reshape(2, 16, 144, 256)
-    wq = from_halves(wq.reshape(2, 8 * 128, HD).transpose(1, 0, 2)).transpose(1, 0, 2)
     wkv = shared[:, :, :128].reshape(2, D, 256)
     vectors = shared[:, :, 128:].reshape(2, 16, 4096)
 
@@ -1458,28 +1819,24 @@
     for s in range(2):
         n1 = layer_norm(hidden, gain_one[s], shift_one[s]).astype(bf16)
         kv_rows = (dot32(n1, wkv[s]) + bias_kv[s]).astype(bf16)
-        if s == 0:
-            all_n1, far_kv, we, wc = gather_window(
-                n1, kv_rows, 3, (expand_weight[0], contract_weight[0])
-            )
-            we = [from_halves(we[n].reshape(8 * 128, 512)) for n in range(2)]
-            wc = [from_halves(wc[n]) for n in range(2)]
-        else:
-            all_n1, far_kv = gather_window(n1, kv_rows, 4)
-        all_n1 = all_n1.reshape(2048, D)
-        q = (dot32(all_n1, wq[s]) + bias_q[s]).astype(bf16).reshape(8, QB, HD)
-        kv = (dot32(all_n1, wkv[s]) + bias_kv[s]).astype(bf16).reshape(2, WINDOW, 256)
-        kv = jnp.concatenate([far_kv.reshape(2, WINDOW, 256), kv], axis=1)
-        k, v = kv[:, :, :HD], kv[:, :, HD:]
-        mixed, lse = attend(lo, q, k, v)
-        mixed = mixed.reshape(2048, HD)
-        part = dot32(mixed, wo[s]).astype(bf16).reshape(16, 128, D)
-        middle = hidden + reduce([part], CUBE, [PLAIN], 5, "reduce_rows")[0] + bias_out[s]
+        rows, all_n1, q, kv, mixed, lse = attend_layer(
+            n1,
+            kv_rows,
+            wq[s],
+            wkv[s],
+            wo[s],
+            bias_q[s][None],
+            bias_kv[s][None],
+            lo,
+            LIGHT if s == 0 else EVEN,
+            3 + s,
+        )
+        middle = hidden + rows + bias_out[s]
         n2 = layer_norm(middle, gain_two[s], shift_two[s]).astype(bf16)
-        rows, all_n2, act, slope = hidden_layer(False, n2, we[s], wc[s], bias_exp[s][None], 9, "hidden")
+        rows, all_n2, act, slope = hidden_layer(False, n2, we[s], wc[s], (bias_exp[s][None],), LIGHT if s == 0 else EVEN, 9 + 2 * s, "hidden")
         result = middle + rows + bias_con[s]
         results.append(result.astype(bf16))
-        kept.append((hidden, n1, all_n1, q, k, v, lse, mixed, middle, all_n2, act, slope))
+        kept.append((hidden, n1, all_n1, q, kv, lse, mixed, middle, all_n2, act, slope))
         hidden = results[-1].astype(f32)
 
     grad = lax.dynamic_index_in_dim(cotangent, sec, 0, keepdims=False).astype(f32)
@@ -1487,33 +1844,20 @@
     weight_grads = [None, None]
     small_grads = [None, None]
     for s in (1, 0):
-        hidden, n1, all_n1, q, k, v, lse, mixed, middle, all_n2, act, slope = kept[s]
+        hidden, n1, all_n1, q, kv, lse, mixed, middle, all_n2, act, slope = kept[s]
         go = grad.astype(bf16)
-        g_n2, all_go, g_pre = hidden_layer(True, go, we[s], wc[s], slope, 10, "hidden_back")
-        all_go, all_n2 = all_go.reshape(2048, D), all_n2.reshape(2048, D)
-        act, g_pre = act.reshape(2048, 512), g_pre.reshape(2048, 512)
-        d_wc = to_halves(dot_tn(act, all_go).astype(bf16))
-        d_we = to_halves(dot_tn(all_n2, g_pre).astype(bf16))
-        d_be = jnp.sum(g_pre.astype(f32), axis=0)
+        g_n2, d_wc, d_we, d_be = hidden_layer(
+            True, go, we[s], wc[s], (slope, act, all_n2), EVEN, 10, "hidden_back"
+        )
+        d_wc, d_we, d_be = d_wc.reshape(2, 256, D), d_we.reshape(2, 1024, 512), d_be[0]
         _, back = jax.vjp(layer_norm, middle, gain_two[s], shift_two[s])
         g_mid, d_gain_two, d_shift_two = back(g_n2)
         g_mid = grad + g_mid
         ga = g_mid.astype(bf16)
-        all_ga = gather(ga, CUBE, PLAIN, 6, "gather_rows").reshape(2048, D)
-        g_mixed = dot_nt(all_ga, wo[s]).astype(bf16).reshape(8, QB, HD)
-        d_wo = dot_tn(mixed, all_ga).astype(bf16)
-        dq, d_far, d_own = attend_back(lo, lse, q, k, v, g_mixed)
-        dq = dq.reshape(2048, HD)
-        d_wq = to_halves(dot_tn(all_n1, dq).astype(bf16))
-        part = dot_nt(dq, wq[s]).astype(bf16).reshape(16, 128, D)
-        rows, kv_own, kv_far = reduce(
-            [part, d_own.reshape(16, 128, 256), d_far.reshape(16, 128, 256)],
-            CUBE,
-            (PLAIN,) + BESIDE,
-            7,
-            "reduce_window",
-            True,
+        rows, kv_own, kv_far, d_wo, d_wq, d_bq, came_wc, came_we = attend_back_layer(
+            ga, all_n1, wq[s], wo[s], q, kv, mixed, lse, lo, d_wc, d_we, LIGHT, 5
         )
+        d_wc, d_we = with_other(d_wc, came_wc), with_other(d_we, came_we)
         dkv_rows = (kv_own + jnp.where(half == 0, kv_far, 0.0)).astype(bf16)
         g_n1 = rows + dot_nt(dkv_rows, wkv[s])
         _, back = jax.vjp(layer_norm, hidden, gain_one[s], shift_one[s])
@@ -1521,10 +1865,10 @@
         g_in = g_mid + g_in
         input_grads[s] = g_in
         d_wkv = dot_tn(n1, dkv_rows)
-        d_bq = jnp.sum(dq.astype(f32), axis=0)
+        d_bq = d_bq[0]
         d_bv = jnp.sum(dkv_rows[:, HD:].astype(f32), axis=0)
         weight_grads[s] = (
-            d_wq.reshape(8, 128, HD),
+            to_halves(d_wq.reshape(HD, 16, 128).transpose(1, 2, 0)).reshape(8, 128, HD),
             d_we.reshape(8, 128, 512),
             d_wo,
             d_wc,

time: 1260 us -> 1080 us (0.86)
  matrix products: 133 us -> 8.86 us
  waiting for transfers between devices: 81.4 us -> 23.4 us
    pallas_call x5 -> x1, Pallas kernels: 261 us -> 23.2 us  [reduce(): pl.pallas_call(functools.partial(reduce_kernel, dims, all_parts, swapped)...]
    pallas_call x13 -> x9, Pallas kernels: 602 us -> 836 us  [the longest x4 320 us: hidden_layer(): pl.pallas_call(functools.partial(hidden_kernel, back, plan), out_shape=ou...]
    dot_general x10 -> x2, matrix products: 64.7 us -> 2.82 us  [dot_tn(): return lax.dot_general(a, b, TN, preferred_element_type=jnp.float32)]
    reduce_scatter x6 -> x2, waiting for transfers between devices: 64 us -> 7.09 us  [to_halves(): lax.psum_scatter(x, 'shard', scatter_dimension=0, tiled=True, axis_index_...]
    dot_general x8 -> x2, matrix products: 37.5 us -> 1.95 us  [dot32(): return jnp.dot(a, b, preferred_element_type=jnp.float32)]
    dot_general x6 -> x2, matrix products: 30.8 us -> 4.09 us  [dot_nt(): return lax.dot_general(a, b, NT, preferred_element_type=jnp.float32)]
  transfers between devices with their start and end apart: 13 -> 8, of which waited for: 4 -> 2; matrix products, arithmetic and copies ran while one was open for 14% -> 4% of each run, Pallas kernels for 51% -> 27%
where the time goes in v3:
time: 1080 us; the launch traced here: 1070 us
  Pallas kernels  926 us (86%)
  other arithmetic  60.2 us (6%)
  local copies, waits for them, and re-layouts  34 us (3%)
  waiting for transfers between devices  23.4 us (2%)
  between operations  15.4 us (1%)
    pallas_call x4, Pallas kernels, hidden_layer(): pl.pallas_call(functools.partial(hidden_kernel, back, plan), out_shape=ou...  320 us
    pallas_call x2, Pallas kernels, attend_back_layer(): pl.pallas_call(functools.partial(attend_back_kernel, plan), out_shape=[ja...  240 us
    pallas_call x2, Pallas kernels, attend_layer(): pl.pallas_call(functools.partial(attend_kernel, plan), out_shape=out, in_...  187 us
    pallas_call x1, Pallas kernels, fetch_weights(): pl.pallas_call(fetch_kernel, out_shape=(jax.ShapeDtypeStruct((32,) + bloc...  90 us
    pallas_call x1, Pallas kernels, return_grads(): pl.pallas_call(return_kernel, out_shape=(jax.ShapeDtypeStruct((128, D), b...  66.1 us
    pallas_call x1, Pallas kernels, reduce(): pl.pallas_call(functools.partial(reduce_kernel, dims, all_parts, swapped)...  23.2 us
  transfers between devices with their start and end apart: 8, of which 2 were waited for; matrix products, arithmetic and copies ran while one was open for 4% of the time, Pallas kernels for 27%

profile of v3, /device:TPU:0, one launch (start us, length us, event | category | flops | bytes accessed | tf_op | source)
XLA Modules:
  0.0 1069.9 jit_solution(12933238785643296429)
XLA Ops:
  9.5 4.1 concatenate.43
  14.2 90.0 %fetch_weights.1 = (bf16[32,144,256]{2,1,0:T(8,128)(2,1)}, bf16[2,16,128,128]{3,2,1,0:T(8,128)(2,1)}, bf16[2,128,2048]{2,1,0:T(8,128)(2,1)}, bf16[2,8,128,512]{3,2,1,0:T(8,128)(2,1)}, bf16[2,256,2048]{2,1,0:T(8,128)(2,1)}) custom-call(bf16[144,256]{1,0:T(8,128)(2,1)} %pad_maximum_fusion.4.block, bf16[128,2304]{1,0:T(8,128)(2,1)} %bitcast.259, ...), custom_call_target="tpu_custom_call" | custom-call | tf_op jit(solution)/shard_map/fetch_weights/pallas_call | solution.py:870
  104.2 3.2 fusion.73
  111.7 3.0 fusion.71
  118.4 2.0 convert_reduce_fusion
  120.5 2.3 fusion.74
  125.4 108.3 %attend.2 = (f32[128,2048]{1,0:T(8,128)}, bf16[16,128,2048]{2,1,0:T(8,128)(2,1)}, bf16[8,256,128]{2,1,0:T(8,128)(2,1)}, bf16[2,2048,256]{2,1,0:T(8,128)(2,1)}, b...) custom-call(bf16[128,2048]{1,0:T(8,128)(2,1)} %fusion.24.refs_0_, bf16[128,256]{1,0:T(8,128)(2,1)} %fusion.18.refs_1_, ...), custom_call_target="tpu_custom_call" | custom-call | tf_op jit(solution)/shard_map/attend/pallas_call | solution.py:1518
  239.3 104.0 %hidden.2 = (f32[128,2048]{1,0:T(8,128)}, bf16[2,16,64,2048]{3,2,1,0:T(8,128)(2,1)}, bf16[2,16,64,512]{3,2,1,0:T(8,128)(2,1)}, bf16[2,16,64,512]{3,2,1,0:T(8,128)(2,1)}) custom-call(bf16[128,2048]{1,0:T(8,128)(2,1)} %add_convert_fusion.3.refs_0_, bf16[2048,512]{1,0:T(8,128)(2,1)} %all-gather.7.cloned.1.call-done.refs_1_, bf16[512,2048]{1,0:T(8,128)(2,1)} %bitcast.230, ...), custom_call_target="tpu_custom_call" | custom-call | tf_op jit(solution)/shard_map/hidden/pallas_call | solution.py:1283
  346.5 78.6 %attend.3 = (f32[128,2048]{1,0:T(8,128)}, bf16[16,128,2048]{2,1,0:T(8,128)(2,1)}, bf16[8,256,128]{2,1,0:T(8,128)(2,1)}, bf16[2,2048,256]{2,1,0:T(8,128)(2,1)}, b...) custom-call(bf16[128,2048]{1,0:T(8,128)(2,1)} %copy-done.10, bf16[128,256]{1,0:T(8,128)(2,1)} %fusion.19.refs_1_, ...), custom_call_target="tpu_custom_call" | custom-call | tf_op jit(solution)/shard_map/attend/pallas_call | solution.py:1518
  428.0 70.0 %hidden.3 = (f32[128,2048]{1,0:T(8,128)}, bf16[2,16,64,2048]{3,2,1,0:T(8,128)(2,1)}, bf16[2,16,64,512]{3,2,1,0:T(8,128)(2,1)}, bf16[2,16,64,512]{3,2,1,0:T(8,128)(2,1)}) custom-call(bf16[128,2048]{1,0:T(8,128)(2,1)} %add_convert_fusion.1.refs_0_, bf16[2048,512]{1,0:T(8,128)(2,1)} %all-gather.9.cloned.1.call-done.refs_1_, bf16[512,2048]{1,0:T(8,128)(2,1)} %bitcast.232, ...), custom_call_target="tpu_custom_call" | custom-call | tf_op jit(solution)/shard_map/hidden/pallas_call | solution.py:1283
  497.9 72.4 %hidden_back.2 = (f32[128,2048]{1,0:T(8,128)}, bf16[512,2048]{1,0:T(8,128)(2,1)}, bf16[2048,512]{1,0:T(8,128)(2,1)}, f32[1,512]{1,0:T(1,128)}) custom-call(bf16[128,2048]{1,0:T(8,128)(2,1)} %get-tuple-element.166.refs_0_, bf16[2048,512]{1,0:T(8,128)(2,1)} %all-gather.9.cloned.1.call-done.refs_1_, bf16[512,2048]{1,0:T(8,128)(2,1)} %bitcast.233, ...), custom_call_target="tpu_custom_call" | custom-call | tf_op jit(solution)/shard_map/hidden_back/pallas_call | solution.py:1283
  570.4 1.7 multiply_reduce_fusion
  574.5 119.5 %attend_back.2 = (f32[128,2048]{1,0:T(8,128)}, f32[128,256]{1,0:T(8,128)}, f32[128,256]{1,0:T(8,128)}, bf16[128,2048]{1,0:T(8,128)(2,1)}, bf16[128,2048]{1,0:T(8...) custom-call(bf16[128,2048]{1,0:T(8,128)(2,1)} %get-tuple-element.140.refs_0_, ...), custom_call_target="tpu_custom_call" | custom-call | tf_op jit(solution)/shard_map/attend_back/pallas_call | solution.py:1679
  696.6 2.0 fusion.59
  699.2 2.1 fusion.60
  701.2 73.4 %hidden_back.3 = (f32[128,2048]{1,0:T(8,128)}, bf16[512,2048]{1,0:T(8,128)(2,1)}, bf16[2048,512]{1,0:T(8,128)(2,1)}, f32[1,512]{1,0:T(1,128)}) custom-call(bf16[128,2048]{1,0:T(8,128)(2,1)} %get-tuple-element.135.refs_0_, bf16[2048,512]{1,0:T(8,128)(2,1)} %all-gather.7.cloned.1.call-done.refs_1_, bf16[512,2048]{1,0:T(8,128)(2,1)} %bitcast.231, ...), custom_call_target="tpu_custom_call" | custom-call | tf_op jit(solution)/shard_map/hidden_back/pallas_call | solution.py:1283
  774.6 1.7 multiply_reduce_fusion.1
  778.4 120.3 %attend_back.3 = (f32[128,2048]{1,0:T(8,128)}, f32[128,256]{1,0:T(8,128)}, f32[128,256]{1,0:T(8,128)}, bf16[128,2048]{1,0:T(8,128)(2,1)}, bf16[128,2048]{1,0:T(8...) custom-call(bf16[128,2048]{1,0:T(8,128)(2,1)} %get-tuple-element.138.refs_0_, ...), custom_call_target="tpu_custom_call" | custom-call | tf_op jit(solution)/shard_map/attend_back/pallas_call | solution.py:1679
  902.6 2.1 fusion.58
  907.3 3.1 maximum_maximum_fusion.refs_0_
  910.4 23.2 %reduce_shared.1 = f32[144,256]{1,0:T(8,128)} custom-call(bf16[32,144,256]{2,1,0:T(8,128)(2,1)} %maximum_maximum_fusion.refs_0_), custom_call_target="tpu_custom_call" | custom-call | tf_op jit(solution)/shard_map/reduce_shared/pallas_call | solution.py:678
  936.3 2.8 fusion.3
  940.4 2.0 copy.33
  942.5 2.0 copy.34
  945.1 3.1 convert_select_fusion.2
  954.5 2.3 pad_maximum_fusion.2.go
  958.3 15.0 %collective-permute-done = bf16[128,2048]{1,0:T(8,128)(2,1)} collective-permute-done((bf16[128,2048]{1,0:T(8,128)(2,1)}, bf16[128,2048]{1,0:T(8,128)(2,1)}, u32[]{:S(2)}, u32[]{:S(2)}) %collective-permute-start) | collective-permute-done | bytes 524320 | tf_op jit(solution)/shard_map/ppermute | solution.py:1911
  977.5 7.1 reduce-scatter.5.cloned.1.call-done
  984.6 1.9 pad_maximum_fusion.3.gq
  986.4 66.1 %return_grads.1 = (bf16[128,2048]{1,0:T(8,128)(2,1)}, bf16[128,8192]{1,0:T(8,128)(2,1)}, bf16[2,128,2048]{2,1,0:T(8,128)(2,1)}, bf16[512,2048]{1,0:T(8,128)(2,1)}) custom-call(bf16[2,8,128,128]{3,2,1,0:T(8,128)(2,1)} %pad_maximum_fusion.3.gq, bf16[2,8,128,512]{3,2,1,0:T(8,128)(2,1)} %pad_maximum_fusion.ge, bf16[2,128,2048]{2,1,0:T(8,128)(2,1)} %pad_maximum_fusion.2.go, ...), custom_call_target="tpu_custom_call" | custom-call | tf_op jit(solution)/shard_map/return_grads/pallas_call | solution.py:991
  1052.5 4.3 bitcast_convert_fusion
  1056.8 2.4 bitcast_convert_fusion.1
  (236 shorter events, 58.6 us)
Async XLA Ops:
  7.2 232.1 %all-gather.7.cloned.1.call-start = ((), (), s32[]{:S(2)}) async-start(), calls=%async_computation.2 | async-start | bytes 3145728 | tf_op jit(solution)/shard_map/all_gather | solution.py:1013
  104.2 3.3 copy-start.23
  107.4 131.9 %all-gather.11.cloned.1.call-start = ((), (), s32[]{:S(2)}) async-start(), calls=%async_computation.6 | async-start | bytes 3145728 | tf_op jit(solution)/shard_map/all_gather | solution.py:1013
  109.0 319.0 %all-gather.9.cloned.1.call-start = ((), (), s32[]{:S(2)}) async-start(), calls=%async_computation.3 | async-start | bytes 3145728 | tf_op jit(solution)/shard_map/all_gather | solution.py:1013
  109.7 318.3 %all-gather.13.cloned.1.call-start = ((), (), s32[]{:S(2)}) async-start(), calls=%async_computation.7 | async-start | bytes 3145728 | tf_op jit(solution)/shard_map/all_gather | solution.py:1013
  110.3 867.2 %reduce-scatter.3.cloned.1.call-start = ((), (), s32[]{:S(2)}) async-start(), calls=%async_computation.4 | async-start | bytes 786432 | tf_op jit(solution)/shard_map/reduce_scatter | solution.py:1022
  111.7 3.1 copy-start
  114.7 9.2 copy-start.7
  114.7 3.7 copy-start.36
  115.2 7.5 copy-start.29
  117.8 6.0 copy-start.35
  117.8 227.8 %copy-start.34 = (f32[1,256]{1,0:T(1,128)}, f32[1,256]{1,0:T(1,128)S(1)}, u32[]{:S(2)}) copy-start(f32[1,256]{1,0:T(1,128)S(1)} %get-tuple-element.209.refs_6_) | copy-start | bytes 3076
  233.8 2.9 copy-start.25
  574.5 120.6 %copy-start.11 = (bf16[128,2048]{1,0:T(8,128)(2,1)S(1)}, bf16[128,2048]{1,0:T(8,128)(2,1)}, u32[]{:S(2)}) copy-start(bf16[128,2048]{1,0:T(8,128)(2,1)} %copy-done.10) | copy-start | bytes 1572868
  694.0 2.6 copy-start.3
  696.6 2.5 copy-start.5
  696.6 2.5 copy-start.26
  778.4 121.4 %copy-start.22 = (bf16[2048,128]{1,0:T(8,128)(2,1)S(1)}, bf16[2048,128]{1,0:T(8,128)(2,1)}, u32[]{:S(2)}) copy-start(bf16[2048,128]{1,0:T(8,128)(2,1)} %copy.35) | copy-start | bytes 1572868
  778.4 123.6 %copy-start.38 = (f32[1,512]{1,0:T(1,128)S(1)}, f32[1,512]{1,0:T(1,128)}, u32[]{:S(2)}) copy-start(f32[1,512]{1,0:T(1,128)} %get-tuple-element.104) | copy-start | bytes 6148
  898.7 3.9 copy-start.1
  902.6 3.8 copy-start.39
  902.6 4.0 copy-start.37
  933.6 5.5 copy-start.13
  933.6 5.5 copy-start.28
  942.5 42.1 %reduce-scatter.5.cloned.1.call-start = ((), (), s32[]{:S(2)}) async-start(), calls=%async_computation.5 | async-start | bytes 786432 | tf_op jit(solution)/shard_map/reduce_scatter | solution.py:1022
  945.1 5.2 copy-start.17
  945.1 5.2 copy-start.18
  948.2 27.4 %collective-permute-start.1 = (bf16[128,2048]{1,0:T(8,128)(2,1)}, bf16[128,2048]{1,0:T(8,128)(2,1)S(1)}, u32[]{:S(2)}, u32[]{:S(2)}) collective-permute-start(bf16[128,2048]{1,0:T(8,128)(2,1)} %get-tuple-element.141), channel_id=1, source_target_pairs={{0,16},{16,0},{1,17},{17,1},{2,18},{18,2},{3,19},{19,3},{4,20},{20... | collective-permute-start | bytes 1572872 | tf_op jit(solution)/shard_map/ppermute | solution.py:1911
  949.5 23.8 %collective-permute-start = (bf16[128,2048]{1,0:T(8,128)(2,1)}, bf16[128,2048]{1,0:T(8,128)(2,1)}, u32[]{:S(2)}, u32[]{:S(2)}) collective-permute-start(bf16[128,2048]{1,0:T(8,128)(2,1)} %get-tuple-element.171), channel_id=1, source_target_pairs={{0,16},{16,0},{1,17},{17,1},{2,18},{18,2},{3,19},{19,3},{4,20},{20... | collective-permute-start | bytes 1572872 | tf_op jit(solution)/shard_map/ppermute | solution.py:1911
  950.3 2.6 copy-start.30
  956.8 16.5 %copy-start.24 = (bf16[128,2048]{1,0:T(8,128)(2,1)S(1)}, bf16[128,2048]{1,0:T(8,128)(2,1)}, u32[]{:S(2)}) copy-start(bf16[128,2048]{1,0:T(8,128)(2,1)} %get-tuple-element.172) | copy-start | bytes 1572868
  1052.5 4.3 copy-start.21
  (17 other events, 30.5 us)
Sparse Core Ops, SparseCore 0:
  107.5 58.4 all-gather.6
  168.2 55.5 all-gather.10
  225.9 55.5 all-gather.8
  283.5 55.5 all-gather.12
  942.6 19.6 reduce-scatter.2
  964.4 20.0 reduce-scatter.4

commit v4 on v3

--- a/solution.py
+++ b/solution.py
@@ -551,38 +551,6 @@
                     self.copy(p, low, j).wait_send()
 
 
-def gather_kernel(dims, parts, x_ref, o_ref, send_sem, recv_sem, local_sem):
-    h = Hyper(dims)
-    h.barrier()
-    own = pltpu.make_async_copy(x_ref, o_ref.at[h.pos], local_sem)
-    own.start()
-    g = Gather(h, parts, x_ref, o_ref, send_sem, recv_sem)
-    chosen = range(len(parts))
-    g.start(chosen)
-    g.forward(chosen)
-    g.finish()
-    own.wait()
-
-
-def gather(x, dims, parts, collective_id, name):
-    n = 1 << len(dims)
-    return pl.pallas_call(
-        functools.partial(gather_kernel, dims, parts),
-        out_shape=jax.ShapeDtypeStruct((n,) + x.shape, x.dtype),
-        in_specs=[pl.BlockSpec(memory_space=pl.ANY)],
-        out_specs=pl.BlockSpec(memory_space=pl.ANY),
-        scratch_shapes=[
-            pltpu.SemaphoreType.DMA((len(parts), n)),
-            pltpu.SemaphoreType.DMA((len(parts), n)),
-            pltpu.SemaphoreType.DMA,
-        ],
-        compiler_params=pltpu.CompilerParams(
-            collective_id=collective_id, has_side_effects=True, vmem_limit_bytes=LIMIT
-        ),
-        name=name,
-    )(x)
-
-
 class Reduce:
     def __init__(self, h, parts, src, buf, send_sem, recv_sem):
         self.h, self.parts, self.src, self.buf = h, parts, src, buf
@@ -631,61 +599,6 @@
             for j in range(len(self.h.dims)):
                 for low in range(1 << j):
                     self.copy(p, j, low).wait_send()
-
-
-def reduce_kernel(dims, all_parts, swapped, *refs):
-    count = len(all_parts)
-    xs, outs, bufs = refs[:count], refs[count : 2 * count], refs[2 * count : 3 * count]
-    sems = refs[3 * count :]
-    h = Hyper(dims)
-    k = len(dims)
-    sec, shd = lax.axis_index("section"), lax.axis_index("shard")
-    other = (sec, shd + 8 * (1 - 2 * lax.rem(shd // 8, 2)))
-    h.barrier((other,) if swapped else ())
-    sums = [
-        Reduce(h, parts, xs[n], bufs[n], sems[2 * n], sems[2 * n + 1])
-        for n, parts in enumerate(all_parts)
-    ]
-    every = [(r, p, outs[n]) for n, r in enumerate(sums) for p in range(len(all_parts[n]))]
-    for low in reversed(range(1 << (k - 1))):
-        for r, p, _ in every:
-            r.copy(p, k - 1, low).start()
-    for j in reversed(range(k)):
-        for low in reversed(range(1 << j)):
-            for r, p, out in every:
-                r.add(p, j, low, out)
-    if swapped:
-        sent, swap_send, swap_recv = sems[2 * count :]
-        out = outs[-1]
-        sent[0] = out[...].astype(sent.dtype)
-        swap = remote(sent.at[0], sent.at[1], swap_send, swap_recv, other)
-        swap.start()
-        swap.wait()
-        out[...] = sent[1].astype(jnp.float32)
-    for r in sums:
-        r.finish()
-
-
-def reduce(xs, dims, all_parts, collective_id, name, swapped=False):
-    n = 1 << len(dims)
-    dma = pltpu.SemaphoreType.DMA
-    vmem = pl.BlockSpec(memory_space=pltpu.VMEM)
-    scratch = [pltpu.VMEM(x.shape, x.dtype) for x in xs]
-    for parts in all_parts:
-        scratch += [dma((len(parts), n))] * 2
-    if swapped:
-        scratch += [pltpu.VMEM((2,) + xs[-1].shape[1:], xs[-1].dtype), dma, dma]
-    return pl.pallas_call(
-        functools.partial(reduce_kernel, dims, all_parts, swapped),
-        out_shape=[jax.ShapeDtypeStruct(x.shape[1:], jnp.float32) for x in xs],
-        in_specs=[vmem] * len(xs),
-        out_specs=[vmem] * len(xs),
-        scratch_shapes=scratch,
-        compiler_params=pltpu.CompilerParams(
-            collective_id=collective_id, has_side_effects=True, vmem_limit_bytes=LIMIT
-        ),
-        name=name,
-    )(*xs)
 
 
 def block_of(sec, shd):
@@ -898,112 +811,116 @@
     )(block, mix, out, exp, con)
 
 
-def return_kernel(gq, ge, go, gc, rq, re, ro, rc, *sems):
-    send, recv, con_send, con_recv, out_send, out_recv, own_sem = sems
+def last_kernel(small, gq0, gq1, go0, go1, cross, total, rq, ro, crossed, *scratch):
+    buf, s_send, s_recv, q_send, q_recv, out_send, out_recv, own_sem, x_send, x_recv = scratch
     sec, shd = lax.axis_index("section"), lax.axis_index("shard")
-    me, place = half_group(sec, shd)
-    half_barrier(me, place, sec, shd)
-    low, half = lax.rem(shd, 8), shd // 8
+    half = shd // 8
     f = block_of(sec, shd)
-
-    def pieces(ts, tj):
-        tlow = lax.rem(tj, 8)
-        yield gq.at[ts, tlow], rq.at[:, columns(f, HD)]
-        for h in range(2):
-            yield (
-                ge.at[ts, tlow, :, pl.ds(256 * h, 256)],
-                re.at[:, columns(2 * (8 * h + low) + sec, 256)],
-            )
-
-    def spread(d):
-        there = place(lax.rem(me + d, 16))
-        return [
-            remote(src, dst, send.at[n, d], recv.at[n, d], there)
-            for n, (src, dst) in enumerate(pieces(*there))
-        ]
-
-    @pl.loop(1, 16)
-    def _(d):
-        for one in spread(d):
-            one.start()
-
-    own = [
-        pltpu.make_async_copy(src, dst, own_sem.at[n])
-        for n, (src, dst) in enumerate(pieces(sec, shd))
-    ]
-    own.append(pltpu.make_async_copy(gc.at[sec], rc.at[pl.ds(256 * sec, 256)], own_sem.at[3]))
-    for one in own:
-        one.start()
-    rows = remote(gc.at[1 - sec], rc.at[pl.ds(256 * sec, 256)], con_send, con_recv, (1 - sec, shd))
-    rows.start()
-
-    own_out = pltpu.make_async_copy(go.at[sec], ro.at[half], own_sem.at[4])
+    everyone_barrier(16 * sec + shd)
+    h = Hyper(ALL)
+    k = len(ALL)
+    r = Reduce(h, SMALL, small, buf, s_send, s_recv)
+    for low in reversed(range(1 << (k - 1))):
+        for p in range(len(SMALL)):
+            r.copy(p, k - 1, low).start()
+    swap = remote(cross, crossed, x_send, x_recv, (1 - sec, shd))
+    pl.when(sec == 1)(swap.start)
+
+    def query(s, d):
+        src = (gq0, gq1)[s].at[lax.rem(shd + d, 16)]
+        dst = rq.at[half, :, columns(f, HD)]
+        return src, dst, remote(src, dst, q_send.at[s, d], q_recv.at[sec, d], (s, lax.rem(shd + d, 16)))
+
+    def rows(s):
+        src, dst = (go0, go1)[s], ro.at[half]
+        return src, dst, remote(src, dst, out_send.at[s], out_recv.at[half], (s, f))
+
+    def either(local, n, copy, start):
+        src, dst, there = copy
+        here = pltpu.make_async_copy(src, dst, own_sem.at[n])
+
+        @pl.when(local)
+        def _():
+            here.start() if start else here.wait()
+
+        @pl.when(jnp.logical_not(local))
+        def _():
+            there.start() if start else there.wait_send()
+
     for s in range(2):
-        mine = jnp.logical_and(sec == s, f == shd)
-        there = remote(go.at[s], ro.at[half], out_send.at[s], out_recv.at[half], (s, f))
-
-        @pl.when(mine)
+        either(sec == s, 0, query(s, 0), True)
+        either(jnp.logical_and(sec == s, f == shd), 1, rows(s), True)
+
+        @pl.loop(1, 16)
+        def _(d):
+            query(s, d)[2].start()
+
+    for j in reversed(range(k)):
+        for low in reversed(range(1 << j)):
+            for p in range(len(SMALL)):
+                r.add(p, j, low, total)
+    pl.when(sec == 1)(swap.wait_send)
+    pl.when(sec == 0)(swap.wait_recv)
+
+    def arrival(s, d):
+        return remote(gq0.at[0], rq.at[0, :, pl.ds(0, HD)], q_send.at[0, 0], q_recv.at[s, d], (1 - sec, shd))
+
+    for s in range(2):
+
+        @pl.when(sec != s)
         def _():
-            own_out.start()
-
-        @pl.when(jnp.logical_not(mine))
+            arrival(s, 0).wait_recv()
+
+        @pl.loop(1, 16)
+        def _(d):
+            arrival(s, d).wait_recv()
+
+        @pl.when(jnp.logical_not(jnp.logical_and(f == shd, half == s)))
         def _():
-            there.start()
-
-    @pl.loop(1, 16)
-    def _(d):
-        for one in spread(d):
-            one.wait_recv()
-
-    remote(gc.at[0], rc.at[pl.ds(256 * (1 - sec), 256)], con_send, con_recv, (1 - sec, shd)).wait_recv()
-    for z in range(2):
-        mine = jnp.logical_and(f == shd, half == z)
-
-        @pl.when(jnp.logical_not(mine))
-        def _():
-            remote(go.at[0], ro.at[z], out_send.at[0], out_recv.at[z], (1 - sec, shd)).wait_recv()
-
-    @pl.loop(1, 16)
-    def _(d):
-        for one in spread(d):
-            one.wait_send()
-
-    rows.wait_send()
+            remote(go0, ro.at[s], out_send.at[0], out_recv.at[s], (1 - sec, shd)).wait_recv()
+
     for s in range(2):
-        mine = jnp.logical_and(sec == s, f == shd)
-        there = remote(go.at[s], ro.at[half], out_send.at[s], out_recv.at[half], (s, f))
-
-        @pl.when(mine)
-        def _():
-            own_out.wait()
-
-        @pl.when(jnp.logical_not(mine))
-        def _():
-            there.wait_send()
-
-    for one in own:
-        one.wait()
-
-
-def return_grads(gq, ge, go, gc):
-    bf16 = jnp.bfloat16
+        either(sec == s, 0, query(s, 0), False)
+        either(jnp.logical_and(sec == s, f == shd), 1, rows(s), False)
+
+        @pl.loop(1, 16)
+        def _(d):
+            query(s, d)[2].wait_send()
+
+    r.finish()
+
+
+def return_last(small, gq, go, cross):
+    bf16, f32 = jnp.bfloat16, jnp.float32
     dma = pltpu.SemaphoreType.DMA
+    hbm, vmem = pl.BlockSpec(memory_space=pl.ANY), pl.BlockSpec(memory_space=pltpu.VMEM)
     return pl.pallas_call(
-        return_kernel,
+        last_kernel,
         out_shape=(
+            jax.ShapeDtypeStruct(small.shape[1:], f32),
+            jax.ShapeDtypeStruct((2, 128, D), bf16),
+            jax.ShapeDtypeStruct((2, 128, D), bf16),
             jax.ShapeDtypeStruct((128, D), bf16),
-            jax.ShapeDtypeStruct((128, 8192), bf16),
-            jax.ShapeDtypeStruct((2, 128, D), bf16),
-            jax.ShapeDtypeStruct((512, D), bf16),
         ),
-        in_specs=[pl.BlockSpec(memory_space=pl.ANY)] * 4,
-        out_specs=[pl.BlockSpec(memory_space=pl.ANY)] * 4,
-        scratch_shapes=[dma((3, 16)), dma((3, 16)), dma, dma, dma((2,)), dma((2,)), dma((5,))],
+        in_specs=[vmem] + [hbm] * 5,
+        out_specs=[vmem] + [hbm] * 3,
+        scratch_shapes=[
+            pltpu.VMEM(small.shape, bf16),
+            dma((3, 32)),
+            dma((3, 32)),
+            dma((2, 16)),
+            dma((2, 16)),
+            dma((2,)),
+            dma((2,)),
+            dma((2,)),
+            dma,
+            dma,
+        ],
         compiler_params=pltpu.CompilerParams(
             collective_id=2, has_side_effects=True, vmem_limit_bytes=LIMIT
         ),
-        name="return_grads",
-    )(gq, ge, go, gc)
+        name="return_last",
+    )(small, *gq, *go, cross)
 
 
 HALVES = [[n, n + 8] for n in range(8)]
@@ -1011,15 +928,6 @@
 
 def from_halves(x):
     return lax.all_gather(x, "shard", axis=0, tiled=True, axis_index_groups=HALVES)
-
-
-def with_other(x, came):
-    mine = lax.dynamic_index_in_dim(x, lax.axis_index("shard") // 8, 0, keepdims=False)
-    return (mine.astype(jnp.float32) + came.astype(jnp.float32)).astype(x.dtype)
-
-
-def to_halves(x):
-    return lax.psum_scatter(x, "shard", scatter_dimension=0, tiled=True, axis_index_groups=HALVES)
 
 
 NT = (((1,), (1,)), ((), ()))
@@ -1385,6 +1293,17 @@
         ]
         return steps, rest
 
+    def following(self, compute):
+        before = []
+
+        def step(o):
+            compute(o)
+            if before:
+                self.core_add(before.pop())
+            before.append(o)
+
+        return step, lambda: self.core_add(before.pop())
+
     def finish(self):
         self.sums.finish()
         for o in range(8):
@@ -1554,35 +1473,164 @@
     )(x, kv, wq, wkv, wo, bq, bkv, lo)
 
 
-def attend_back_kernel(plan, *refs):
-    x_ref, n1_hbm, wq_hbm, wo_hbm, q_hbm, kv_hbm, mixed_hbm, lse_ref, lo_ref, gc, ge = refs[:11]
-    o_ref, own_ref, far_ref, wo_ref, wq_ref, bq_ref, rc, re = refs[11:19]
-    x_all, n1, wq, wo, q_all, kv_all, mixed, dq_all, g_all, dk, dv, part, came, buf = refs[19:33]
-    kv_parts, kv_bufs, sent = refs[33:35], refs[35:37], refs[37]
-    g_send, g_recv, swap_send, swap_recv, own_sem, load_sem, bg_send, bg_recv = refs[38:46]
-    pair_sems, kv_sems = refs[46:50], refs[50:54]
+class Home:
+    def __init__(self, home, c_count, c, e, rc, re, sems):
+        self.home, self.c_count, self.c, self.e, self.rc, self.re = home, c_count, c, e, rc, re
+        self.send, self.c_recv, self.e_recv, self.own_sem = sems
+        self.sec, self.shd = lax.axis_index("section"), lax.axis_index("shard")
+        self.half, self.low = self.shd // 8, lax.rem(self.shd, 8)
+        self.me, self.place = half_group(self.sec, self.shd)
+        self.here = self.sec == home
+
+    def copies(self, n):
+        if n < self.c_count:
+            size = 256 // self.c_count
+            src = self.c.at[pl.ds(size * n, size)]
+            dst = self.rc.at[pl.ds(256 * self.sec + size * n, size)]
+            return self.here, [(src, dst, (self.home, self.shd), self.send.at[n, 0], self.c_recv.at[n], self.own_sem.at[n, 0])]
+        k = n - self.c_count
+        return jnp.logical_and(self.here, self.low == k), [
+            (
+                self.e.at[pl.ds(128 * k, 128), pl.ds(256 * c, 256)],
+                self.re.at[:, columns(2 * (8 * c + self.low) + self.sec, 256)],
+                (self.home, 8 * self.half + k),
+                self.send.at[n, c],
+                self.e_recv.at[self.me, c],
+                self.own_sem.at[n, c],
+            )
+            for c in range(2)
+        ]
+
+    def go(self, n, start):
+        local, copies = self.copies(n)
+
+        @pl.when(local)
+        def _():
+            for src, dst, _, _, _, sem in copies:
+                one = pltpu.make_async_copy(src, dst, sem)
+                one.start() if start else one.wait()
+
+        @pl.when(jnp.logical_not(local))
+        def _():
+            for src, dst, there, send, recv, _ in copies:
+                one = remote(src, dst, send, recv, there)
+                one.start() if start else one.wait_send()
+
+    def finish(self):
+        for n in range(self.c_count + 8):
+            self.go(n, False)
+
+        @pl.when(self.here)
+        def _():
+            size = 256 // self.c_count
+            for n in range(self.c_count):
+                rows = pl.ds(size * n, size)
+                remote(
+                    self.c.at[rows], self.rc.at[rows], self.send.at[n, 0], self.c_recv.at[n], (1 - self.sec, self.shd)
+                ).wait_recv()
+
+            @pl.loop(1, 16)
+            def _(d):
+                n = lax.rem(self.me + d, 16)
+                for c in range(2):
+                    remote(
+                        self.e.at[pl.ds(0, 128), pl.ds(0, 256)],
+                        self.re.at[:, pl.ds(256 * c, 256)],
+                        self.send.at[self.c_count, c],
+                        self.e_recv.at[n, c],
+                        self.place(n),
+                    ).wait_recv()
+
+
+def attend_back_kernel(plan, home, *refs):
+    x_ref, n1_hbm, wq_hbm, wo_hbm, q_hbm, kv_hbm, mixed_hbm, lse_ref, lo_ref, gc, ge, cross = refs[:12]
+    if home == 0:
+        c_before, e_before = refs[12:14]
+        refs = refs[:12] + refs[14:]
+    o_ref, own_ref, far_ref, wo_ref, wq_ref, bq_ref, rc, re, crossed = refs[12:21]
+    if home == 0:
+        rc_before, re_before = refs[21:23]
+        refs = refs[:21] + refs[23:]
+    x_all, n1, wq, wo, q_all, kv_all, mixed, dq_all, dk, dv, part, came, buf = refs[21:34]
+    kv_parts, kv_bufs, sent = refs[34:36], refs[36:38], refs[38]
+    c_kept, c_came, e_kept, e_came = refs[39:43]
+    g_send, g_recv, swap_send, swap_recv, own_sem, load_sem, bg_send, bg_recv = refs[43:51]
+    pair_sems, kv_sems = refs[51:55], refs[55:59]
+    home_sems, (kept_sem, x_send, x_recv) = refs[59:63], refs[63:66]
+    deliver = home == 0
+    if deliver:
+        back_home = Home(home, 8, c_kept, e_kept, rc, re, home_sems)
+        before = Home(1, 8, c_before, e_before, rc_before, re_before, refs[66:])
     h, trio = Hyper(CUBE), Hyper(TRIO)
     sec, shd = lax.axis_index("section"), lax.axis_index("shard")
-    half = shd // 8
+    half, low = shd // 8, lax.rem(shd, 8)
     other = (sec, shd + 8 * (1 - 2 * half))
-    h.barrier((other,))
+    me, place = half_group(sec, shd)
+    barrier = pltpu.get_barrier_semaphore()
+
+    @pl.loop(1, 16)
+    def _(d):
+        pl.semaphore_signal(
+            barrier, inc=1, device_id=place(lax.rem(me + d, 16)), device_id_type=MESH
+        )
+
+    pl.semaphore_signal(barrier, inc=1, device_id=other, device_id_type=MESH)
+    pl.semaphore_wait(barrier, 16)
 
     def beside(n):
         if n < 8:
             rows = pl.ds(32 * n, 32)
-            src, dst = gc.at[1 - half, rows], rc.at[rows]
+            src, dst = gc.at[1 - half, rows], c_came.at[rows]
         else:
             rows = pl.ds(128 * (n - 8), 128)
-            src, dst = ge.at[1 - half, rows], re.at[rows]
+            src, dst = ge.at[1 - half, rows], e_came.at[rows]
         return remote(src, dst, bg_send.at[n], bg_recv.at[n], other)
 
-    pending = list(range(16))
+    def land(n):
+        beside(n).wait_recv()
+        mine, theirs, first, count = (c_kept, c_came, 32 * n, 2) if n < 8 else (e_kept, e_came, 128 * (n - 8), 8)
+
+        @pl.loop(0, count)
+        def _(i):
+            rows = pl.ds(pl.multiple_of(first + 16 * i, 16), 16)
+            total = mine[rows, :].astype(jnp.float32) + theirs[rows, :].astype(jnp.float32)
+            mine[rows, :] = total.astype(mine.dtype)
+
+        if deliver:
+            back_home.go(n, True)
+
+    LAG = 7 if home == 0 else 16
+    turns = []
+    for n in range(16 + LAG):
+        turn = []
+        if n < 16:
+            turn.append(beside(n).start)
+            if deliver:
+                turn.append(functools.partial(before.go, n, True))
+        if n >= LAG:
+            turn.append(functools.partial(land, n - LAG))
+        turns.append(turn)
 
     def feed(steps, every):
         for n, step in enumerate(steps):
             step()
-            if pending and n % every == 0:
-                beside(pending.pop(0)).start()
+            if turns and n % every == every - 1:
+                for one in turns.pop(0):
+                    one()
+
+    kept = [
+        pltpu.make_async_copy(gc.at[half], c_kept, kept_sem.at[0]),
+        pltpu.make_async_copy(ge.at[half], e_kept, kept_sem.at[1]),
+    ]
+    for one in kept:
+        one.start()
+    swap_rows = remote(cross, crossed, x_send, x_recv, (1 - sec, shd))
+
+    def swap_step(step, sending):
+        if home == 1:
+            step()
+        else:
+            pl.when(sec == (0 if sending else 1))(step)
 
     own = pltpu.make_async_copy(x_ref, x_all.at[h.pos], own_sem)
     own.start()
@@ -1593,25 +1641,20 @@
     for one in loads:
         one.start()
     own.wait()
-    for one in loads[:5]:
+    for one in loads[:5] + kept:
         one.wait()
     sums = PairSum(h, trio, plan, part, came, buf, pair_sems)
 
-    def project(o):
-        n = sums.pair(o)
-        g_all[n] = dot_nt(x_all[pl.ds(2 * n, 2)].reshape(QB, D), wo[...]).astype(jnp.bfloat16)
-
-    feed(pair_gather_steps(g, project), 3)
     bq_ref[...] = jnp.zeros_like(bq_ref)
+    dk[...] = jnp.zeros_like(dk)
+    dv[...] = jnp.zeros_like(dv)
 
     def compute(o):
         n = sums.pair(o)
         m, a = n // 4, pl.multiple_of(QB * lax.rem(n, 4), QB)
         keys = pl.ds(a, KB)
-        if o % 4 == 3:
-            dk[...] = jnp.zeros_like(dk)
-            dv[...] = jnp.zeros_like(dv)
-        q, gm, k = q_all[n], g_all[n], kv_all[m, keys, :HD]
+        q, k = q_all[n], kv_all[m, keys, :HD]
+        gm = dot_nt(x_all[pl.ds(2 * n, 2)].reshape(QB, D), wo[...]).astype(jnp.bfloat16)
         s = dot_nt(k, q) * SCALE
         probs = jnp.where(kept_pairs(lo_ref[n], a), jnp.exp(s - lse_ref[n]), 0.0)
         gp = dot_nt(kv_all[m, keys, HD:], gm)
@@ -1626,17 +1669,18 @@
                 dot_nt(dq, wq[rows, :]).astype(jnp.bfloat16).reshape(2, 128, 512)
             )
         sums.core_copy(o).start()
-        dk[keys] += dot32(gs, q) * SCALE
-        dv[keys] += dot32(probs.astype(jnp.bfloat16), gm)
-        if o % 4 == 0:
-            eight = pl.ds(8 * m, 8)
-            for one, first in zip(kv_parts, (WINDOW, 0)):
-                rows = pl.ds(first, WINDOW)
-                one[eight, :, :HD] = dk[rows].astype(jnp.bfloat16).reshape(8, 128, HD)
-                one[eight, :, HD:] = dv[rows].astype(jnp.bfloat16).reshape(8, 128, HD)
-
-    steps, rest = sums.schedule(compute, o_ref)
-    feed(steps, 3)
+        dk[m, keys] += dot32(gs, q) * SCALE
+        dv[m, keys] += dot32(probs.astype(jnp.bfloat16), gm)
+
+    step, last_add = sums.following(compute)
+    feed(pair_gather_steps(g, step), 2)
+    last_add()
+    swap_step(swap_rows.start, True)
+    for one, first in zip(kv_parts, (WINDOW, 0)):
+        rows = pl.ds(first, WINDOW)
+        one[:, :, :HD] = dk[:, rows].astype(jnp.bfloat16).reshape(16, 128, HD)
+        one[:, :, HD:] = dv[:, rows].astype(jnp.bfloat16).reshape(16, 128, HD)
+    rest = chunk_reduce_steps(sums.sums, o_ref)
     kv_sums = [
         Reduce(h, BESIDE[n], kv_parts[n], kv_bufs[n], kv_sems[2 * n], kv_sems[2 * n + 1]) for n in range(2)
     ]
@@ -1644,52 +1688,75 @@
         for r in kv_sums:
             r.copy(0, 3, n).start()
 
-    def product(out, left, right, c):
+    def product(left, right, c):
         cols = pl.ds(512 * c, 512)
-        out[:, cols] = dot_tn(left[...].reshape(D, HD), right[:, :, cols].reshape(D, 512)).astype(out.dtype)
-
-    products = [functools.partial(product, wo_ref, mixed, x_all, c) for c in range(4)]
-    products += [loads[5].wait] + [functools.partial(product, wq_ref, dq_all, n1, c) for c in range(4)]
+        tile = dot_tn(left[...].reshape(D, HD), right[:, :, cols].reshape(D, 512))
+        if right is x_all:
+            wo_ref[:, cols] = tile.astype(wo_ref.dtype)
+        else:
+            wq_ref[cols, :] = tile.T.astype(wq_ref.dtype)
+
+    products = [functools.partial(product, mixed, x_all, c) for c in range(4)]
+    products += [loads[5].wait] + [functools.partial(product, dq_all, n1, c) for c in range(4)]
     kv_steps = [
         step
         for pair in zip(chunk_reduce_steps(kv_sums[0], own_ref), chunk_reduce_steps(kv_sums[1], far_ref))
         for step in pair
     ]
     feed(spaced(spaced(rest, kv_steps), products), 3)
-    while pending:
-        beside(pending.pop(0)).start()
     sent[0] = far_ref[...].astype(sent.dtype)
     swap = remote(sent.at[0], sent.at[1], swap_send, swap_recv, other)
     swap.start()
+    while turns:
+        for one in turns.pop(0):
+            one()
     g.finish()
     sums.finish()
     for r in kv_sums:
         r.finish()
     swap.wait()
     far_ref[...] = sent[1].astype(jnp.float32)
+    swap_step(swap_rows.wait_send, True)
+    swap_step(swap_rows.wait_recv, False)
     for n in range(16):
-        beside(n).wait()
-
-
-def attend_back_layer(x, n1, wq, wo, q, kv, mixed, lse, lo, gc, ge, plan, collective_id):
+        beside(n).wait_send()
+    if deliver:
+        back_home.finish()
+        before.finish()
+    else:
+        summed = [
+            pltpu.make_async_copy(c_kept, rc, kept_sem.at[0]),
+            pltpu.make_async_copy(e_kept, re, kept_sem.at[1]),
+        ]
+        for one in summed:
+            one.start()
+        for one in summed:
+            one.wait()
+
+
+def attend_back_layer(x, n1, wq, wo, q, kv, mixed, lse, lo, gc, ge, cross, before, home, plan, collective_id):
     bf16, f32 = jnp.bfloat16, jnp.float32
     dma = pltpu.SemaphoreType.DMA
     hbm, vmem = pl.BlockSpec(memory_space=pl.ANY), pl.BlockSpec(memory_space=pltpu.VMEM)
     pair = pltpu.VMEM((16, 128, 2 * HD), bf16)
+    homes = [jax.ShapeDtypeStruct((512, D), bf16), jax.ShapeDtypeStruct((128, 8192), bf16)]
+    sums = [jax.ShapeDtypeStruct((256, D), bf16), jax.ShapeDtypeStruct((1024, 512), bf16)]
+    home_sems = [dma((16, 2)), dma((8,)), dma((16, 2)), dma((16, 2))]
     return pl.pallas_call(
-        functools.partial(attend_back_kernel, plan),
+        functools.partial(attend_back_kernel, plan, home),
         out_shape=[
             jax.ShapeDtypeStruct((128, D), f32),
             jax.ShapeDtypeStruct((128, 2 * HD), f32),
             jax.ShapeDtypeStruct((128, 2 * HD), f32),
             jax.ShapeDtypeStruct((HD, D), bf16),
-            jax.ShapeDtypeStruct((HD, D), bf16),
+            jax.ShapeDtypeStruct((D, HD), bf16),
             jax.ShapeDtypeStruct((1, HD), f32),
-            jax.ShapeDtypeStruct((256, D), bf16),
-            jax.ShapeDtypeStruct((1024, 512), bf16),
-        ],
-        in_specs=[hbm] * 7 + [vmem] * 2 + [hbm] * 2,
-        out_specs=[vmem] * 6 + [hbm] * 2,
+        ]
+        + (homes if home == 0 else sums)
+        + [jax.ShapeDtypeStruct((128, D), bf16)]
+        + (homes if home == 0 else []),
+        in_specs=[hbm] * 7 + [vmem] * 2 + [hbm] * (3 + len(before)),
+        out_specs=[vmem] * 6 + [hbm] * (3 + len(before)),
         scratch_shapes=[
             pltpu.VMEM((16, 128, D), bf16),
             pltpu.VMEM((16, 128, D), bf16),
@@ -1699,9 +1766,8 @@
             pltpu.VMEM((2, 2 * WINDOW, 2 * HD), bf16),
             pltpu.VMEM((8, QB, HD), bf16),
             pltpu.VMEM((8, QB, HD), bf16),
-            pltpu.VMEM((8, QB, HD), bf16),
-            pltpu.VMEM((2 * WINDOW, HD), f32),
-            pltpu.VMEM((2 * WINDOW, HD), f32),
+            pltpu.VMEM((2, 2 * WINDOW, HD), f32),
+            pltpu.VMEM((2, 2 * WINDOW, HD), f32),
             pltpu.VMEM((16, 128, D), bf16),
             pltpu.VMEM((8, 128, D), bf16),
             pltpu.VMEM((8, 128, D), bf16),
@@ -1710,6 +1776,10 @@
             pair,
             pair,
             pltpu.VMEM((2, 128, 2 * HD), bf16),
+            pltpu.VMEM((256, D), bf16),
+            pltpu.VMEM((256, D), bf16),
+            pltpu.VMEM((1024, 512), bf16),
+            pltpu.VMEM((1024, 512), bf16),
             dma((3, 16)),
             dma((3, 16)),
             dma,
@@ -1726,12 +1796,17 @@
             dma((1, 16)),
             dma((1, 16)),
             dma((1, 16)),
-        ],
+            *home_sems,
+            dma((2,)),
+            dma,
+            dma,
+        ]
+        + (home_sems if home == 0 else []),
         compiler_params=pltpu.CompilerParams(
             collective_id=collective_id, has_side_effects=True, vmem_limit_bytes=LIMIT
         ),
         name="attend_back",
-    )(x, n1, wq, wo, q, kv, mixed, lse, lo, gc, ge)
+    )(x, n1, wq, wo, q, kv, mixed, lse, lo, gc, ge, cross, *before)
 
 
 BESIDE = ((0, 128, 0, 256, (4, 2, "x", 1)),), ((0, 128, 0, 256, (2, "x", 4, 1)),)
@@ -1840,6 +1915,8 @@
         hidden = results[-1].astype(f32)
 
     grad = lax.dynamic_index_in_dim(cotangent, sec, 0, keepdims=False).astype(f32)
+    cross = jnp.where(sec == 0, results[1], results[0])
+    came = [None, None]
     input_grads = [None, None]
     weight_grads = [None, None]
     small_grads = [None, None]
@@ -1854,10 +1931,24 @@
         g_mid, d_gain_two, d_shift_two = back(g_n2)
         g_mid = grad + g_mid
         ga = g_mid.astype(bf16)
-        rows, kv_own, kv_far, d_wo, d_wq, d_bq, came_wc, came_we = attend_back_layer(
-            ga, all_n1, wq[s], wo[s], q, kv, mixed, lse, lo, d_wc, d_we, LIGHT, 5
+        rows, kv_own, kv_far, d_wo, d_wq, d_bq, d_wc, d_we, crossed, *before = attend_back_layer(
+            ga,
+            all_n1,
+            wq[s],
+            wo[s],
+            q,
+            kv,
+            mixed,
+            lse,
+            lo,
+            d_wc,
+            d_we,
+            cross,
+            () if s == 1 else weight_grads[1][2:],
+            s,
+            LIGHT,
+            5 + s,
         )
-        d_wc, d_we = with_other(d_wc, came_wc), with_other(d_we, came_we)
         dkv_rows = (kv_own + jnp.where(half == 0, kv_far, 0.0)).astype(bf16)
         g_n1 = rows + dot_nt(dkv_rows, wkv[s])
         _, back = jax.vjp(layer_norm, hidden, gain_one[s], shift_one[s])
@@ -1867,12 +1958,9 @@
         d_wkv = dot_tn(n1, dkv_rows)
         d_bq = d_bq[0]
         d_bv = jnp.sum(dkv_rows[:, HD:].astype(f32), axis=0)
-        weight_grads[s] = (
-            to_halves(d_wq.reshape(HD, 16, 128).transpose(1, 2, 0)).reshape(8, 128, HD),
-            d_we.reshape(8, 128, 512),
-            d_wo,
-            d_wc,
-        )
+        weight_grads[s] = (d_wq.reshape(16, 128, HD), d_wo, d_wc, d_we)
+        came[s] = crossed
+        cross = g_in.astype(bf16)
         spread = [
             d_gain_one,
             d_shift_one,
@@ -1892,41 +1980,40 @@
         )
         vec = jnp.pad(vec, ((0, 0), (0, 4096 - vec.shape[1]))).reshape(16, 16, 256)
         small_grads[s] = jnp.concatenate([d_wkv.reshape(16, 128, 256), vec], axis=1)
-        grad = g_in.astype(bf16).astype(f32)
-
-    mine = reduce(
-        [jnp.concatenate(small_grads, axis=0).astype(bf16)], ALL, [SMALL], 8, "reduce_shared"
-    )[0]
+        grad = cross.astype(f32)
+
+    mine, rq, ro, last_came = return_last(
+        jnp.concatenate(small_grads, axis=0).astype(bf16),
+        (weight_grads[0][0], weight_grads[1][0]),
+        (weight_grads[0][1], weight_grads[1][1]),
+        cross,
+    )
     vec = mine[128:].reshape(4096)
-    rq, re, ro, rc = return_grads(
-        *[jnp.stack([weight_grads[0][n], weight_grads[1][n]]) for n in range(4)]
-    )
 
     def both(r):
         return r[0].astype(f32) + r[1].astype(f32)
 
-    def swap(pair):
-        theirs = jnp.where(sec == 0, pair[1].astype(bf16), pair[0].astype(bf16))
-        own = jnp.where(sec == 0, pair[0], pair[1])
-        came = lax.ppermute(theirs, "section", [(0, 1), (1, 0)]).astype(own.dtype)
-        first = jnp.where(sec == 0, own, came)
-        second = jnp.where(sec == 0, came, own)
-        return jnp.stack([first, second])[None]
-
+    def here(pair):
+        return jnp.where(sec == 0, pair[0], pair[1])
+
+    def by_micro(own, theirs):
+        return jnp.stack([jnp.where(sec == 0, own, theirs), jnp.where(sec == 0, theirs, own)])[None]
+
+    grad_rows = here((last_came, came[0])).astype(f32)
     return (
-        swap(results),
-        swap(input_grads),
+        by_micro(here(results), came[1]),
+        by_micro(here(input_grads), grad_rows),
         vec[0:128][None],
         vec[128:256][None],
-        jnp.concatenate([rq.astype(f32), mine[:128]], axis=1)[None],
+        jnp.concatenate([both(rq), mine[:128]], axis=1)[None],
         vec[1280 : 1280 + 136][None],
         both(ro)[None],
         vec[512:640][None],
         vec[256:384][None],
         vec[384:512][None],
-        re.astype(f32)[None],
+        here((weight_grads[0][3], before[1])).astype(f32)[None],
         vec[768:1280][None],
-        rc.astype(f32)[None],
+        here((weight_grads[0][2], before[0])).astype(f32)[None],
         vec[640:768][None],
     )
 

time: 1080 us -> 1030 us (0.954)
  waiting for transfers between devices: 23.4 us -> 1.07 us
  other arithmetic: 60.2 us -> 46.2 us
    ppermute x2 -> x0, waiting for transfers between devices: 15 us -> none  [swap(): came = lax.ppermute(theirs, 'section', [(0, 1), (1, 0)]).astype(own.dtype)]
    pallas_call x4 -> x3, Pallas kernels: 329 us -> 332 us  [the longest x2 270 us: attend_back_layer(): pl.pallas_call(functools.partial(attend_back_kernel, plan, home), out_sha...]
  transfers between devices with their start and end apart: 8 -> 4, of which waited for: 2 -> 0; matrix products, arithmetic and copies ran while one was open for 4% -> 3% of each run, Pallas kernels for 27% -> 28%
where the time goes in v4:
time: 1030 us
  Pallas kernels  925 us (90%)
  other arithmetic  46.2 us (4%)
  local copies, waits for them, and re-layouts  30 us (3%)
  between operations  15 us (1%)
    pallas_call x4, Pallas kernels, hidden_layer(): pl.pallas_call(functools.partial(hidden_kernel, back, plan), out_shape=ou...  312 us
    pallas_call x2, Pallas kernels, attend_back_layer(): pl.pallas_call(functools.partial(attend_back_kernel, plan, home), out_sha...  270 us
    pallas_call x2, Pallas kernels, attend_layer(): pl.pallas_call(functools.partial(attend_kernel, plan), out_shape=out, in_...  192 us
    pallas_call x1, Pallas kernels, fetch_weights(): pl.pallas_call(fetch_kernel, out_shape=(jax.ShapeDtypeStruct((32,) + bloc...  90 us
    pallas_call x1, Pallas kernels, return_last(): pl.pallas_call(last_kernel, out_shape=(jax.ShapeDtypeStruct(small.shape[1...  61.5 us
  transfers between devices with their start and end apart: 4, of which 0 were waited for; matrix products, arithmetic and copies ran while one was open for 3% of the time, Pallas kernels for 28%

profile of v4, /device:TPU:0, one launch (start us, length us, event | category | flops | bytes accessed | tf_op | source)
XLA Modules:
  0.0 1026.3 jit_solution(11652079874360222754)
XLA Ops:
  9.5 4.1 concatenate.43
  14.2 90.0 %fetch_weights.1 = (bf16[32,144,256]{2,1,0:T(8,128)(2,1)}, bf16[2,16,128,128]{3,2,1,0:T(8,128)(2,1)}, bf16[2,128,2048]{2,1,0:T(8,128)(2,1)}, bf16[2,8,128,512]{3,2,1,0:T(8,128)(2,1)}, bf16[2,256,2048]{2,1,0:T(8,128)(2,1)}) custom-call(bf16[144,256]{1,0:T(8,128)(2,1)} %pad_maximum_fusion.block, bf16[128,2304]{1,0:T(8,128)(2,1)} %bitcast.227, ...), custom_call_target="tpu_custom_call" | custom-call | tf_op jit(solution)/shard_map/fetch_weights/pallas_call | solution.py:783
  104.2 3.2 fusion.68
  107.5 1.5 fusion.67
  111.4 3.0 fusion.66
  117.3 2.1 convert_reduce_fusion
  119.5 2.4 fusion.69
  124.5 108.1 %attend.2 = (f32[128,2048]{1,0:T(8,128)}, bf16[16,128,2048]{2,1,0:T(8,128)(2,1)}, bf16[8,256,128]{2,1,0:T(8,128)(2,1)}, bf16[2,2048,256]{2,1,0:T(8,128)(2,1)}, b...) custom-call(bf16[128,2048]{1,0:T(8,128)(2,1)} %fusion.20.refs_0_, bf16[128,256]{1,0:T(8,128)(2,1)} %fusion.14.refs_1_, ...), custom_call_target="tpu_custom_call" | custom-call | tf_op jit(solution)/shard_map/attend/pallas_call | solution.py:1437
  232.7 1.6 fusion.64
  238.2 97.3 %hidden.2 = (f32[128,2048]{1,0:T(8,128)}, bf16[2,16,64,2048]{3,2,1,0:T(8,128)(2,1)}, bf16[2,16,64,512]{3,2,1,0:T(8,128)(2,1)}, bf16[2,16,64,512]{3,2,1,0:T(8,128)(2,1)}) custom-call(bf16[128,2048]{1,0:T(8,128)(2,1)} %add_convert_fusion.3.refs_0_, bf16[2048,512]{1,0:T(8,128)(2,1)} %all-gather.7.cloned.1.call-done.refs_1_, bf16[512,2048]{1,0:T(8,128)(2,1)} %bitcast.206, ...), custom_call_target="tpu_custom_call" | custom-call | tf_op jit(solution)/shard_map/hidden/pallas_call | solution.py:1191
  335.5 1.5 convert_reduce_fusion.1
  338.7 83.6 %attend.3 = (f32[128,2048]{1,0:T(8,128)}, bf16[16,128,2048]{2,1,0:T(8,128)(2,1)}, bf16[8,256,128]{2,1,0:T(8,128)(2,1)}, bf16[2,2048,256]{2,1,0:T(8,128)(2,1)}, b...) custom-call(bf16[128,2048]{1,0:T(8,128)(2,1)} %copy-done.12, bf16[128,256]{1,0:T(8,128)(2,1)} %fusion.15.refs_1_, ...), custom_call_target="tpu_custom_call" | custom-call | tf_op jit(solution)/shard_map/attend/pallas_call | solution.py:1437
  422.3 1.5 fusion.62
  425.1 69.1 %hidden.3 = (f32[128,2048]{1,0:T(8,128)}, bf16[2,16,64,2048]{3,2,1,0:T(8,128)(2,1)}, bf16[2,16,64,512]{3,2,1,0:T(8,128)(2,1)}, bf16[2,16,64,512]{3,2,1,0:T(8,128)(2,1)}) custom-call(bf16[128,2048]{1,0:T(8,128)(2,1)} %add_convert_fusion.1.refs_0_, bf16[2048,512]{1,0:T(8,128)(2,1)} %all-gather.9.cloned.1.call-done.refs_1_, bf16[512,2048]{1,0:T(8,128)(2,1)} %bitcast.208, ...), custom_call_target="tpu_custom_call" | custom-call | tf_op jit(solution)/shard_map/hidden/pallas_call | solution.py:1191
  494.2 72.2 %hidden_back.2 = (f32[128,2048]{1,0:T(8,128)}, bf16[512,2048]{1,0:T(8,128)(2,1)}, bf16[2048,512]{1,0:T(8,128)(2,1)}, f32[1,512]{1,0:T(1,128)}) custom-call(bf16[128,2048]{1,0:T(8,128)(2,1)} %get-tuple-element.174.refs_0_, bf16[2048,512]{1,0:T(8,128)(2,1)} %all-gather.9.cloned.1.call-done.refs_1_, bf16[512,2048]{1,0:T(8,128)(2,1)} %bitcast.209, ...), custom_call_target="tpu_custom_call" | custom-call | tf_op jit(solution)/shard_map/hidden_back/pallas_call | solution.py:1191
  566.4 1.7 multiply_reduce_fusion
  571.7 122.7 %attend_back.2 = (f32[128,2048]{1,0:T(8,128)}, f32[128,256]{1,0:T(8,128)}, f32[128,256]{1,0:T(8,128)}, bf16[128,2048]{1,0:T(8,128)(2,1)}, bf16[2048,128]{1,0:T(8...) custom-call(bf16[128,2048]{1,0:T(8,128)(2,1)} %get-tuple-element.150, ...), custom_call_target="tpu_custom_call" | custom-call | tf_op jit(solution)/shard_map/attend_back/pallas_call | solution.py:1745
  695.5 1.4 convolution_convert_fusion
  696.9 1.9 fusion.53
  699.4 2.1 fusion.55
  701.6 73.0 %hidden_back.3 = (f32[128,2048]{1,0:T(8,128)}, bf16[512,2048]{1,0:T(8,128)(2,1)}, bf16[2048,512]{1,0:T(8,128)(2,1)}, f32[1,512]{1,0:T(1,128)}) custom-call(bf16[128,2048]{1,0:T(8,128)(2,1)} %get-tuple-element.145.refs_0_.refs_11_, bf16[2048,512]{1,0:T(8,128)(2,1)} %all-gather.7.cloned.1.call-done.refs_1_, bf16[512,2048]{1,0:T(8,128)(2,1)} %bitcast.207, ...), custom_call_target="tpu_custom_call" | custom-call | tf_op jit(solution)/shard_map/hidden_back/pallas_call | solution.py:1191
  774.6 1.7 multiply_reduce_fusion.1
  778.4 147.7 %attend_back.3 = (f32[128,2048]{1,0:T(8,128)}, f32[128,256]{1,0:T(8,128)}, f32[128,256]{1,0:T(8,128)}, bf16[128,2048]{1,0:T(8,128)(2,1)}, bf16[2048,128]{1,0:T(8...) custom-call(bf16[128,2048]{1,0:T(8,128)(2,1)} %get-tuple-element.148, ...), custom_call_target="tpu_custom_call" | custom-call | tf_op jit(solution)/shard_map/attend_back/pallas_call | solution.py:1745
  930.1 1.8 fusion.52
  934.5 3.0 fusion.54
  937.5 1.6 maximum_maximum_fusion.small
  939.1 61.5 %return_last.1 = (f32[144,256]{1,0:T(8,128)}, bf16[2,128,2048]{2,1,0:T(8,128)(2,1)}, bf16[2,128,2048]{2,1,0:T(8,128)(2,1)}, bf16[128,2048]{1,0:T(8,128)(2,1)}) custom-call(bf16[32,144,256]{2,1,0:T(8,128)(2,1)} %maximum_maximum_fusion.small, bf16[16,128,128]{2,1,0:T(8,128)(2,1)} %bitcast.229, bf16[16,128,128]{2,1,0:T(8,128)(2,1)} %bitcast.228, ...), custom_call_target="tpu_custom_call" | custom-call | tf_op jit(solution)/shard_map/return_last/pallas_call | solution.py:897
  1004.0 1.5 add_bitcast_fusion
  1005.5 2.4 convert_add_fusion.1
  1008.5 2.4 bitcast_convert_fusion
  1012.2 2.3 bitcast_convert_fusion.1
  1016.9 1.5 maximum_bitcast_fusion
  (214 shorter events, 40.1 us)
Async XLA Ops:
  7.2 231.0 %all-gather.7.cloned.1.call-start = ((), (), s32[]{:S(2)}) async-start(), calls=%async_computation | async-start | bytes 3145728 | tf_op jit(solution)/shard_map/all_gather | solution.py:930
  104.2 3.3 copy-start.21
  107.4 130.8 %all-gather.11.cloned.1.call-start = ((), (), s32[]{:S(2)}) async-start(), calls=%async_computation.2 | async-start | bytes 3145728 | tf_op jit(solution)/shard_map/all_gather | solution.py:930
  109.0 316.1 %all-gather.9.cloned.1.call-start = ((), (), s32[]{:S(2)}) async-start(), calls=%async_computation.1 | async-start | bytes 3145728 | tf_op jit(solution)/shard_map/all_gather | solution.py:930
  109.7 315.4 %all-gather.13.cloned.1.call-start = ((), (), s32[]{:S(2)}) async-start(), calls=%async_computation.3 | async-start | bytes 3145728 | tf_op jit(solution)/shard_map/all_gather | solution.py:930
  111.4 3.0 copy-start
  114.4 8.5 copy-start.9
  114.4 2.9 copy-start.36
  116.8 6.1 copy-start.35
  116.8 221.0 %copy-start.34 = (f32[1,256]{1,0:T(1,128)}, f32[1,256]{1,0:T(1,128)S(1)}, u32[]{:S(2)}) copy-start(f32[1,256]{1,0:T(1,128)S(1)} %get-tuple-element.217.refs_6_) | copy-start | bytes 3076
  119.4 2.4 copy-start.28
  335.5 2.3 copy-start.2
  568.2 2.4 copy-start.29
  571.7 123.8 %copy-start.13 = (bf16[128,2048]{1,0:T(8,128)(2,1)S(1)}, bf16[128,2048]{1,0:T(8,128)(2,1)}, u32[]{:S(2)}) copy-start(bf16[128,2048]{1,0:T(8,128)(2,1)} %copy-done.12) | copy-start | bytes 1572868
  694.4 2.6 copy-start.3
  696.9 2.5 copy-start.8
  696.9 2.5 copy-start.30
  778.4 148.9 %copy-start.20 = (bf16[2048,128]{1,0:T(8,128)(2,1)S(1)}, bf16[2048,128]{1,0:T(8,128)(2,1)}, u32[]{:S(2)}) copy-start(bf16[2048,128]{1,0:T(8,128)(2,1)} %copy.31) | copy-start | bytes 1572868
  778.4 151.1 %copy-start.38 = (f32[1,512]{1,0:T(1,128)S(1)}, f32[1,512]{1,0:T(1,128)}, u32[]{:S(2)}) copy-start(f32[1,512]{1,0:T(1,128)} %get-tuple-element.111) | copy-start | bytes 6148
  926.1 3.9 copy-start.1
  926.1 3.9 copy-start.10
  930.0 3.5 copy-start.39
  930.0 3.7 copy-start.37
  931.9 2.6 copy-start.5
  934.5 3.1 copy-start.15
  934.5 3.1 copy-start.16
  1004.0 4.5 copy-start.26
  1004.0 4.5 copy-start.27
  1008.5 2.4 copy-start.24
  1008.5 3.7 copy-start.25
  1012.2 3.4 copy-start.31
  1012.2 3.4 copy-start.32
  (12 other events, 17.5 us)
Sparse Core Ops, SparseCore 0:
  107.5 58.4 all-gather.6
  168.2 55.5 all-gather.10
  225.9 55.5 all-gather.8
  283.5 55.5 all-gather.12

commit v5 on v4

--- a/solution.py
+++ b/solution.py
@@ -610,29 +610,11 @@
     return 8 * sec + lax.rem(shd, 8), lambda n: (n // 8, first + lax.rem(n, 8))
 
 
-def half_barrier(me, place, sec, shd):
-    sem = pltpu.get_barrier_semaphore()
-
-    @pl.loop(1, 16)
-    def _(d):
-        pl.semaphore_signal(
-            sem, inc=1, device_id=place(lax.rem(me + d, 16)), device_id_type=MESH
-        )
-
-    across = shd + 8 * (1 - 2 * (shd // 8))
-    for s in range(2):
-        pl.semaphore_signal(sem, inc=1, device_id=(s, across), device_id_type=MESH)
-    pl.semaphore_wait(sem, 17)
-
-
 class Spread:
     def __init__(self, pieces, own_sem, send, recv):
         self.sec, self.shd = lax.axis_index("section"), lax.axis_index("shard")
         self.me, self.place = half_group(self.sec, self.shd)
         self.pieces, self.own_sem, self.send, self.recv = pieces, own_sem, send, recv
-
-    def barrier(self):
-        half_barrier(self.me, self.place, self.sec, self.shd)
 
     def copies(self, d):
         there = self.place(lax.rem(self.me + d, 16))
@@ -656,20 +638,6 @@
         for one in self.own():
             one.start()
 
-    def wait(self):
-        @pl.loop(1, 16)
-        def _(d):
-            for one in self.copies(d):
-                one.wait_recv()
-
-        @pl.loop(1, 16)
-        def _(d):
-            for one in self.copies(d):
-                one.wait_send()
-
-        for one in self.own():
-            one.wait()
-
 
 def everyone_barrier(me):
     sem = pltpu.get_barrier_semaphore()
@@ -684,15 +652,32 @@
     pl.semaphore_wait(sem, 31)
 
 
-def fetch_kernel(block, mix, out, exp, con, shared, wq, wo, we, wc, *sems):
-    q_send, q_recv, send, recv, con_send, con_recv, out_send, out_recv, own_sem, sh_send, sh_recv = sems
+def fetch_kernel(small, mix, out, exp, con, wkv, vec, wq, wo, we_0, we_1, wc_0, wc_1, *sems):
+    q_send, q_recv, send, recv, con_send, con_recv, out_send, out_recv, own_sem = sems[:9]
+    kv_send, kv_recv, v_send, v_recv = sems[9:]
     sec, shd = lax.axis_index("section"), lax.axis_index("shard")
     low, half = lax.rem(shd, 8), shd // 8
     me = 16 * sec + shd
     everyone_barrier(me)
     h = Hyper(ALL)
-    g = Gather(h, SMALL, block, shared, sh_send, sh_recv)
-    g.start(range(3))
+    mix_kv = mix.at[:, pl.ds(D, 2 * HD)]
+    gathers = [Gather(h, ALL_KV, mix_kv, wkv, kv_send, kv_recv), Gather(h, ALL_SMALL, small, vec, v_send, v_recv)]
+    for g in gathers:
+        g.start(range(len(g.parts)))
+
+    def spread_to(we):
+        def pieces(ts, tj):
+            for n in range(2):
+                yield (
+                    exp.at[:, columns(2 * (8 * n + lax.rem(tj, 8)) + ts, 256)],
+                    we.at[low, :, pl.ds(256 * n, 256)],
+                )
+
+        return Spread(pieces, own_sem, send, recv)
+
+    def to_section(step):
+        for s, arrays in enumerate(((spread_to(we_0), wc_0), (spread_to(we_1), wc_1))):
+            pl.when(sec == s)(functools.partial(step, *arrays))
 
     def query(d):
         there = lax.rem(me + d, 32)
@@ -705,9 +690,11 @@
     def _(d):
         query(d).start()
 
+    to_section(lambda spread, wc: spread.start())
+
     to_x = lax.rem(half + lax.rem(shd, 2), 2)
     from_half = lax.rem(sec + lax.rem(shd, 2), 2)
-    own_out = pltpu.make_async_copy(out, wo.at[sec], own_sem.at[5])
+    own_out = pltpu.make_async_copy(out, wo.at[sec], own_sem.at[6])
     for z in range(2):
         mine = jnp.logical_and(to_x == sec, half == z)
         there = remote(out, wo.at[sec], out_send.at[z], out_recv.at[sec], (to_x, 8 * z + low))
@@ -721,25 +708,31 @@
             there.start()
 
     own = [
-        pltpu.make_async_copy(block, shared.at[h.pos], own_sem.at[2]),
-        pltpu.make_async_copy(mix.at[:, columns(block_of(sec, shd), HD)], wq.at[sec, shd], own_sem.at[3]),
-        pltpu.make_async_copy(con.at[pl.ds(256 * sec, 256)], wc.at[sec], own_sem.at[4]),
+        pltpu.make_async_copy(mix_kv, wkv.at[h.pos], own_sem.at[2]),
+        pltpu.make_async_copy(small, vec.at[h.pos], own_sem.at[3]),
+        pltpu.make_async_copy(mix.at[:, columns(block_of(sec, shd), HD)], wq.at[sec, shd], own_sem.at[4]),
     ]
     for one in own:
         one.start()
 
-    def pieces(ts, tj):
-        for n in range(2):
-            yield (
-                exp.at[:, columns(2 * (8 * n + lax.rem(tj, 8)) + ts, 256)],
-                we.at[sec, low, :, pl.ds(256 * n, 256)],
-            )
-
-    spread = Spread(pieces, own_sem, send, recv)
-    spread.start()
-    rows = remote(con.at[pl.ds(256 * (1 - sec), 256)], wc.at[sec], con_send, con_recv, (1 - sec, shd))
-    rows.start()
-    g.forward(range(3))
+    def own_rows(wc):
+        return pltpu.make_async_copy(con.at[pl.ds(256 * sec, 256)], wc, own_sem.at[5])
+
+    def rows(wc):
+        return remote(con.at[pl.ds(256 * (1 - sec), 256)], wc, con_send, con_recv, (1 - sec, shd))
+
+    def start_rows(spread, wc):
+        own_rows(wc).start()
+        rows(wc).start()
+
+    to_section(start_rows)
+    for j in range(len(ALL)):
+        for n in range(1 << j):
+            for g in gathers:
+                for p in range(len(g.parts)):
+                    g.copy(p, n, j).wait_recv()
+                    for later in range(j + 1, len(ALL)):
+                        g.copy(p, n | 1 << j, later).start()
 
     @pl.loop(1, 32)
     def _(d):
@@ -752,9 +745,29 @@
         def _():
             remote(out, wo.at[s], out_send.at[0], out_recv.at[s], (1 - sec, shd)).wait_recv()
 
-    spread.wait()
-    remote(con.at[pl.ds(0, 256)], wc.at[1 - sec], con_send, con_recv, (1 - sec, shd)).wait_recv()
-    rows.wait_send()
+    for s, wc in enumerate((wc_0, wc_1)):
+        pl.when(sec != s)(rows(wc).wait_recv)
+
+    @pl.loop(1, 16)
+    def _(d):
+        for n in range(2):
+            some = pl.ds(256 * n, 256)
+            remote(
+                exp.at[:, some], we_0.at[0, :, some], send.at[n, d], recv.at[n, d], (1 - sec, shd)
+            ).wait_recv()
+
+    def sent(spread, wc):
+        @pl.loop(1, 16)
+        def _(d):
+            for one in spread.copies(d):
+                one.wait_send()
+
+        for one in spread.own():
+            one.wait()
+        own_rows(wc).wait()
+        rows(wc).wait_send()
+
+    to_section(sent)
 
     @pl.loop(1, 32)
     def _(d):
@@ -772,25 +785,29 @@
         def _():
             there.wait_send()
 
-    g.finish()
+    for g in gathers:
+        g.finish()
     for one in own:
         one.wait()
 
 
-def fetch_weights(block, mix, out, exp, con):
+def fetch_weights(small, mix, out, exp, con):
     bf16 = jnp.bfloat16
     dma = pltpu.SemaphoreType.DMA
     return pl.pallas_call(
         fetch_kernel,
         out_shape=(
-            jax.ShapeDtypeStruct((32,) + block.shape, bf16),
+            jax.ShapeDtypeStruct((32, 128, 2 * HD), bf16),
+            jax.ShapeDtypeStruct((32,) + small.shape, bf16),
             jax.ShapeDtypeStruct((2, 16, 128, HD), bf16),
             jax.ShapeDtypeStruct((2, 128, D), bf16),
-            jax.ShapeDtypeStruct((2, 8, 128, 512), bf16),
-            jax.ShapeDtypeStruct((2, 256, D), bf16),
+            jax.ShapeDtypeStruct((8, 128, 512), bf16),
+            jax.ShapeDtypeStruct((8, 128, 512), bf16),
+            jax.ShapeDtypeStruct((256, D), bf16),
+            jax.ShapeDtypeStruct((256, D), bf16),
         ),
         in_specs=[pl.BlockSpec(memory_space=pl.ANY)] * 5,
-        out_specs=[pl.BlockSpec(memory_space=pl.ANY)] * 5,
+        out_specs=[pl.BlockSpec(memory_space=pl.ANY)] * 8,
         scratch_shapes=[
             dma((32,)),
             dma((32,)),
@@ -800,15 +817,17 @@
             dma,
             dma((2,)),
             dma((2,)),
-            dma((6,)),
+            dma((7,)),
             dma((3, 32)),
             dma((3, 32)),
+            dma((1, 32)),
+            dma((1, 32)),
         ],
         compiler_params=pltpu.CompilerParams(
             collective_id=1, has_side_effects=True, vmem_limit_bytes=LIMIT
         ),
         name="fetch_weights",
-    )(block, mix, out, exp, con)
+    )(small, mix, out, exp, con)
 
 
 def last_kernel(small, gq0, gq1, go0, go1, cross, total, rq, ro, crossed, *scratch):
@@ -1335,7 +1354,7 @@
     return steps
 
 
-def attend_kernel(plan, *refs):
+def attend_kernel(plan, section, *refs):
     ins, refs = refs[:8], refs[8:]
     x_ref, kv_ref, wq_hbm, wkv_hbm, wo_hbm, bq_ref, bkv_ref, lo_ref = ins
     o_ref, x_out, q_out, kv_out, mixed_out, lse_ref = refs[:6]
@@ -1351,9 +1370,9 @@
     swap.start()
     loads = [
         pltpu.make_async_copy(x_ref, x_all.at[h.pos], own_sem),
-        pltpu.make_async_copy(wq_hbm, wq, load_sem.at[0]),
-        pltpu.make_async_copy(wkv_hbm, wkv, load_sem.at[1]),
-        pltpu.make_async_copy(wo_hbm, wo, load_sem.at[2]),
+        pltpu.make_async_copy(wq_hbm.at[section], wq, load_sem.at[0]),
+        pltpu.make_async_copy(wkv_hbm.at[section], wkv, load_sem.at[1]),
+        pltpu.make_async_copy(wo_hbm.at[section], wo, load_sem.at[2]),
     ]
     for one in loads:
         one.start()
@@ -1421,7 +1440,7 @@
         one.wait()
 
 
-def attend_layer(x, kv, wq, wkv, wo, bq, bkv, lo, plan, collective_id):
+def attend_layer(x, kv, wq, wkv, wo, bq, bkv, lo, plan, section):
     bf16, f32 = jnp.bfloat16, jnp.float32
     dma = pltpu.SemaphoreType.DMA
     hbm, vmem = pl.BlockSpec(memory_space=pl.ANY), pl.BlockSpec(memory_space=pltpu.VMEM)
@@ -1435,7 +1454,7 @@
     ]
     out_specs = [vmem, hbm, hbm, hbm, hbm, vmem]
     return pl.pallas_call(
-        functools.partial(attend_kernel, plan),
+        functools.partial(attend_kernel, plan, section),
         out_shape=out,
         in_specs=[hbm] * 5 + [vmem] * 3,
         out_specs=out_specs,
@@ -1467,7 +1486,7 @@
             dma((3, 8)),
         ],
         compiler_params=pltpu.CompilerParams(
-            collective_id=collective_id, has_side_effects=True, vmem_limit_bytes=LIMIT
+            collective_id=3 + section, has_side_effects=True, vmem_limit_bytes=LIMIT
         ),
         name="attend",
     )(x, kv, wq, wkv, wo, bq, bkv, lo)
@@ -1599,7 +1618,7 @@
         if deliver:
             back_home.go(n, True)
 
-    LAG = 7 if home == 0 else 16
+    LAG = 7 if home == 0 else 12
     turns = []
     for n in range(16 + LAG):
         turn = []
@@ -1636,7 +1655,7 @@
     own.start()
     g = Gather(h, plan, x_ref, x_all, g_send, g_recv)
     g.start(range(len(plan)))
-    pairs = ((wq_hbm, wq), (wo_hbm, wo), (q_hbm, q_all), (kv_hbm, kv_all), (mixed_hbm, mixed), (n1_hbm, n1))
+    pairs = ((wq_hbm.at[home], wq), (wo_hbm.at[home], wo), (q_hbm, q_all), (kv_hbm, kv_all), (mixed_hbm, mixed), (n1_hbm, n1))
     loads = [pltpu.make_async_copy(src, dst, load_sem.at[n]) for n, (src, dst) in enumerate(pairs)]
     for one in loads:
         one.start()
@@ -1814,6 +1833,10 @@
     (48 * n, 48, 0, 256, order)
     for n, order in enumerate(((8, "x", 4, 2, 1), (8, 4, 2, "x", 1), (8, 2, "x", 4, 1)))
 )
+ALL_KV = tuple(
+    (first, count, 0, 2 * HD, part[4]) for (first, count), part in zip(((0, 48), (48, 48), (96, 32)), SMALL)
+)
+ALL_SMALL = ((0, 16, 0, 128, SMALL[0][4]),)
 BIAS = D + HD
 
 
@@ -1841,43 +1864,40 @@
 
     small = jnp.concatenate(
         [
-            first_gain[0],
-            first_shift[0],
-            second_gain[0],
-            second_shift[0],
-            output_bias[0],
-            contract_bias[0],
-            expand_bias[0],
-            mixer_bias[0],
-        ]
-    )
-    small = jnp.concatenate([small, jnp.zeros((16 * 256 - small.shape[0],), bf16)]).reshape(16, 256)
-    shared, wq, wo, we, wc = fetch_weights(
-        jnp.concatenate([mixer_weight[0][:, D:], small], axis=0),
-        mixer_weight[0],
-        output_weight[0],
-        expand_weight[0],
-        contract_weight[0],
-    )
-    we = [we[s].reshape(8 * 128, 512) for s in range(2)]
-    for s in range(2):
-        we[s] = from_halves(we[s])
-    wc = [from_halves(wc[s]) for s in range(2)]
+            one[0].reshape(-1, 128)
+            for one in (
+                first_gain,
+                first_shift,
+                second_gain,
+                second_shift,
+                output_bias,
+                contract_bias,
+                expand_bias,
+                jnp.pad(mixer_bias, ((0, 0), (0, 256 - mixer_bias.shape[1]))),
+            )
+        ],
+        axis=0,
+    )
+    small = jnp.pad(small, ((0, 16 - small.shape[0]), (0, 0)))
+    wkv, vectors, wq, wo, *halves = fetch_weights(
+        small, mixer_weight[0], output_weight[0], expand_weight[0], contract_weight[0]
+    )
+    we = [from_halves(halves[s].reshape(8 * 128, 512)) for s in range(2)]
+    wc = [from_halves(halves[2 + s]) for s in range(2)]
     wq = wq.reshape(2, D, HD)
-    shared = shared.reshape(2, 16, 144, 256)
-    wkv = shared[:, :, :128].reshape(2, D, 256)
-    vectors = shared[:, :, 128:].reshape(2, 16, 4096)
+    wkv = wkv.reshape(2, D, 2 * HD)
+    vectors = vectors.reshape(2, 16, 16, 128)
 
     def vector(n):
-        return vectors[:, :, 128 * n : 128 * (n + 1)].reshape(2, D).astype(f32)
+        return vectors[:, :, n].reshape(2, D).astype(f32)
 
     gain_one, shift_one, gain_two, shift_two, bias_out, bias_con = [vector(n) for n in range(6)]
-    bias_exp = vectors[:, :, 768:1280].reshape(2, 8192).astype(f32)
+    bias_exp = vectors[:, :, 6:10].reshape(2, 8192).astype(f32)
     hidden_units = [512 * (8 * h + lax.rem(shd, 8)) + 256 * sec for h in range(2)]
     bias_exp = jnp.concatenate(
         [lax.dynamic_slice_in_dim(bias_exp, first, 256, 1) for first in hidden_units], axis=1
     )
-    bias_mix = vectors[:, :, 1280 : 1280 + 136].reshape(2, BIAS).astype(f32)
+    bias_mix = vectors[:, :, 10:12].reshape(2, 16, 256)[:, :, :136].reshape(2, BIAS).astype(f32)
     bias_q = lax.dynamic_slice_in_dim(bias_mix, f * HD, HD, 1)
     bias_kv = jnp.concatenate([jnp.zeros((2, HD), f32), bias_mix[:, D:]], axis=1)
 
@@ -1897,14 +1917,14 @@
         rows, all_n1, q, kv, mixed, lse = attend_layer(
             n1,
             kv_rows,
-            wq[s],
-            wkv[s],
-            wo[s],
+            wq,
+            wkv,
+            wo,
             bias_q[s][None],
             bias_kv[s][None],
             lo,
             LIGHT if s == 0 else EVEN,
-            3 + s,
+            s,
         )
         middle = hidden + rows + bias_out[s]
         n2 = layer_norm(middle, gain_two[s], shift_two[s]).astype(bf16)
@@ -1934,8 +1954,8 @@
         rows, kv_own, kv_far, d_wo, d_wq, d_bq, d_wc, d_we, crossed, *before = attend_back_layer(
             ga,
             all_n1,
-            wq[s],
-            wo[s],
+            wq,
+            wo,
             q,
             kv,
             mixed,

time: 1030 us -> 1020 us (level)
  local copies, waits for them, and re-layouts: 30 us -> 16.6 us
  transfers between devices with their start and end apart: 4 -> 4, of which waited for: 0 -> 0; matrix products, arithmetic and copies ran while one was open for 3% -> 2% of each run, Pallas kernels for 28% -> 28%
where the time goes in v5:
time: 1020 us; the launch traced here: 1010 us
  Pallas kernels  923 us (90%)
  other arithmetic  47.1 us (5%)
  local copies, waits for them, and re-layouts  16.6 us (2%)
  between operations  14.9 us (1%)
    pallas_call x4, Pallas kernels, hidden_layer(): pl.pallas_call(functools.partial(hidden_kernel, back, plan), out_shape=ou...  312 us
    pallas_call x2, Pallas kernels, attend_back_layer(): pl.pallas_call(functools.partial(attend_back_kernel, plan, home), out_sha...  268 us
    pallas_call x2, Pallas kernels, attend_layer(): pl.pallas_call(functools.partial(attend_kernel, plan, section), out_shape...  188 us
    pallas_call x1, Pallas kernels, fetch_weights(): pl.pallas_call(fetch_kernel, out_shape=(jax.ShapeDtypeStruct((32, 128, 2...  91.9 us
    pallas_call x1, Pallas kernels, return_last(): pl.pallas_call(last_kernel, out_shape=(jax.ShapeDtypeStruct(small.shape[1...  62.7 us
  transfers between devices with their start and end apart: 4, of which 0 were waited for; matrix products, arithmetic and copies ran while one was open for 2% of the time, Pallas kernels for 28%

profile of v5, /device:TPU:0, one launch (start us, length us, event | category | flops | bytes accessed | tf_op | source)
XLA Modules:
  0.0 1013.5 jit_solution(10806733112646275894)
XLA Ops:
  10.1 91.9 %fetch_weights.1 = (bf16[32,128,256]{2,1,0:T(8,128)(2,1)}, bf16[32,16,128]{2,1,0:T(8,128)(2,1)}, bf16[2,16,128,128]{3,2,1,0:T(8,128)(2,1)}, bf16[2,128,2048]{2,1...) custom-call(bf16[16,128]{1,0:T(8,128)(2,1)} %pad.19.small, ...), custom_call_target="tpu_custom_call" | custom-call | tf_op jit(solution)/shard_map/fetch_weights/pallas_call | solution.py:797
  107.4 1.5 fusion.66
  109.4 2.1 convert_reduce_fusion
  111.6 2.3 fusion.14.refs_1_
  114.4 109.0 %attend.2 = (f32[128,2048]{1,0:T(8,128)}, bf16[16,128,2048]{2,1,0:T(8,128)(2,1)}, bf16[8,256,128]{2,1,0:T(8,128)(2,1)}, bf16[2,2048,256]{2,1,0:T(8,128)(2,1)}, b...) custom-call(bf16[128,2048]{1,0:T(8,128)(2,1)} %fusion.20.refs_0_, bf16[128,256]{1,0:T(8,128)(2,1)} %fusion.14.refs_1_, ...), custom_call_target="tpu_custom_call" | custom-call | tf_op jit(solution)/shard_map/attend/pallas_call | solution.py:1456
  223.5 1.6 fusion.64
  225.4 2.0 dynamic-slice_reduce_fusion
  230.1 98.5 %hidden.2 = (f32[128,2048]{1,0:T(8,128)}, bf16[2,16,64,2048]{3,2,1,0:T(8,128)(2,1)}, bf16[2,16,64,512]{3,2,1,0:T(8,128)(2,1)}, bf16[2,16,64,512]{3,2,1,0:T(8,128)(2,1)}) custom-call(bf16[128,2048]{1,0:T(8,128)(2,1)} %add_convert_fusion.3.refs_0_, bf16[2048,512]{1,0:T(8,128)(2,1)} %all-gather.5.cloned.1.call-done.refs_1_, ...), custom_call_target="tpu_custom_call" | custom-call | tf_op jit(solution)/shard_map/hidden/pallas_call | solution.py:1210
  328.6 1.5 convert_reduce_fusion.1
  331.8 79.0 %attend.3 = (f32[128,2048]{1,0:T(8,128)}, bf16[16,128,2048]{2,1,0:T(8,128)(2,1)}, bf16[8,256,128]{2,1,0:T(8,128)(2,1)}, bf16[2,2048,256]{2,1,0:T(8,128)(2,1)}, b...) custom-call(bf16[128,2048]{1,0:T(8,128)(2,1)} %copy-done.11, bf16[128,256]{1,0:T(8,128)(2,1)} %fusion.15.refs_1_, ...), custom_call_target="tpu_custom_call" | custom-call | tf_op jit(solution)/shard_map/attend/pallas_call | solution.py:1456
  410.8 1.4 fusion.62
  413.6 67.8 %hidden.3 = (f32[128,2048]{1,0:T(8,128)}, bf16[2,16,64,2048]{3,2,1,0:T(8,128)(2,1)}, bf16[2,16,64,512]{3,2,1,0:T(8,128)(2,1)}, bf16[2,16,64,512]{3,2,1,0:T(8,128)(2,1)}) custom-call(bf16[128,2048]{1,0:T(8,128)(2,1)} %add_convert_fusion.1.refs_0_, bf16[2048,512]{1,0:T(8,128)(2,1)} %all-gather.9.cloned.1.call-done.refs_1_, ...), custom_call_target="tpu_custom_call" | custom-call | tf_op jit(solution)/shard_map/hidden/pallas_call | solution.py:1210
  481.4 72.1 %hidden_back.2 = (f32[128,2048]{1,0:T(8,128)}, bf16[512,2048]{1,0:T(8,128)(2,1)}, bf16[2048,512]{1,0:T(8,128)(2,1)}, f32[1,512]{1,0:T(1,128)}) custom-call(bf16[128,2048]{1,0:T(8,128)(2,1)} %get-tuple-element.176.refs_0_, bf16[2048,512]{1,0:T(8,128)(2,1)} %all-gather.9.cloned.1.call-done.refs_1_, bf16[512,2048]{1,0:T(8,128)(2,1)} %all-gather.11.cloned.1.call-done.refs_2_, ...), custom_call_target="tpu_custom_call" | custom-call | tf_op jit(solution)/shard_map/hidden_back/pallas_call | solution.py:1210
  553.6 1.7 multiply_reduce_fusion
  559.0 121.2 %attend_back.2 = (f32[128,2048]{1,0:T(8,128)}, f32[128,256]{1,0:T(8,128)}, f32[128,256]{1,0:T(8,128)}, bf16[128,2048]{1,0:T(8,128)(2,1)}, bf16[2048,128]{1,0:T(8...) custom-call(bf16[128,2048]{1,0:T(8,128)(2,1)} %get-tuple-element.156, ...), custom_call_target="tpu_custom_call" | custom-call | tf_op jit(solution)/shard_map/attend_back/pallas_call | solution.py:1764
  681.4 1.4 convolution_convert_fusion
  682.9 2.0 fusion.53
  685.4 2.1 fusion.55
  687.5 74.0 %hidden_back.3 = (f32[128,2048]{1,0:T(8,128)}, bf16[512,2048]{1,0:T(8,128)(2,1)}, bf16[2048,512]{1,0:T(8,128)(2,1)}, f32[1,512]{1,0:T(1,128)}) custom-call(bf16[128,2048]{1,0:T(8,128)(2,1)} %get-tuple-element.151.refs_0_.refs_11_, bf16[2048,512]{1,0:T(8,128)(2,1)} %all-gather.5.cloned.1.call-done.refs_1_, ...), custom_call_target="tpu_custom_call" | custom-call | tf_op jit(solution)/shard_map/hidden_back/pallas_call | solution.py:1210
  761.5 1.7 multiply_reduce_fusion.1
  765.3 146.7 %attend_back.3 = (f32[128,2048]{1,0:T(8,128)}, f32[128,256]{1,0:T(8,128)}, f32[128,256]{1,0:T(8,128)}, bf16[128,2048]{1,0:T(8,128)(2,1)}, bf16[2048,128]{1,0:T(8...) custom-call(bf16[128,2048]{1,0:T(8,128)(2,1)} %get-tuple-element.154, ...), custom_call_target="tpu_custom_call" | custom-call | tf_op jit(solution)/shard_map/attend_back/pallas_call | solution.py:1764
  913.2 1.4 convolution_convert_fusion.1
  916.0 1.8 fusion.52
  920.4 3.0 fusion.54
  923.5 1.6 maximum_maximum_fusion.small
  925.1 62.7 %return_last.1 = (f32[144,256]{1,0:T(8,128)}, bf16[2,128,2048]{2,1,0:T(8,128)(2,1)}, bf16[2,128,2048]{2,1,0:T(8,128)(2,1)}, bf16[128,2048]{1,0:T(8,128)(2,1)}) custom-call(bf16[32,144,256]{2,1,0:T(8,128)(2,1)} %maximum_maximum_fusion.small, bf16[16,128,128]{2,1,0:T(8,128)(2,1)} %bitcast.196, bf16[16,128,128]{2,1,0:T(8,128)(2,1)} %bitcast.195, ...), custom_call_target="tpu_custom_call" | custom-call | tf_op jit(solution)/shard_map/return_last/pallas_call | solution.py:916
  991.2 1.5 add_bitcast_fusion
  992.7 2.4 convert_add_fusion.1
  995.7 2.4 bitcast_convert_fusion
  998.1 1.3 copy-done.26
  999.4 2.3 bitcast_convert_fusion.1
  1004.1 1.5 maximum_bitcast_fusion
  (206 shorter events, 35.1 us)
Async XLA Ops:
  7.2 222.9 %all-gather.5.cloned.1.call-start = ((), (), s32[]{:S(2)}) async-start(), calls=%async_computation | async-start | bytes 3145728 | tf_op jit(solution)/shard_map/all_gather | solution.py:949
  102.0 2.1 copy-start.33
  102.0 2.3 copy-start.1
  102.0 128.0 %all-gather.7.cloned.1.call-start = ((), (), s32[]{:S(2)}) async-start(), calls=%async_computation.1 | async-start | bytes 3145728 | tf_op jit(solution)/shard_map/all_gather | solution.py:949
  102.8 310.8 %all-gather.11.cloned.1.call-start = ((), (), s32[]{:S(2)}) async-start(), calls=%async_computation.3 | async-start | bytes 3145728 | tf_op jit(solution)/shard_map/all_gather | solution.py:949
  103.5 310.1 %all-gather.9.cloned.1.call-start = ((), (), s32[]{:S(2)}) async-start(), calls=%async_computation.2 | async-start | bytes 3145728 | tf_op jit(solution)/shard_map/all_gather | solution.py:949
  104.1 3.3 copy-start
  107.4 4.2 copy-start.36
  107.4 223.5 %copy-start.34 = (f32[1,256]{1,0:T(1,128)}, f32[1,256]{1,0:T(1,128)S(1)}, u32[]{:S(2)}) copy-start(f32[1,256]{1,0:T(1,128)S(1)} %get-tuple-element.215.refs_6_) | copy-start | bytes 3076
  223.4 4.0 copy-start.23
  328.6 2.3 copy-start.5
  555.4 2.4 copy-start.29
  559.0 122.3 %copy-start.12 = (bf16[128,2048]{1,0:T(8,128)(2,1)S(1)}, bf16[128,2048]{1,0:T(8,128)(2,1)}, u32[]{:S(2)}) copy-start(bf16[128,2048]{1,0:T(8,128)(2,1)} %copy-done.11) | copy-start | bytes 1572868
  680.3 2.6 copy-start.6
  682.8 2.6 copy-start.9
  682.8 2.6 copy-start.24
  682.9 2.6 copy-start.30
  765.3 147.9 %copy-start.20 = (bf16[2048,128]{1,0:T(8,128)(2,1)S(1)}, bf16[2048,128]{1,0:T(8,128)(2,1)}, u32[]{:S(2)}) copy-start(bf16[2048,128]{1,0:T(8,128)(2,1)} %copy.31) | copy-start | bytes 1572868
  765.3 150.2 %copy-start.38 = (f32[1,512]{1,0:T(1,128)S(1)}, f32[1,512]{1,0:T(1,128)}, u32[]{:S(2)}) copy-start(f32[1,512]{1,0:T(1,128)} %get-tuple-element.117) | copy-start | bytes 6148
  912.0 4.0 copy-start.2
  912.0 4.0 copy-start.18
  916.0 3.5 copy-start.39
  916.0 3.7 copy-start.37
  917.9 2.6 copy-start.4
  920.4 3.1 copy-start.14
  920.4 3.1 copy-start.15
  991.2 4.5 copy-start.27
  991.2 4.5 copy-start.28
  995.7 2.4 copy-start.25
  995.7 3.7 copy-start.26
  999.4 3.4 copy-start.31
  999.4 3.4 copy-start.32
  (12 other events, 17.6 us)
Sparse Core Ops, SparseCore 0:
  102.1 58.7 all-gather.4
  162.5 55.5 all-gather.6
  219.6 55.6 all-gather.10
  276.7 55.5 all-gather.8

commit v6 on v5

--- a/solution.py
+++ b/solution.py
@@ -1567,9 +1567,6 @@
         c_before, e_before = refs[12:14]
         refs = refs[:12] + refs[14:]
     o_ref, own_ref, far_ref, wo_ref, wq_ref, bq_ref, rc, re, crossed = refs[12:21]
-    if home == 0:
-        rc_before, re_before = refs[21:23]
-        refs = refs[:21] + refs[23:]
     x_all, n1, wq, wo, q_all, kv_all, mixed, dq_all, dk, dv, part, came, buf = refs[21:34]
     kv_parts, kv_bufs, sent = refs[34:36], refs[36:38], refs[38]
     c_kept, c_came, e_kept, e_came = refs[39:43]
@@ -1579,7 +1576,7 @@
     deliver = home == 0
     if deliver:
         back_home = Home(home, 8, c_kept, e_kept, rc, re, home_sems)
-        before = Home(1, 8, c_before, e_before, rc_before, re_before, refs[66:])
+        before = Home(1, 8, c_before, e_before, rc, re, refs[66:])
     h, trio = Hyper(CUBE), Hyper(TRIO)
     sec, shd = lax.axis_index("section"), lax.axis_index("shard")
     half, low = shd // 8, lax.rem(shd, 8)
@@ -1692,6 +1689,9 @@
         dv[m, keys] += dot32(probs.astype(jnp.bfloat16), gm)
 
     step, last_add = sums.following(compute)
+    for _ in range(2):
+        for one in turns.pop(0):
+            one()
     feed(pair_gather_steps(g, step), 2)
     last_add()
     swap_step(swap_rows.start, True)
@@ -1772,10 +1772,9 @@
             jax.ShapeDtypeStruct((1, HD), f32),
         ]
         + (homes if home == 0 else sums)
-        + [jax.ShapeDtypeStruct((128, D), bf16)]
-        + (homes if home == 0 else []),
+        + [jax.ShapeDtypeStruct((128, D), bf16)],
         in_specs=[hbm] * 7 + [vmem] * 2 + [hbm] * (3 + len(before)),
-        out_specs=[vmem] * 6 + [hbm] * (3 + len(before)),
+        out_specs=[vmem] * 6 + [hbm] * 3,
         scratch_shapes=[
             pltpu.VMEM((16, 128, D), bf16),
             pltpu.VMEM((16, 128, D), bf16),
@@ -1951,7 +1950,7 @@
         g_mid, d_gain_two, d_shift_two = back(g_n2)
         g_mid = grad + g_mid
         ga = g_mid.astype(bf16)
-        rows, kv_own, kv_far, d_wo, d_wq, d_bq, d_wc, d_we, crossed, *before = attend_back_layer(
+        rows, kv_own, kv_far, d_wo, d_wq, d_bq, d_wc, d_we, crossed = attend_back_layer(
             ga,
             all_n1,
             wq,
@@ -2031,9 +2030,9 @@
         vec[512:640][None],
         vec[256:384][None],
         vec[384:512][None],
-        here((weight_grads[0][3], before[1])).astype(f32)[None],
+        weight_grads[0][3].astype(f32)[None],
         vec[768:1280][None],
-        here((weight_grads[0][2], before[0])).astype(f32)[None],
+        weight_grads[0][2].astype(f32)[None],
         vec[640:768][None],
     )
 

time: 1020 us -> 1020 us (level)
  no operation moved by 1% of the time
where the time goes in v6:
time: 1020 us; the launch traced here: 1010 us
  Pallas kernels  923 us (90%)
  other arithmetic  46 us (5%)
  local copies, waits for them, and re-layouts  15.4 us (2%)
  between operations  14.9 us (1%)
    pallas_call x4, Pallas kernels, hidden_layer(): pl.pallas_call(functools.partial(hidden_kernel, back, plan), out_shape=ou...  311 us
    pallas_call x2, Pallas kernels, attend_back_layer(): pl.pallas_call(functools.partial(attend_back_kernel, plan, home), out_sha...  274 us
    pallas_call x2, Pallas kernels, attend_layer(): pl.pallas_call(functools.partial(attend_kernel, plan, section), out_shape...  188 us
    pallas_call x1, Pallas kernels, fetch_weights(): pl.pallas_call(fetch_kernel, out_shape=(jax.ShapeDtypeStruct((32, 128, 2...  91.9 us
    pallas_call x1, Pallas kernels, return_last(): pl.pallas_call(last_kernel, out_shape=(jax.ShapeDtypeStruct(small.shape[1...  58.5 us
  transfers between devices with their start and end apart: 4, of which 0 were waited for; matrix products, arithmetic and copies ran while one was open for 2% of the time, Pallas kernels for 28%

profile of v6, /device:TPU:0, one launch (start us, length us, event | category | flops | bytes accessed | tf_op | source)
XLA Modules:
  0.0 1011.5 jit_solution(1879820537143244858)
XLA Ops:
  10.1 91.9 %fetch_weights.1 = (bf16[32,128,256]{2,1,0:T(8,128)(2,1)}, bf16[32,16,128]{2,1,0:T(8,128)(2,1)}, bf16[2,16,128,128]{3,2,1,0:T(8,128)(2,1)}, bf16[2,128,2048]{2,1...) custom-call(bf16[16,128]{1,0:T(8,128)(2,1)} %pad.19.small, ...), custom_call_target="tpu_custom_call" | custom-call | tf_op jit(solution)/shard_map/fetch_weights/pallas_call | solution.py:797
  104.8 1.2 fusion.20.refs_0_
  107.4 1.5 fusion.66
  109.4 2.1 convert_reduce_fusion
  111.6 2.3 fusion.14.refs_1_
  114.4 109.0 %attend.2 = (f32[128,2048]{1,0:T(8,128)}, bf16[16,128,2048]{2,1,0:T(8,128)(2,1)}, bf16[8,256,128]{2,1,0:T(8,128)(2,1)}, bf16[2,2048,256]{2,1,0:T(8,128)(2,1)}, b...) custom-call(bf16[128,2048]{1,0:T(8,128)(2,1)} %fusion.20.refs_0_, bf16[128,256]{1,0:T(8,128)(2,1)} %fusion.14.refs_1_, ...), custom_call_target="tpu_custom_call" | custom-call | tf_op jit(solution)/shard_map/attend/pallas_call | solution.py:1456
  223.5 1.6 fusion.64
  225.4 2.0 dynamic-slice_reduce_fusion
  230.1 98.5 %hidden.2 = (f32[128,2048]{1,0:T(8,128)}, bf16[2,16,64,2048]{3,2,1,0:T(8,128)(2,1)}, bf16[2,16,64,512]{3,2,1,0:T(8,128)(2,1)}, bf16[2,16,64,512]{3,2,1,0:T(8,128)(2,1)}) custom-call(bf16[128,2048]{1,0:T(8,128)(2,1)} %add_convert_fusion.3.refs_0_, bf16[2048,512]{1,0:T(8,128)(2,1)} %all-gather.5.cloned.1.call-done.refs_1_, ...), custom_call_target="tpu_custom_call" | custom-call | tf_op jit(solution)/shard_map/hidden/pallas_call | solution.py:1210
  328.6 1.5 convert_reduce_fusion.1
  331.8 79.0 %attend.3 = (f32[128,2048]{1,0:T(8,128)}, bf16[16,128,2048]{2,1,0:T(8,128)(2,1)}, bf16[8,256,128]{2,1,0:T(8,128)(2,1)}, bf16[2,2048,256]{2,1,0:T(8,128)(2,1)}, b...) custom-call(bf16[128,2048]{1,0:T(8,128)(2,1)} %copy-done.11, bf16[128,256]{1,0:T(8,128)(2,1)} %fusion.15.refs_1_, ...), custom_call_target="tpu_custom_call" | custom-call | tf_op jit(solution)/shard_map/attend/pallas_call | solution.py:1456
  410.8 1.4 fusion.62
  413.6 67.8 %hidden.3 = (f32[128,2048]{1,0:T(8,128)}, bf16[2,16,64,2048]{3,2,1,0:T(8,128)(2,1)}, bf16[2,16,64,512]{3,2,1,0:T(8,128)(2,1)}, bf16[2,16,64,512]{3,2,1,0:T(8,128)(2,1)}) custom-call(bf16[128,2048]{1,0:T(8,128)(2,1)} %add_convert_fusion.1.refs_0_, bf16[2048,512]{1,0:T(8,128)(2,1)} %all-gather.9.cloned.1.call-done.refs_1_, ...), custom_call_target="tpu_custom_call" | custom-call | tf_op jit(solution)/shard_map/hidden/pallas_call | solution.py:1210
  481.4 72.1 %hidden_back.2 = (f32[128,2048]{1,0:T(8,128)}, bf16[512,2048]{1,0:T(8,128)(2,1)}, bf16[2048,512]{1,0:T(8,128)(2,1)}, f32[1,512]{1,0:T(1,128)}) custom-call(bf16[128,2048]{1,0:T(8,128)(2,1)} %get-tuple-element.172.refs_0_, bf16[2048,512]{1,0:T(8,128)(2,1)} %all-gather.9.cloned.1.call-done.refs_1_, bf16[512,2048]{1,0:T(8,128)(2,1)} %all-gather.11.cloned.1.call-done.refs_2_, ...), custom_call_target="tpu_custom_call" | custom-call | tf_op jit(solution)/shard_map/hidden_back/pallas_call | solution.py:1210
  553.6 1.7 multiply_reduce_fusion
  557.8 1.2 broadcast_select_fusion.2
  559.0 116.1 %attend_back.2 = (f32[128,2048]{1,0:T(8,128)}, f32[128,256]{1,0:T(8,128)}, f32[128,256]{1,0:T(8,128)}, bf16[128,2048]{1,0:T(8,128)(2,1)}, bf16[2048,128]{1,0:T(8...) custom-call(bf16[128,2048]{1,0:T(8,128)(2,1)} %get-tuple-element.152, ...), custom_call_target="tpu_custom_call" | custom-call | tf_op jit(solution)/shard_map/attend_back/pallas_call | solution.py:1764
  676.3 1.4 convolution_convert_fusion
  677.8 2.0 fusion.53
  680.3 2.1 fusion.55
  682.4 72.5 %hidden_back.3 = (f32[128,2048]{1,0:T(8,128)}, bf16[512,2048]{1,0:T(8,128)(2,1)}, bf16[2048,512]{1,0:T(8,128)(2,1)}, f32[1,512]{1,0:T(1,128)}) custom-call(bf16[128,2048]{1,0:T(8,128)(2,1)} %get-tuple-element.147.refs_0_.refs_11_, bf16[2048,512]{1,0:T(8,128)(2,1)} %all-gather.5.cloned.1.call-done.refs_1_, ...), custom_call_target="tpu_custom_call" | custom-call | tf_op jit(solution)/shard_map/hidden_back/pallas_call | solution.py:1210
  755.0 1.7 multiply_reduce_fusion.1
  758.8 157.8 %attend_back.3 = (f32[128,2048]{1,0:T(8,128)}, f32[128,256]{1,0:T(8,128)}, f32[128,256]{1,0:T(8,128)}, bf16[128,2048]{1,0:T(8,128)(2,1)}, bf16[2048,128]{1,0:T(8...) custom-call(bf16[128,2048]{1,0:T(8,128)(2,1)} %get-tuple-element.150, ...), custom_call_target="tpu_custom_call" | custom-call | tf_op jit(solution)/shard_map/attend_back/pallas_call | solution.py:1764
  917.8 1.4 convolution_convert_fusion.1
  920.6 1.8 fusion.52
  925.0 3.0 fusion.54
  928.1 1.6 maximum_maximum_fusion.small
  929.7 58.5 %return_last.1 = (f32[144,256]{1,0:T(8,128)}, bf16[2,128,2048]{2,1,0:T(8,128)(2,1)}, bf16[2,128,2048]{2,1,0:T(8,128)(2,1)}, bf16[128,2048]{1,0:T(8,128)(2,1)}) custom-call(bf16[32,144,256]{2,1,0:T(8,128)(2,1)} %maximum_maximum_fusion.small, bf16[16,128,128]{2,1,0:T(8,128)(2,1)} %bitcast.196, bf16[16,128,128]{2,1,0:T(8,128)(2,1)} %bitcast.195, ...), custom_call_target="tpu_custom_call" | custom-call | tf_op jit(solution)/shard_map/return_last/pallas_call | solution.py:916
  991.7 1.5 add_bitcast_fusion
  994.9 2.5 bitcast_convert_fusion
  997.5 2.4 bitcast_convert_fusion.1
  1002.2 1.5 maximum_bitcast_fusion
  (204 shorter events, 33.7 us)
Async XLA Ops:
  7.2 222.9 %all-gather.5.cloned.1.call-start = ((), (), s32[]{:S(2)}) async-start(), calls=%async_computation | async-start | bytes 3145728 | tf_op jit(solution)/shard_map/all_gather | solution.py:949
  102.0 2.1 copy-start.32
  102.0 2.3 copy-start.1
  102.0 128.0 %all-gather.7.cloned.1.call-start = ((), (), s32[]{:S(2)}) async-start(), calls=%async_computation.1 | async-start | bytes 3145728 | tf_op jit(solution)/shard_map/all_gather | solution.py:949
  102.8 310.8 %all-gather.11.cloned.1.call-start = ((), (), s32[]{:S(2)}) async-start(), calls=%async_computation.3 | async-start | bytes 3145728 | tf_op jit(solution)/shard_map/all_gather | solution.py:949
  103.5 310.1 %all-gather.9.cloned.1.call-start = ((), (), s32[]{:S(2)}) async-start(), calls=%async_computation.2 | async-start | bytes 3145728 | tf_op jit(solution)/shard_map/all_gather | solution.py:949
  104.1 3.3 copy-start
  107.4 4.2 copy-start.35
  107.4 223.5 %copy-start.33 = (f32[1,256]{1,0:T(1,128)}, f32[1,256]{1,0:T(1,128)S(1)}, u32[]{:S(2)}) copy-start(f32[1,256]{1,0:T(1,128)S(1)} %get-tuple-element.211.refs_6_) | copy-start | bytes 3076
  107.4 2.0 copy-start.34
  223.4 4.0 copy-start.25
  328.6 2.3 copy-start.5
  555.4 2.4 copy-start.28
  559.0 117.2 %copy-start.12 = (bf16[128,2048]{1,0:T(8,128)(2,1)S(1)}, bf16[128,2048]{1,0:T(8,128)(2,1)}, u32[]{:S(2)}) copy-start(bf16[128,2048]{1,0:T(8,128)(2,1)} %copy-done.11) | copy-start | bytes 1572868
  675.2 2.6 copy-start.6
  677.7 2.6 copy-start.9
  677.8 2.6 copy-start.26
  677.8 2.6 copy-start.29
  758.8 159.0 %copy-start.22 = (bf16[2048,128]{1,0:T(8,128)(2,1)S(1)}, bf16[2048,128]{1,0:T(8,128)(2,1)}, u32[]{:S(2)}) copy-start(bf16[2048,128]{1,0:T(8,128)(2,1)} %copy.31) | copy-start | bytes 1572868
  758.8 161.3 %copy-start.37 = (f32[1,512]{1,0:T(1,128)S(1)}, f32[1,512]{1,0:T(1,128)}, u32[]{:S(2)}) copy-start(f32[1,512]{1,0:T(1,128)} %get-tuple-element.115) | copy-start | bytes 6148
  916.6 4.0 copy-start.2
  916.6 4.0 copy-start.18
  920.6 3.5 copy-start.38
  920.6 3.7 copy-start.36
  922.5 2.6 copy-start.4
  925.0 3.1 copy-start.14
  925.0 3.1 copy-start.15
  988.2 5.0 copy-start.27
  991.7 3.2 copy-start.21
  994.9 2.5 copy-start.20
  997.5 3.5 copy-start.30
  997.5 3.5 copy-start.31
  (11 other events, 15.6 us)
Sparse Core Ops, SparseCore 0:
  102.1 58.7 all-gather.4
  162.5 55.5 all-gather.6
  219.6 55.6 all-gather.10
  276.7 55.5 all-gather.8
